TPU v7x, 32 devices: a whole 2x2x4 slice. The times are simulated.
32 devices in a mesh: groups: 2 (over x), kv: 16 (over z, y, core).
Axes of the slice: x: 2, y: 2, z: 4, core: 2. Of those that a mesh axis runs over, the one named last changes fastest.
Arguments:
- queries: bfloat16 [64, 8192], P(('groups', 'kv')), parts along dimension 0, may hold values from -48 to 48
- keys: bfloat16 [16384, 1024], P(('groups', 'kv')), parts along dimension 0, may hold values from -6 to 6
- values: bfloat16 [16384, 1024], P(('groups', 'kv')), parts along dimension 0, may hold values from -6 to 6
- block_live: int32 [32, 128], P('groups', 'kv'), parts along dimension 0, may hold values from 0 to 1, as said below
- span_offset: int32 [2], P('groups'), parts along dimension 0, may hold values from 2048 to 7648
Outputs:
- attended: bfloat16 [64, 8192], P(('groups', 'kv')), parts along dimension 0
There are 2 independent parts, one for each index of `groups`. A program takes and returns all parts, laid end to end along the dimension named above; each array names one. Nothing has to cross between parts.
Inputs may be any that keep to these rules, and one draw needn't show every extreme that they name: `block_live`: column 0 is 1 for every query shard.
All inputs are finite; a program needn't handle non-finite values.
Results may differ from a plain program's by a relative error of at most 0.0018.
Values may be sent and summed in bfloat16 or wider, within the bound.
No kernel may reach another device: no remote copies, remote signals or barrier semaphores. Data moves between devices by JAX's collectives and lax.ppermute only.
A program may use at most 128 MiB of HBM per device.

v0:
```python
import functools
import math

import jax
import jax.numpy as jnp
from jax import lax
from jax.experimental import pallas as pl
from jax.experimental.pallas import tpu as pltpu
from jax.sharding import PartitionSpec as P

H = 64
KVH = 8
HD = 128
BLK = 64
GROUP = H // KVH
SCORE_FLOOR = -30.0
ROOT = math.sqrt(HD)
TO_BITS = math.log2(math.e) / ROOT
FIX = 2.0**17
STEPS = 32766.0
NO_WEIGHT = -8191.0
MASKED = -1e30
KINDS = 3
SLOT = HD // 2
STATS = 2 * HD
VMEM = pl.BlockSpec(memory_space=pltpu.VMEM)
PARAMS = pltpu.CompilerParams(vmem_limit_bytes=24 * 2**20)


def swap(array, delta):
    count = lax.axis_size("kv")
    return lax.ppermute(array, "kv", [(i, i ^ delta) for i in range(count)])


def exchange_steps(count):
    bits = count.bit_length() - 1
    steps = [[0, 1], [0, 2]]
    bit = 2
    while bit < bits:
        width = min(2, bits - bit)
        steps.append([d << bit for d in range(1 << width)])
        bit += width
    return steps[::-1]


def prep_kernel(v_ref, live_ref, offset_ref, v_turned, *bias_refs, places):
    me = lax.axis_index("kv")
    kv_dev = v_ref.shape[0]
    count = 2 ** len(places)
    lanes = bias_refs[0].shape[1]
    rows = lanes // GROUP
    q_dev = rows * len(bias_refs) // count
    offset = offset_ref[0]
    row = lax.broadcasted_iota(jnp.int32, (1, lanes), 1) % rows
    at_key = me * kv_dev + lax.broadcasted_iota(jnp.int32, (kv_dev, lanes), 0)
    live = live_ref[...].astype(jnp.float32)
    for c, bias_ref in enumerate(bias_refs):
        index = c * (count // len(bias_refs)) + row // q_dev
        owner = me
        for bit, place in enumerate(places):
            owner = owner ^ (((index >> bit) & 1) << place)
        token = owner * q_dev + row % q_dev
        chosen = lax.broadcasted_iota(jnp.int32, (count, lanes), 0) == owner
        seen = jnp.dot(live, chosen.astype(jnp.float32), preferred_element_type=jnp.float32)
        seen = jnp.concatenate(
            [jnp.broadcast_to(seen[b : b + 1], (BLK, lanes)) for b in range(kv_dev // BLK)], 0
        )
        allowed = (at_key <= offset + token) & ((at_key >= offset) | (seen > 0.5))
        bias_ref[...] = jnp.where(allowed, 0.0, MASKED)
    v_turned[...] = v_ref[...].T


def join_kernel(*refs):
    *in_refs, out_ref = refs
    joined = jnp.concatenate([ref[...].astype(jnp.float32) for ref in in_refs], 0)
    out_ref[...] = joined.astype(out_ref.dtype)


def join(pieces):
    rows, width = pieces[0].shape
    return pl.pallas_call(
        join_kernel,
        out_shape=jax.ShapeDtypeStruct((len(pieces) * rows, width), pieces[0].dtype),
        in_specs=[VMEM] * len(pieces),
        out_specs=VMEM,
        compiler_params=PARAMS,
    )(*pieces)


def attend_kernel(*refs, segment):
    *q_refs, k_ref, vt_ref, bias_ref, out_ref = refs
    queries_all = jnp.concatenate([ref[...] for ref in q_refs], 0)
    rows, width = queries_all.shape
    kv_heads = width // (GROUP * HD)
    segments = k_ref.shape[0] // segment
    lanes = GROUP * rows
    target = lax.broadcasted_iota(jnp.int32, (STATS, lanes), 0)
    head_of = lax.broadcasted_iota(jnp.int32, (STATS, lanes), 1) // rows
    stats = jnp.zeros((STATS, lanes), jnp.float32)
    for g in range(kv_heads):
        queries = jnp.concatenate(
            [queries_all[:, (g * GROUP + h) * HD : (g * GROUP + h + 1) * HD] for h in range(GROUP)],
            0,
        )
        peaks, totals, outs = [], [], []
        for s in range(segments):
            at = slice(s * segment, (s + 1) * segment)
            scores = lax.dot_general(
                k_ref[at, g * HD : (g + 1) * HD],
                queries,
                (((1,), (1,)), ((), ())),
                preferred_element_type=jnp.float32,
            )
            scores = scores + bias_ref[at, :]
            peak = jnp.maximum(jnp.max(scores, 0, keepdims=True), SCORE_FLOOR * ROOT)
            weights = jnp.exp2((scores - peak) * TO_BITS)
            peaks.append(peak)
            totals.append(jnp.sum(weights, 0, keepdims=True))
            outs.append(
                jnp.dot(
                    vt_ref[g * HD : (g + 1) * HD, at],
                    weights.astype(jnp.bfloat16),
                    preferred_element_type=jnp.float32,
                )
            )
        top = functools.reduce(jnp.maximum, peaks)
        scales = [jnp.exp2((peak - top) * TO_BITS) for peak in peaks]
        total = sum(e * t for e, t in zip(scales, totals))
        out = sum(e * o for e, o in zip(scales, outs))
        live = total > 0
        safe = jnp.where(live, total, 1.0)
        level = jnp.where(live, top * TO_BITS + jnp.log2(safe), NO_WEIGHT)
        out = out * jnp.where(live, 1.0 / safe, 0.0)
        largest = jnp.max(jnp.abs(out), 0, keepdims=True)
        power = jnp.clip(jnp.ceil(jnp.log2(jnp.maximum(largest, 1e-37))), -100.0, 8.0)
        out = jnp.round((out * (jnp.exp2(-power) * STEPS)).T).astype(jnp.int32).astype(jnp.int16)
        fixed = jnp.round(level * FIX).astype(jnp.int32)
        values = [fixed >> 16, (fixed & 0xFFFF) - 32768, power]
        for kind in range(KINDS):
            stats = jnp.where(
                target == kind * SLOT + g * GROUP + head_of,
                values[kind].astype(jnp.float32),
                stats,
            )
        for h in range(GROUP):
            out_ref[:, (g * GROUP + h) * HD : (g * GROUP + h + 1) * HD] = out[h * rows : (h + 1) * rows]
    stats = stats.T
    packed = sum(stats[h * rows : (h + 1) * rows] for h in range(GROUP))
    out_ref[:, kv_heads * GROUP * HD :] = packed.astype(jnp.int32).astype(jnp.int16)


def combine_kernel(*refs, parts, heads, final):
    in_refs, out_refs = refs[:parts], refs[parts:]
    wide = heads * HD
    rows = in_refs[0].shape[0]
    chunk = rows // len(out_refs)
    fixed, powers = [], []
    for ref in in_refs:
        stats = ref[:, wide : wide + HD].astype(jnp.int32)
        fixed.append((stats << 16) + pltpu.roll(stats, SLOT, 1) + 32768)
        powers.append(ref[:, wide + HD :].astype(jnp.int32).astype(jnp.float32))
    top = functools.reduce(jnp.maximum, fixed)
    weights = [jnp.exp2((f - top).astype(jnp.float32) * (1.0 / FIX)) for f in fixed]
    total = sum(weights)
    shares = [w / total for w in weights]
    amounts = [s * jnp.exp2(p) for s, p in zip(shares, powers)]
    if final:
        factors = [a * (1.0 / STEPS) for a in amounts]
    else:
        power = jnp.clip(jnp.ceil(jnp.log2(jnp.maximum(sum(amounts), 1e-37))), -100.0, 8.0)
        back = jnp.exp2(-power)
        factors = [a * back for a in amounts]
    for h in range(heads):
        at = slice(h * HD, (h + 1) * HD)
        out = sum(
            f[:, h : h + 1] * ref[:, at].astype(jnp.int32).astype(jnp.float32)
            for f, ref in zip(factors, in_refs)
        )
        if final:
            out = out.astype(jnp.bfloat16)
        else:
            out = jnp.round(out).astype(jnp.int32).astype(jnp.int16)
        for c, out_ref in enumerate(out_refs):
            out_ref[:, at] = out[c * chunk : (c + 1) * chunk]
    if not final:
        level = top + jnp.round(jnp.log2(total) * FIX).astype(jnp.int32)
        lane = lax.broadcasted_iota(jnp.int32, level.shape, 1)
        low = pltpu.roll((level & 0xFFFF) - 32768, SLOT, 1)
        packed = jnp.concatenate(
            [jnp.where(lane < SLOT, level >> 16, low), power.astype(jnp.int32)], 1
        )
        packed = packed.astype(jnp.int16)
        for c, out_ref in enumerate(out_refs):
            out_ref[:, wide:] = packed[c * chunk : (c + 1) * chunk]


def combine(arrays, pieces, heads, final):
    rows = arrays[0].shape[0]
    width = heads * HD if final else arrays[0].shape[1]
    dtype = jnp.bfloat16 if final else jnp.int16
    return pl.pallas_call(
        functools.partial(combine_kernel, parts=len(arrays), heads=heads, final=final),
        out_shape=[jax.ShapeDtypeStruct((rows // pieces, width), dtype)] * pieces,
        in_specs=[VMEM] * len(arrays),
        out_specs=[VMEM] * pieces,
        compiler_params=PARAMS,
    )(*arrays)


def on_device(queries, keys, values, block_live, span_offset):
    count = lax.axis_size("kv")
    q_dev, q_width = queries.shape
    kv_dev, kv_width = keys.shape
    heads = q_width // HD
    steps = exchange_steps(count)
    places = []
    for deltas in steps:
        places += [(deltas[1] << b).bit_length() - 1 for b in range(len(deltas).bit_length() - 1)]
    parts = len(steps[-1])
    chunk = count * q_dev // parts

    prepared = pl.pallas_call(
        functools.partial(prep_kernel, places=places),
        out_shape=[jax.ShapeDtypeStruct((kv_width, kv_dev), values.dtype)]
        + [jax.ShapeDtypeStruct((kv_dev, chunk * GROUP), jnp.float32)] * parts,
        in_specs=[VMEM] * 2 + [pl.BlockSpec(memory_space=pltpu.SMEM)],
        out_specs=[VMEM] * (1 + parts),
        compiler_params=PARAMS,
        cost_estimate=pl.CostEstimate(flops=0, bytes_accessed=4 * 2**20, transcendentals=0),
    )(values, block_live.T, span_offset)

    block = queries
    for stage, deltas in enumerate(steps[:-2]):
        others = [swap(block, d) for d in reversed(deltas[1:])][::-1]
        if stage == 0:
            block, others, prepared = lax.optimization_barrier((block, others, prepared))
        block = join([block] + others)
    v_turned, *biases = prepared
    pieces = [block]
    for deltas in steps[-2:]:
        pieces = pieces + [swap(p, d) for d in deltas[1:] for p in pieces]

    def attend(pieces, bias):
        return pl.pallas_call(
            functools.partial(attend_kernel, segment=kv_dev // 2),
            out_shape=jax.ShapeDtypeStruct((chunk, q_width + STATS), jnp.int16),
            in_specs=[VMEM] * (len(pieces) + 3),
            out_specs=VMEM,
            compiler_params=PARAMS,
            cost_estimate=pl.CostEstimate(
                flops=4 * chunk * q_width * kv_dev,
                bytes_accessed=4 * 2**20,
                transcendentals=chunk * heads * kv_dev,
            ),
        )(*pieces, keys, v_turned, bias)

    share = len(pieces) // parts
    first = attend(pieces[:share], biases[0])
    *others, first = lax.optimization_barrier((*pieces[share:], first))
    outs = [first] + [
        attend(others[c * share : (c + 1) * share], biases[c + 1]) for c in range(parts - 1)
    ]
    splits = [len(deltas) for deltas in steps[::-1]] + [1]
    for stage, deltas in enumerate(steps[::-1]):
        sent = [swap(p, d) for p, d in zip(outs[:0:-1], deltas[:0:-1])]
        arrays = [outs[0]] + sent[::-1]
        outs = combine(arrays, splits[stage + 1], heads, stage == len(steps) - 1)
    return outs[0]


def solution(mesh):
    placed = (
        P(("groups", "kv"), None),
        P(("groups", "kv"), None),
        P(("groups", "kv"), None),
        P("groups", "kv"),
        P("groups"),
    )
    return jax.shard_map(
        on_device, mesh=mesh, in_specs=placed, out_specs=P(("groups", "kv"), None), check_vma=False
    )
```

profile of v0, /device:TPU:0, one launch (start us, length us, event | category | flops | bytes accessed | tf_op | source)
XLA Modules:
  0.0 38.0 jit_solution(10963077644852777335)
XLA Ops:
  0.0 0.0 copy-start
  0.0 4.0 %collective-permute-start.1 = (bf16[2,8192]{1,0:T(2,128)(2,1)}, bf16[2,8192]{1,0:T(2,128)(2,1)S(1)}, u32[]{:S(2)}, u32[]{:S(2)}) collective-permute-start(bf16[2,8192]{1,0:T(2,128)(2,1)} %refs_0_), channel_id=1, source_target_pairs={{0,8},{1,9},{2,10},{3,11},{4,12},{5,13},{6,14},{7,15},{8,0},{9,1},... | collective-permute-start | bytes 98312 | tf_op jit(solution)/shard_map/ppermute | solution.py:32
  4.0 1.6 %collective-permute-start = (bf16[2,8192]{1,0:T(2,128)(2,1)}, bf16[2,8192]{1,0:T(2,128)(2,1)S(1)}, u32[]{:S(2)}, u32[]{:S(2)}) collective-permute-start(bf16[2,8192]{1,0:T(2,128)(2,1)} %refs_0_), channel_id=1, source_target_pairs={{0,4},{1,5},{2,6},{3,7},{4,0},{5,1},{6,2},{7,3},{8,12},{9,13},{10,... | collective-permute-start | bytes 98312 | tf_op jit(solution)/shard_map/ppermute | solution.py:32
  5.6 0.0 collective-permute-start.2
  6.3 0.0 copy-start.1
  6.3 1.2 %copy-done.1 = bf16[512,1024]{1,0:T(8,128)(2,1)S(1)} copy-done((bf16[512,1024]{1,0:T(8,128)(2,1)S(1)}, bf16[512,1024]{1,0:T(8,128)(2,1)}, u32[]{:S(2)}) %copy-start.1) | copy-done | bytes 1048600
  7.5 0.0 copy-start.3
  7.5 0.7 %copy-done.3 = s32[16,8]{0,1:T(8,128)S(1)} copy-done((s32[16,8]{0,1:T(8,128)S(1)}, s32[16,8]{0,1:T(8,128)}, u32[]{:S(2)}) %copy-start.3) | copy-done | bytes 536
  8.2 0.4 %shard_map.55 = (bf16[1024,512]{1,0:T(8,128)(2,1)S(1)}, f32[512,128]{1,0:T(8,128)S(1)}, f32[512,128]{1,0:T(8,128)S(1)}) custom-call(bf16[512,1024]{1,0:T(8,128)(2,1)S(1)} %copy-done.1, s32[8,16]{1,0:T(8,128)S(1)} %bitcast.1, s32[1]{0:T(128)S(6)} %copy.6.offset_ref), custom_call_target="tpu_custom_call" | custom-call | bytes 4194304 | tf_op jit(solution)/shard_map/pallas_call | solution.py:222
  8.6 0.0 collective-permute-done.1.refs_2_
  8.6 0.0 collective-permute-done.refs_1_
  8.6 2.9 %collective-permute-done.2.refs_3_ = bf16[2,8192]{1,0:T(2,128)(2,1)S(1)} collective-permute-done((bf16[2,8192]{1,0:T(2,128)(2,1)}, bf16[2,8192]{1,0:T(2,128)(2,1)S(1)}, u32[]{:S(2)}, u32[]{:S(2)}) %collective-permute-start.2) | collective-permute-done | bytes 32800 | tf_op jit(solution)/shard_map/ppermute | solution.py:32
  11.5 0.0 copy-start.2
  11.5 0.8 %copy-done.2 = bf16[2,8192]{1,0:T(2,128)(2,1)S(1)} copy-done((bf16[2,8192]{1,0:T(2,128)(2,1)S(1)}, bf16[2,8192]{1,0:T(2,128)(2,1)}, u32[]{:S(2)}) %copy-start.2) | copy-done | bytes 32792
  12.3 0.1 shard_map.56.refs_0_
  12.4 1.6 %collective-permute-start.4 = (bf16[8,8192]{1,0:T(8,128)(2,1)S(1)}, bf16[8,8192]{1,0:T(8,128)(2,1)S(1)}, u32[]{:S(2)}, u32[]{:S(2)}) collective-permute-start(bf16[8,8192]{1,0:T(8,128)(2,1)S(1)} %shard_map.56.refs_0_), channel_id=1, source_target_pairs={{0,2},{1,3},{2,0},{3,1},{4,6},{5,7},{6,4},{7,5},{8,10},{9,11},{10,... | collective-permute-start | bytes 393224 | tf_op jit(solution)/shard_map/ppermute | solution.py:32
  14.0 0.0 collective-permute-start.3
  14.0 3.4 %collective-permute-done.4.refs_1_ = bf16[8,8192]{1,0:T(8,128)(2,1)S(1)} collective-permute-done((bf16[8,8192]{1,0:T(8,128)(2,1)S(1)}, bf16[8,8192]{1,0:T(8,128)(2,1)S(1)}, u32[]{:S(2)}, u32[]{:S(2)}) %collective-permute-start.4) | collective-permute-done | bytes 131104 | tf_op jit(solution)/shard_map/ppermute | solution.py:32
  17.4 0.0 collective-permute-start.5
  17.4 0.0 copy-done
  17.4 1.8 %shard_map.57.refs_0_ = s16[16,8448]{1,0:T(8,128)(2,1)S(1)} custom-call(bf16[8,8192]{1,0:T(8,128)(2,1)S(1)} %shard_map.56.refs_0_, bf16[8,8192]{1,0:T(8,128)(2,1)S(1)} %collective-permute-done.4.refs_1_, bf16[512,1024]{1,0:T(8,128)(2,1)S(1)} %copy-done, bf16[1024,512]{1,0:T(8,128)(2,1)S(1)} %get-tuple-element.31.refs_3_, ...), custom_call_target="tpu_custom_call" | custom-call | flops 268435456 | bytes 4194304 | tf_op jit(solution)/shard_map/pallas_call | solution.py:244
  19.2 0.0 collective-permute-done.3.refs_0_
  19.2 0.0 collective-permute-done.5.refs_1_
  19.2 1.8 %shard_map.58 = s16[16,8448]{1,0:T(8,128)(2,1)S(1)} custom-call(bf16[8,8192]{1,0:T(8,128)(2,1)S(1)} %collective-permute-done.3.refs_0_, bf16[8,8192]{1,0:T(8,128)(2,1)S(1)} %collective-permute-done.5.refs_1_, bf16[512,1024]{1,0:T(8,128)(2,1)S(1)} %copy-done, bf16[1024,512]{1,0:T(8,128)(2,1)S(1)} %get-tuple-element.31.refs_3_, ...), custom_call_target="tpu_custom_call" | custom-call | flops 268435456 | bytes 4194304 | tf_op jit(solution)/shard_map/pallas_call | solution.py:244
  21.0 0.6 %collective-permute-start.6 = (s16[16,8448]{1,0:T(8,128)(2,1)S(1)}, s16[16,8448]{1,0:T(8,128)(2,1)S(1)}, u32[]{:S(2)}, u32[]{:S(2)}) collective-permute-start(s16[16,8448]{1,0:T(8,128)(2,1)S(1)} %shard_map.58), channel_id=1, source_target_pairs={{0,1},{1,0},{2,3},{3,2},{4,5},{5,4},{6,7},{7,6},{8,9},{9,8},{10,11... | collective-permute-start | bytes 811016 | tf_op jit(solution)/shard_map/ppermute | solution.py:32
  21.6 1.2 %collective-permute-done.6.refs_1_ = s16[16,8448]{1,0:T(8,128)(2,1)S(1)} collective-permute-done((s16[16,8448]{1,0:T(8,128)(2,1)S(1)}, s16[16,8448]{1,0:T(8,128)(2,1)S(1)}, u32[]{:S(2)}, u32[]{:S(2)}) %collective-permute-start.6) | collective-permute-done | bytes 270368 | tf_op jit(solution)/shard_map/ppermute | solution.py:32
  22.7 0.5 %shard_map.59 = (s16[8,8448]{1,0:T(8,128)(2,1)S(1)}, s16[8,8448]{1,0:T(8,128)(2,1)S(1)}) custom-call(s16[16,8448]{1,0:T(8,128)(2,1)S(1)} %shard_map.57.refs_0_, s16[16,8448]{1,0:T(8,128)(2,1)S(1)} %collective-permute-done.6.refs_1_), custom_call_target="tpu_custom_call" | custom-call | tf_op jit(solution)/shard_map/pallas_call | solution.py:201
  23.3 1.6 %collective-permute-start.7 = (s16[8,8448]{1,0:T(8,128)(2,1)S(1)}, s16[8,8448]{1,0:T(8,128)(2,1)S(1)}, u32[]{:S(2)}, u32[]{:S(2)}) collective-permute-start(s16[8,8448]{1,0:T(8,128)(2,1)S(1)} %get-tuple-element.38), channel_id=1, source_target_pairs={{0,2},{1,3},{2,0},{3,1},{4,6},{5,7},{6,4},{7,5},{8,10},{9,11},{10,... | collective-permute-start | bytes 405512 | tf_op jit(solution)/shard_map/ppermute | solution.py:32
  24.9 4.3 %collective-permute-done.7.refs_1_ = s16[8,8448]{1,0:T(8,128)(2,1)S(1)} collective-permute-done((s16[8,8448]{1,0:T(8,128)(2,1)S(1)}, s16[8,8448]{1,0:T(8,128)(2,1)S(1)}, u32[]{:S(2)}, u32[]{:S(2)}) %collective-permute-start.7) | collective-permute-done | bytes 135200 | tf_op jit(solution)/shard_map/ppermute | solution.py:32
  29.2 0.4 %shard_map.60 = (s16[2,8448]{1,0:T(2,128)(2,1)S(1)}, s16[2,8448]{1,0:T(2,128)(2,1)S(1)}, s16[2,8448]{1,0:T(2,128)(2,1)S(1)}, s16[2,8448]{1,0:T(2,128)(2,1)S(1)}) custom-call(s16[8,8448]{1,0:T(8,128)(2,1)S(1)} %get-tuple-element.37.refs_0_, s16[8,8448]{1,0:T(8,128)(2,1)S(1)} %collective-permute-done.7.refs_1_), custom_call_target="tpu_custom_call" | custom-call | tf_op jit(solution)/shard_map/pallas_call | solution.py:201
  29.6 0.1 collective-permute-start.8
  29.7 1.4 %collective-permute-start.9 = (s16[2,8448]{1,0:T(2,128)(2,1)S(1)}, s16[2,8448]{1,0:T(2,128)(2,1)S(1)}, u32[]{:S(2)}, u32[]{:S(2)}) collective-permute-start(s16[2,8448]{1,0:T(2,128)(2,1)S(1)} %get-tuple-element.41), channel_id=1, source_target_pairs={{0,8},{1,9},{2,10},{3,11},{4,12},{5,13},{6,14},{7,15},{8,0},{9,1},... | collective-permute-start | bytes 101384 | tf_op jit(solution)/shard_map/ppermute | solution.py:32
  31.1 2.9 %collective-permute-start.10 = (s16[2,8448]{1,0:T(2,128)(2,1)S(1)}, s16[2,8448]{1,0:T(2,128)(2,1)S(1)}, u32[]{:S(2)}, u32[]{:S(2)}) collective-permute-start(s16[2,8448]{1,0:T(2,128)(2,1)S(1)} %get-tuple-element.42), channel_id=1, source_target_pairs={{0,12},{1,13},{2,14},{3,15},{4,8},{5,9},{6,10},{7,11},{8,4},{9,5},... | collective-permute-start | bytes 101384 | tf_op jit(solution)/shard_map/ppermute | solution.py:32
  34.1 0.0 collective-permute-done.8.refs_1_
  34.1 0.9 %collective-permute-done.9.refs_2_ = s16[2,8448]{1,0:T(2,128)(2,1)S(1)} collective-permute-done((s16[2,8448]{1,0:T(2,128)(2,1)S(1)}, s16[2,8448]{1,0:T(2,128)(2,1)S(1)}, u32[]{:S(2)}, u32[]{:S(2)}) %collective-permute-start.9) | collective-permute-done | bytes 33824 | tf_op jit(solution)/shard_map/ppermute | solution.py:32
  35.0 1.9 %collective-permute-done.10.refs_3_ = s16[2,8448]{1,0:T(2,128)(2,1)S(1)} collective-permute-done((s16[2,8448]{1,0:T(2,128)(2,1)S(1)}, s16[2,8448]{1,0:T(2,128)(2,1)S(1)}, u32[]{:S(2)}, u32[]{:S(2)}) %collective-permute-start.10) | collective-permute-done | bytes 33824 | tf_op jit(solution)/shard_map/ppermute | solution.py:32
  36.9 1.2 %shard_map.61 = bf16[2,8192]{1,0:T(2,128)(2,1)} custom-call(s16[2,8448]{1,0:T(2,128)(2,1)S(1)} %get-tuple-element.39.refs_0_, s16[2,8448]{1,0:T(2,128)(2,1)S(1)} %collective-permute-done.8.refs_1_, s16[2,8448]{1,0:T(2,128)(2,1)S(1)} %collective-permute-done.9.refs_2_, s16[2,8448]{1,0:T(2,128)(2,1)S(1)} %collective-permute-done.10.refs_3_), custom_call_target="tpu_custom_call" | custom-call | tf_op jit(solution)/shard_map/pallas_call | solution.py:201
Async XLA Ops:
  0.0 17.4 %copy-start = (bf16[512,1024]{1,0:T(8,128)(2,1)S(1)}, bf16[512,1024]{1,0:T(8,128)(2,1)}, u32[]{:S(2)}) copy-start(bf16[512,1024]{1,0:T(8,128)(2,1)} %refs_2_.3) | copy-start | bytes 3145732
  0.0 8.6 %collective-permute-start.1 = (bf16[2,8192]{1,0:T(2,128)(2,1)}, bf16[2,8192]{1,0:T(2,128)(2,1)S(1)}, u32[]{:S(2)}, u32[]{:S(2)}) collective-permute-start(bf16[2,8192]{1,0:T(2,128)(2,1)} %refs_0_), channel_id=1, source_target_pairs={{0,8},{1,9},{2,10},{3,11},{4,12},{5,13},{6,14},{7,15},{8,0},{9,1},... | collective-permute-start | bytes 98312 | tf_op jit(solution)/shard_map/ppermute | solution.py:32
  4.0 4.5 %collective-permute-start = (bf16[2,8192]{1,0:T(2,128)(2,1)}, bf16[2,8192]{1,0:T(2,128)(2,1)S(1)}, u32[]{:S(2)}, u32[]{:S(2)}) collective-permute-start(bf16[2,8192]{1,0:T(2,128)(2,1)} %refs_0_), channel_id=1, source_target_pairs={{0,4},{1,5},{2,6},{3,7},{4,0},{5,1},{6,2},{7,3},{8,12},{9,13},{10,... | collective-permute-start | bytes 98312 | tf_op jit(solution)/shard_map/ppermute | solution.py:32
  5.6 5.9 %collective-permute-start.2 = (bf16[2,8192]{1,0:T(2,128)(2,1)}, bf16[2,8192]{1,0:T(2,128)(2,1)S(1)}, u32[]{:S(2)}, u32[]{:S(2)}) collective-permute-start(bf16[2,8192]{1,0:T(2,128)(2,1)} %refs_0_), channel_id=1, source_target_pairs={{0,12},{1,13},{2,14},{3,15},{4,8},{5,9},{6,10},{7,11},{8,4},{9,5},... | collective-permute-start | bytes 98312 | tf_op jit(solution)/shard_map/ppermute | solution.py:32
  6.3 1.2 %copy-start.1 = (bf16[512,1024]{1,0:T(8,128)(2,1)S(1)}, bf16[512,1024]{1,0:T(8,128)(2,1)}, u32[]{:S(2)}) copy-start(bf16[512,1024]{1,0:T(8,128)(2,1)} %v_ref.1) | copy-start | bytes 3145732
  7.5 0.7 %copy-start.3 = (s32[16,8]{0,1:T(8,128)S(1)}, s32[16,8]{0,1:T(8,128)}, u32[]{:S(2)}) copy-start(s32[16,8]{0,1:T(8,128)} %param.8) | copy-start | bytes 1540
  11.5 0.8 %copy-start.2 = (bf16[2,8192]{1,0:T(2,128)(2,1)S(1)}, bf16[2,8192]{1,0:T(2,128)(2,1)}, u32[]{:S(2)}) copy-start(bf16[2,8192]{1,0:T(2,128)(2,1)} %refs_0_) | copy-start | bytes 98308
  12.4 5.0 %collective-permute-start.4 = (bf16[8,8192]{1,0:T(8,128)(2,1)S(1)}, bf16[8,8192]{1,0:T(8,128)(2,1)S(1)}, u32[]{:S(2)}, u32[]{:S(2)}) collective-permute-start(bf16[8,8192]{1,0:T(8,128)(2,1)S(1)} %shard_map.56.refs_0_), channel_id=1, source_target_pairs={{0,2},{1,3},{2,0},{3,1},{4,6},{5,7},{6,4},{7,5},{8,10},{9,11},{10,... | collective-permute-start | bytes 393224 | tf_op jit(solution)/shard_map/ppermute | solution.py:32
  14.0 5.2 %collective-permute-start.3 = (bf16[8,8192]{1,0:T(8,128)(2,1)S(1)}, bf16[8,8192]{1,0:T(8,128)(2,1)S(1)}, u32[]{:S(2)}, u32[]{:S(2)}) collective-permute-start(bf16[8,8192]{1,0:T(8,128)(2,1)S(1)} %shard_map.56.refs_0_), channel_id=1, source_target_pairs={{0,1},{1,0},{2,3},{3,2},{4,5},{5,4},{6,7},{7,6},{8,9},{9,8},{10,11... | collective-permute-start | bytes 393224 | tf_op jit(solution)/shard_map/ppermute | solution.py:32
  17.4 1.8 %collective-permute-start.5 = (bf16[8,8192]{1,0:T(8,128)(2,1)S(1)}, bf16[8,8192]{1,0:T(8,128)(2,1)S(1)}, u32[]{:S(2)}, u32[]{:S(2)}) collective-permute-start(bf16[8,8192]{1,0:T(8,128)(2,1)S(1)} %collective-permute-done.4.refs_1_), channel_id=1, source_target_pairs={{0,1},{1,0},{2,3},{3,2},{4,5},{5,4},{6,7},{7,6},{8,9},{9,8},{10,11... | collective-permute-start | bytes 393224 | tf_op jit(solution)/shard_map/ppermute | solution.py:32
  21.0 1.7 %collective-permute-start.6 = (s16[16,8448]{1,0:T(8,128)(2,1)S(1)}, s16[16,8448]{1,0:T(8,128)(2,1)S(1)}, u32[]{:S(2)}, u32[]{:S(2)}) collective-permute-start(s16[16,8448]{1,0:T(8,128)(2,1)S(1)} %shard_map.58), channel_id=1, source_target_pairs={{0,1},{1,0},{2,3},{3,2},{4,5},{5,4},{6,7},{7,6},{8,9},{9,8},{10,11... | collective-permute-start | bytes 811016 | tf_op jit(solution)/shard_map/ppermute | solution.py:32
  23.3 5.9 %collective-permute-start.7 = (s16[8,8448]{1,0:T(8,128)(2,1)S(1)}, s16[8,8448]{1,0:T(8,128)(2,1)S(1)}, u32[]{:S(2)}, u32[]{:S(2)}) collective-permute-start(s16[8,8448]{1,0:T(8,128)(2,1)S(1)} %get-tuple-element.38), channel_id=1, source_target_pairs={{0,2},{1,3},{2,0},{3,1},{4,6},{5,7},{6,4},{7,5},{8,10},{9,11},{10,... | collective-permute-start | bytes 405512 | tf_op jit(solution)/shard_map/ppermute | solution.py:32
  29.6 4.5 %collective-permute-start.8 = (s16[2,8448]{1,0:T(2,128)(2,1)S(1)}, s16[2,8448]{1,0:T(2,128)(2,1)S(1)}, u32[]{:S(2)}, u32[]{:S(2)}) collective-permute-start(s16[2,8448]{1,0:T(2,128)(2,1)S(1)} %get-tuple-element.40), channel_id=1, source_target_pairs={{0,4},{1,5},{2,6},{3,7},{4,0},{5,1},{6,2},{7,3},{8,12},{9,13},{10,... | collective-permute-start | bytes 101384 | tf_op jit(solution)/shard_map/ppermute | solution.py:32
  29.7 5.3 %collective-permute-start.9 = (s16[2,8448]{1,0:T(2,128)(2,1)S(1)}, s16[2,8448]{1,0:T(2,128)(2,1)S(1)}, u32[]{:S(2)}, u32[]{:S(2)}) collective-permute-start(s16[2,8448]{1,0:T(2,128)(2,1)S(1)} %get-tuple-element.41), channel_id=1, source_target_pairs={{0,8},{1,9},{2,10},{3,11},{4,12},{5,13},{6,14},{7,15},{8,0},{9,1},... | collective-permute-start | bytes 101384 | tf_op jit(solution)/shard_map/ppermute | solution.py:32
  31.1 5.7 %collective-permute-start.10 = (s16[2,8448]{1,0:T(2,128)(2,1)S(1)}, s16[2,8448]{1,0:T(2,128)(2,1)S(1)}, u32[]{:S(2)}, u32[]{:S(2)}) collective-permute-start(s16[2,8448]{1,0:T(2,128)(2,1)S(1)} %get-tuple-element.42), channel_id=1, source_target_pairs={{0,12},{1,13},{2,14},{3,15},{4,8},{5,9},{6,10},{7,11},{8,4},{9,5},... | collective-permute-start | bytes 101384 | tf_op jit(solution)/shard_map/ppermute | solution.py:32
where the time goes:
time: 38.3 us; the launch traced here: 38 us
  waiting for transfers between devices  14.7 us (38%)
  starting transfers between devices  13.8 us (36%)
  Pallas kernels  6.11 us (16%)
  local copies, waits for them, and re-layouts  2.67 us (7%)
  between operations  0.74 us (2%)
    ppermute x11, waiting for transfers between devices, swap(): return lax.ppermute(array, 'kv', [(i, i ^ delta) for i in range(count)])  14.7 us
    ppermute x11, starting transfers between devices, swap(): return lax.ppermute(array, 'kv', [(i, i ^ delta) for i in range(count)])  13.8 us
    pallas_call x2, Pallas kernels, attend(): pl.pallas_call(functools.partial(attend_kernel, segment=kv_dev // 2), out...  3.54 us
    unnamed x8, local copies, waits for them, and re-layouts  2.67 us
    pallas_call x3, Pallas kernels, combine(): pl.pallas_call(functools.partial(combine_kernel, parts=len(arrays), heads...  2.1 us
  transfers between devices with their start and end apart: 11, of which 6 were waited for; matrix products, arithmetic and copies ran while one was open for 0% of the time, Pallas kernels for 6%

commit v1 on v0

--- a/solution.py
+++ b/solution.py
@@ -87,10 +87,12 @@
     )(*pieces)
 
 
-def attend_kernel(*refs, segment):
+def attend_kernel(*refs, segment, first):
     *q_refs, k_ref, vt_ref, bias_ref, out_ref = refs
-    queries_all = jnp.concatenate([ref[...] for ref in q_refs], 0)
-    rows, width = queries_all.shape
+    width = out_ref.shape[1] - STATS
+    start = first * GROUP * HD
+    queries_all = jnp.concatenate([ref[:, start : start + width] for ref in q_refs], 0)
+    rows = queries_all.shape[0]
     kv_heads = width // (GROUP * HD)
     segments = k_ref.shape[0] // segment
     lanes = GROUP * rows
@@ -106,7 +108,7 @@
         for s in range(segments):
             at = slice(s * segment, (s + 1) * segment)
             scores = lax.dot_general(
-                k_ref[at, g * HD : (g + 1) * HD],
+                k_ref[at, (first + g) * HD : (first + g + 1) * HD],
                 queries,
                 (((1,), (1,)), ((), ())),
                 preferred_element_type=jnp.float32,
@@ -118,7 +120,7 @@
             totals.append(jnp.sum(weights, 0, keepdims=True))
             outs.append(
                 jnp.dot(
-                    vt_ref[g * HD : (g + 1) * HD, at],
+                    vt_ref[(first + g) * HD : (first + g + 1) * HD, at],
                     weights.astype(jnp.bfloat16),
                     preferred_element_type=jnp.float32,
                 )
@@ -138,7 +140,7 @@
         values = [fixed >> 16, (fixed & 0xFFFF) - 32768, power]
         for kind in range(KINDS):
             stats = jnp.where(
-                target == kind * SLOT + g * GROUP + head_of,
+                target == kind * SLOT + (first + g) * GROUP + head_of,
                 values[kind].astype(jnp.float32),
                 stats,
             )
@@ -149,16 +151,21 @@
     out_ref[:, kv_heads * GROUP * HD :] = packed.astype(jnp.int32).astype(jnp.int16)
 
 
-def combine_kernel(*refs, parts, heads, final):
-    in_refs, out_refs = refs[:parts], refs[parts:]
+def combine_kernel(*refs, layout, heads, final):
     wide = heads * HD
-    rows = in_refs[0].shape[0]
+    sources = []
+    for number in layout:
+        sources.append(refs[:number])
+        refs = refs[number:]
+    out_refs = refs
+    rows = sources[0][0].shape[0]
     chunk = rows // len(out_refs)
     fixed, powers = [], []
-    for ref in in_refs:
-        stats = ref[:, wide : wide + HD].astype(jnp.int32)
-        fixed.append((stats << 16) + pltpu.roll(stats, SLOT, 1) + 32768)
-        powers.append(ref[:, wide + HD :].astype(jnp.int32).astype(jnp.float32))
+    for source in sources:
+        stats = sum(ref[:, wide // len(source) :].astype(jnp.int32) for ref in source)
+        level = stats[:, :HD]
+        fixed.append((level << 16) + pltpu.roll(level, SLOT, 1) + 32768)
+        powers.append(stats[:, HD:].astype(jnp.float32))
     top = functools.reduce(jnp.maximum, fixed)
     weights = [jnp.exp2((f - top).astype(jnp.float32) * (1.0 / FIX)) for f in fixed]
     total = sum(weights)
@@ -172,10 +179,12 @@
         factors = [a * back for a in amounts]
     for h in range(heads):
         at = slice(h * HD, (h + 1) * HD)
-        out = sum(
-            f[:, h : h + 1] * ref[:, at].astype(jnp.int32).astype(jnp.float32)
-            for f, ref in zip(factors, in_refs)
-        )
+        values = []
+        for source in sources:
+            share = heads // len(source)
+            ref, local = source[h // share], h % share
+            values.append(ref[:, local * HD : (local + 1) * HD].astype(jnp.int32))
+        out = sum(f[:, h : h + 1] * v.astype(jnp.float32) for f, v in zip(factors, values))
         if final:
             out = out.astype(jnp.bfloat16)
         else:
@@ -194,17 +203,37 @@
             out_ref[:, wide:] = packed[c * chunk : (c + 1) * chunk]
 
 
-def combine(arrays, pieces, heads, final):
-    rows = arrays[0].shape[0]
-    width = heads * HD if final else arrays[0].shape[1]
+def combine(sources, pieces, heads, final):
+    rows = sources[0][0].shape[0]
+    width = heads * HD + (0 if final else STATS)
     dtype = jnp.bfloat16 if final else jnp.int16
+    arrays = [array for source in sources for array in source]
     return pl.pallas_call(
-        functools.partial(combine_kernel, parts=len(arrays), heads=heads, final=final),
+        functools.partial(
+            combine_kernel, layout=[len(source) for source in sources], heads=heads, final=final
+        ),
         out_shape=[jax.ShapeDtypeStruct((rows // pieces, width), dtype)] * pieces,
         in_specs=[VMEM] * len(arrays),
         out_specs=[VMEM] * pieces,
         compiler_params=PARAMS,
     )(*arrays)
+
+
+def fetch_kernel(in_ref, out_ref, sem):
+    copy = pltpu.make_async_copy(in_ref, out_ref, sem)
+    copy.start()
+    copy.wait()
+
+
+def fetch(array):
+    return pl.pallas_call(
+        fetch_kernel,
+        out_shape=jax.ShapeDtypeStruct(array.shape, array.dtype),
+        in_specs=[pl.BlockSpec(memory_space=pl.ANY)],
+        out_specs=VMEM,
+        scratch_shapes=[pltpu.SemaphoreType.DMA],
+        compiler_params=PARAMS,
+    )(array)
 
 
 def on_device(queries, keys, values, block_live, span_offset):
@@ -231,40 +260,50 @@
 
     block = queries
     for stage, deltas in enumerate(steps[:-2]):
-        others = [swap(block, d) for d in reversed(deltas[1:])][::-1]
+        others = [swap(block, d) for d in deltas[2:] + deltas[1:2]]
         if stage == 0:
-            block, others, prepared = lax.optimization_barrier((block, others, prepared))
-        block = join([block] + others)
-    v_turned, *biases = prepared
+            others, block = lax.optimization_barrier((others, fetch(block)))
+        block = join([block] + others[-1:] + others[:-1])
     pieces = [block]
     for deltas in steps[-2:]:
-        pieces = pieces + [swap(p, d) for d in deltas[1:] for p in pieces]
-
-    def attend(pieces, bias):
+        moved = [swap(p, d) for d in deltas[1:] for p in pieces]
+        if deltas is steps[-2]:
+            moved, prepared = lax.optimization_barrier((moved, prepared))
+        pieces = pieces + moved
+    v_turned, *biases = prepared
+
+    def attend(pieces, bias, part, cuts):
+        width = q_width // cuts
         return pl.pallas_call(
-            functools.partial(attend_kernel, segment=kv_dev // 2),
-            out_shape=jax.ShapeDtypeStruct((chunk, q_width + STATS), jnp.int16),
+            functools.partial(
+                attend_kernel, segment=kv_dev // 2, first=part * (heads // GROUP // cuts)
+            ),
+            out_shape=jax.ShapeDtypeStruct((chunk, width + STATS), jnp.int16),
             in_specs=[VMEM] * (len(pieces) + 3),
             out_specs=VMEM,
             compiler_params=PARAMS,
             cost_estimate=pl.CostEstimate(
-                flops=4 * chunk * q_width * kv_dev,
-                bytes_accessed=4 * 2**20,
-                transcendentals=chunk * heads * kv_dev,
+                flops=4 * chunk * width * kv_dev,
+                bytes_accessed=4 * 2**20 // cuts,
+                transcendentals=chunk * width // HD * kv_dev,
             ),
         )(*pieces, keys, v_turned, bias)
 
     share = len(pieces) // parts
-    first = attend(pieces[:share], biases[0])
-    *others, first = lax.optimization_barrier((*pieces[share:], first))
-    outs = [first] + [
-        attend(others[c * share : (c + 1) * share], biases[c + 1]) for c in range(parts - 1)
+    early = attend(pieces[:share], biases[0], 0, 2)
+    *others, early = lax.optimization_barrier((*pieces[share:], early))
+    late = [
+        attend(others[c * share : (c + 1) * share], biases[c + 1], 0, 1) for c in range(parts - 1)
     ]
+    outs = [early] + late
     splits = [len(deltas) for deltas in steps[::-1]] + [1]
     for stage, deltas in enumerate(steps[::-1]):
-        sent = [swap(p, d) for p, d in zip(outs[:0:-1], deltas[:0:-1])]
-        arrays = [outs[0]] + sent[::-1]
-        outs = combine(arrays, splits[stage + 1], heads, stage == len(steps) - 1)
+        sources = [[swap(p, d)] for p, d in zip(outs[:0:-1], deltas[:0:-1])]
+        own = [outs[0]]
+        if stage == 0:
+            own.append(attend(pieces[:share], biases[0], 1, 2))
+            own[1], sources = lax.optimization_barrier((own[1], sources))
+        outs = combine([own] + sources, splits[stage + 1], heads, stage == len(steps) - 1)
     return outs[0]
 
 

time: 38.3 us -> 34.9 us (0.911)
  waiting for transfers between devices: 14.7 us -> 10.9 us
  Pallas kernels: 6.11 us -> 6.55 us
    ppermute x11, waiting for transfers between devices: 14.7 us -> 10.9 us  [swap(): return lax.ppermute(array, 'kv', [(i, i ^ delta) for i in range(count)])]
    pallas_call x5 -> x7, Pallas kernels: 5.64 us -> 6.09 us  [the longest x3 3.96 us: attend(): pl.pallas_call(functools.partial(attend_kernel, segment=kv_dev // 2, firs...]
  transfers between devices with their start and end apart: 11 -> 11, of which waited for: 6 -> 9; matrix products, arithmetic and copies ran while one was open for 0% -> 0% of each run, Pallas kernels for 6% -> 8%
where the time goes in v1:
time: 34.9 us; the launch traced here: 34.7 us
  starting transfers between devices  13.8 us (40%)
  waiting for transfers between devices  10.9 us (31%)
  Pallas kernels  6.55 us (19%)
  local copies, waits for them, and re-layouts  2.7 us (8%)
  between operations  0.73 us (2%)
    ppermute x11, starting transfers between devices, swap(): return lax.ppermute(array, 'kv', [(i, i ^ delta) for i in range(count)])  13.8 us
    ppermute x11, waiting for transfers between devices, swap(): return lax.ppermute(array, 'kv', [(i, i ^ delta) for i in range(count)])  10.9 us
    pallas_call x3, Pallas kernels, attend(): pl.pallas_call(functools.partial(attend_kernel, segment=kv_dev // 2, firs...  3.96 us
    unnamed x8, local copies, waits for them, and re-layouts  2.7 us
    pallas_call x3, Pallas kernels, combine(): pl.pallas_call(functools.partial(combine_kernel, layout=[len(source) for...  2.1 us
  transfers between devices with their start and end apart: 11, of which 9 were waited for; matrix products, arithmetic and copies ran while one was open for 0% of the time, Pallas kernels for 8%

profile of v1, /device:TPU:0, one launch (start us, length us, event | category | flops | bytes accessed | tf_op | source)
XLA Modules:
  0.0 34.7 jit_solution(6418277468394200946)
XLA Ops:
  0.0 0.0 copy-start
  0.0 5.0 %collective-permute-start.1 = (bf16[2,8192]{1,0:T(2,128)(2,1)}, bf16[2,8192]{1,0:T(2,128)(2,1)S(1)}, u32[]{:S(2)}, u32[]{:S(2)}) collective-permute-start(bf16[2,8192]{1,0:T(2,128)(2,1)} %in_ref.1), channel_id=1, source_target_pairs={{0,12},{1,13},{2,14},{3,15},{4,8},{5,9},{6,10},{7,11},{8,4},{9,5},... | collective-permute-start | bytes 98312 | tf_op jit(solution)/shard_map/ppermute | solution.py:32
  5.1 0.0 collective-permute-start
  5.1 0.6 %collective-permute-start.2 = (bf16[2,8192]{1,0:T(2,128)(2,1)}, bf16[2,8192]{1,0:T(2,128)(2,1)S(1)}, u32[]{:S(2)}, u32[]{:S(2)}) collective-permute-start(bf16[2,8192]{1,0:T(2,128)(2,1)} %in_ref.1), channel_id=1, source_target_pairs={{0,4},{1,5},{2,6},{3,7},{4,0},{5,1},{6,2},{7,3},{8,12},{9,13},{10,... | collective-permute-start | bytes 98312 | tf_op jit(solution)/shard_map/ppermute | solution.py:32
  5.7 0.0 copy-start.2
  5.7 0.8 %copy-done.2 = bf16[2,8192]{1,0:T(2,128)(2,1)S(1)} copy-done((bf16[2,8192]{1,0:T(2,128)(2,1)S(1)}, bf16[2,8192]{1,0:T(2,128)(2,1)}, u32[]{:S(2)}) %copy-start.2) | copy-done | bytes 32792
  6.5 0.7 %collective-permute-done.1.refs_3_ = bf16[2,8192]{1,0:T(2,128)(2,1)S(1)} collective-permute-done((bf16[2,8192]{1,0:T(2,128)(2,1)}, bf16[2,8192]{1,0:T(2,128)(2,1)S(1)}, u32[]{:S(2)}, u32[]{:S(2)}) %collective-permute-start.1) | collective-permute-done | bytes 32800 | tf_op jit(solution)/shard_map/ppermute | solution.py:32
  7.2 2.9 %collective-permute-done.refs_2_ = bf16[2,8192]{1,0:T(2,128)(2,1)S(1)} collective-permute-done((bf16[2,8192]{1,0:T(2,128)(2,1)}, bf16[2,8192]{1,0:T(2,128)(2,1)S(1)}, u32[]{:S(2)}, u32[]{:S(2)}) %collective-permute-start) | collective-permute-done | bytes 32800 | tf_op jit(solution)/shard_map/ppermute | solution.py:32
  10.1 0.0 collective-permute-done.2.refs_1_
  10.1 0.1 shard_map.56.refs_0_
  10.2 1.6 %collective-permute-start.4 = (bf16[8,8192]{1,0:T(8,128)(2,1)S(1)}, bf16[8,8192]{1,0:T(8,128)(2,1)S(1)}, u32[]{:S(2)}, u32[]{:S(2)}) collective-permute-start(bf16[8,8192]{1,0:T(8,128)(2,1)S(1)} %shard_map.56.refs_0_), channel_id=1, source_target_pairs={{0,2},{1,3},{2,0},{3,1},{4,6},{5,7},{6,4},{7,5},{8,10},{9,11},{10,... | collective-permute-start | bytes 393224 | tf_op jit(solution)/shard_map/ppermute | solution.py:32
  12.4 0.0 copy-start.1
  12.4 1.2 %copy-done.1 = bf16[512,1024]{1,0:T(8,128)(2,1)S(1)} copy-done((bf16[512,1024]{1,0:T(8,128)(2,1)S(1)}, bf16[512,1024]{1,0:T(8,128)(2,1)}, u32[]{:S(2)}) %copy-start.1) | copy-done | bytes 1048600
  13.6 0.0 copy-start.3
  13.6 0.7 %copy-done.3 = s32[16,8]{0,1:T(8,128)S(1)} copy-done((s32[16,8]{0,1:T(8,128)S(1)}, s32[16,8]{0,1:T(8,128)}, u32[]{:S(2)}) %copy-start.3) | copy-done | bytes 536
  14.3 0.4 %shard_map.57 = (bf16[1024,512]{1,0:T(8,128)(2,1)S(1)}, f32[512,128]{1,0:T(8,128)S(1)}, f32[512,128]{1,0:T(8,128)S(1)}) custom-call(bf16[512,1024]{1,0:T(8,128)(2,1)S(1)} %copy-done.1, s32[8,16]{1,0:T(8,128)S(1)} %bitcast.1, s32[1]{0:T(128)S(6)} %copy.6.offset_ref), custom_call_target="tpu_custom_call" | custom-call | bytes 4194304 | tf_op jit(solution)/shard_map/pallas_call | solution.py:251
  14.7 0.1 collective-permute-start.3
  14.8 0.4 %collective-permute-done.4.refs_1_ = bf16[8,8192]{1,0:T(8,128)(2,1)S(1)} collective-permute-done((bf16[8,8192]{1,0:T(8,128)(2,1)S(1)}, bf16[8,8192]{1,0:T(8,128)(2,1)S(1)}, u32[]{:S(2)}, u32[]{:S(2)}) %collective-permute-start.4) | collective-permute-done | bytes 131104 | tf_op jit(solution)/shard_map/ppermute | solution.py:32
  15.2 0.1 collective-permute-start.5
  15.3 0.0 copy-done
  15.3 1.1 %shard_map.58.refs_0_ = s16[16,4352]{1,0:T(8,128)(2,1)S(1)} custom-call(bf16[8,8192]{1,0:T(8,128)(2,1)S(1)} %shard_map.56.refs_0_, bf16[8,8192]{1,0:T(8,128)(2,1)S(1)} %collective-permute-done.4.refs_1_, bf16[512,1024]{1,0:T(8,128)(2,1)S(1)} %copy-done, bf16[1024,512]{1,0:T(8,128)(2,1)S(1)} %get-tuple-element.35.refs_3_, ...), custom_call_target="tpu_custom_call" | custom-call | flops 134217728 | bytes 2097152 | tf_op jit(solution)/shard_map/pallas_call | solution.py:277
  16.4 0.0 collective-permute-done.3.refs_0_
  16.4 0.1 collective-permute-done.5.refs_1_
  16.6 1.7 %shard_map.60 = s16[16,8448]{1,0:T(8,128)(2,1)S(1)} custom-call(bf16[8,8192]{1,0:T(8,128)(2,1)S(1)} %collective-permute-done.3.refs_0_, bf16[8,8192]{1,0:T(8,128)(2,1)S(1)} %collective-permute-done.5.refs_1_, bf16[512,1024]{1,0:T(8,128)(2,1)S(1)} %copy-done, bf16[1024,512]{1,0:T(8,128)(2,1)S(1)} %get-tuple-element.35.refs_3_, ...), custom_call_target="tpu_custom_call" | custom-call | flops 268435456 | bytes 4194304 | tf_op jit(solution)/shard_map/pallas_call | solution.py:277
  18.3 0.4 %collective-permute-start.6 = (s16[16,8448]{1,0:T(8,128)(2,1)S(1)}, s16[16,8448]{1,0:T(8,128)(2,1)S(1)}, u32[]{:S(2)}, u32[]{:S(2)}) collective-permute-start(s16[16,8448]{1,0:T(8,128)(2,1)S(1)} %shard_map.60), channel_id=1, source_target_pairs={{0,1},{1,0},{2,3},{3,2},{4,5},{5,4},{6,7},{7,6},{8,9},{9,8},{10,11... | collective-permute-start | bytes 811016 | tf_op jit(solution)/shard_map/ppermute | solution.py:32
  18.7 1.1 %shard_map.59.refs_1_ = s16[16,4352]{1,0:T(8,128)(2,1)S(1)} custom-call(bf16[8,8192]{1,0:T(8,128)(2,1)S(1)} %shard_map.56.refs_0_, bf16[8,8192]{1,0:T(8,128)(2,1)S(1)} %collective-permute-done.4.refs_1_, bf16[512,1024]{1,0:T(8,128)(2,1)S(1)} %copy-done, bf16[1024,512]{1,0:T(8,128)(2,1)S(1)} %get-tuple-element.35.refs_3_, ...), custom_call_target="tpu_custom_call" | custom-call | flops 134217728 | bytes 2097152 | tf_op jit(solution)/shard_map/pallas_call | solution.py:277
  19.8 0.1 collective-permute-done.6.refs_2_
  19.9 0.6 %shard_map.61 = (s16[8,8448]{1,0:T(8,128)(2,1)S(1)}, s16[8,8448]{1,0:T(8,128)(2,1)S(1)}) custom-call(s16[16,4352]{1,0:T(8,128)(2,1)S(1)} %shard_map.58.refs_0_, s16[16,4352]{1,0:T(8,128)(2,1)S(1)} %shard_map.59.refs_1_, s16[16,8448]{1,0:T(8,128)(2,1)S(1)} %collective-permute-done.6.refs_2_), custom_call_target="tpu_custom_call" | custom-call | tf_op jit(solution)/shard_map/pallas_call | solution.py:211
  20.5 1.6 %collective-permute-start.7 = (s16[8,8448]{1,0:T(8,128)(2,1)S(1)}, s16[8,8448]{1,0:T(8,128)(2,1)S(1)}, u32[]{:S(2)}, u32[]{:S(2)}) collective-permute-start(s16[8,8448]{1,0:T(8,128)(2,1)S(1)} %get-tuple-element.44), channel_id=1, source_target_pairs={{0,2},{1,3},{2,0},{3,1},{4,6},{5,7},{6,4},{7,5},{8,10},{9,11},{10,... | collective-permute-start | bytes 405512 | tf_op jit(solution)/shard_map/ppermute | solution.py:32
  22.0 4.3 %collective-permute-done.7.refs_1_ = s16[8,8448]{1,0:T(8,128)(2,1)S(1)} collective-permute-done((s16[8,8448]{1,0:T(8,128)(2,1)S(1)}, s16[8,8448]{1,0:T(8,128)(2,1)S(1)}, u32[]{:S(2)}, u32[]{:S(2)}) %collective-permute-start.7) | collective-permute-done | bytes 135200 | tf_op jit(solution)/shard_map/ppermute | solution.py:32
  26.3 0.4 %shard_map.62 = (s16[2,8448]{1,0:T(2,128)(2,1)S(1)}, s16[2,8448]{1,0:T(2,128)(2,1)S(1)}, s16[2,8448]{1,0:T(2,128)(2,1)S(1)}, s16[2,8448]{1,0:T(2,128)(2,1)S(1)}) custom-call(s16[8,8448]{1,0:T(8,128)(2,1)S(1)} %get-tuple-element.43.refs_0_, s16[8,8448]{1,0:T(8,128)(2,1)S(1)} %collective-permute-done.7.refs_1_), custom_call_target="tpu_custom_call" | custom-call | tf_op jit(solution)/shard_map/pallas_call | solution.py:211
  26.7 1.6 %collective-permute-start.8 = (s16[2,8448]{1,0:T(2,128)(2,1)S(1)}, s16[2,8448]{1,0:T(2,128)(2,1)S(1)}, u32[]{:S(2)}, u32[]{:S(2)}) collective-permute-start(s16[2,8448]{1,0:T(2,128)(2,1)S(1)} %get-tuple-element.46), channel_id=1, source_target_pairs={{0,12},{1,13},{2,14},{3,15},{4,8},{5,9},{6,10},{7,11},{8,4},{9,5},... | collective-permute-start | bytes 101384 | tf_op jit(solution)/shard_map/ppermute | solution.py:32
  28.3 0.6 %collective-permute-start.9 = (s16[2,8448]{1,0:T(2,128)(2,1)S(1)}, s16[2,8448]{1,0:T(2,128)(2,1)S(1)}, u32[]{:S(2)}, u32[]{:S(2)}) collective-permute-start(s16[2,8448]{1,0:T(2,128)(2,1)S(1)} %get-tuple-element.47), channel_id=1, source_target_pairs={{0,8},{1,9},{2,10},{3,11},{4,12},{5,13},{6,14},{7,15},{8,0},{9,1},... | collective-permute-start | bytes 101384 | tf_op jit(solution)/shard_map/ppermute | solution.py:32
  28.9 2.3 %collective-permute-start.10 = (s16[2,8448]{1,0:T(2,128)(2,1)S(1)}, s16[2,8448]{1,0:T(2,128)(2,1)S(1)}, u32[]{:S(2)}, u32[]{:S(2)}) collective-permute-start(s16[2,8448]{1,0:T(2,128)(2,1)S(1)} %get-tuple-element.48), channel_id=1, source_target_pairs={{0,4},{1,5},{2,6},{3,7},{4,0},{5,1},{6,2},{7,3},{8,12},{9,13},{10,... | collective-permute-start | bytes 101384 | tf_op jit(solution)/shard_map/ppermute | solution.py:32
  31.2 1.8 %collective-permute-done.8.refs_1_ = s16[2,8448]{1,0:T(2,128)(2,1)S(1)} collective-permute-done((s16[2,8448]{1,0:T(2,128)(2,1)S(1)}, s16[2,8448]{1,0:T(2,128)(2,1)S(1)}, u32[]{:S(2)}, u32[]{:S(2)}) %collective-permute-start.8) | collective-permute-done | bytes 33824 | tf_op jit(solution)/shard_map/ppermute | solution.py:32
  32.9 0.3 collective-permute-done.9.refs_2_
  33.3 0.2 collective-permute-done.10.refs_3_
  33.5 1.2 %shard_map.63 = bf16[2,8192]{1,0:T(2,128)(2,1)} custom-call(s16[2,8448]{1,0:T(2,128)(2,1)S(1)} %get-tuple-element.45.refs_0_, s16[2,8448]{1,0:T(2,128)(2,1)S(1)} %collective-permute-done.8.refs_1_, s16[2,8448]{1,0:T(2,128)(2,1)S(1)} %collective-permute-done.9.refs_2_, s16[2,8448]{1,0:T(2,128)(2,1)S(1)} %collective-permute-done.10.refs_3_), custom_call_target="tpu_custom_call" | custom-call | tf_op jit(solution)/shard_map/pallas_call | solution.py:211
  (1 shorter events, 0.0 us)
Async XLA Ops:
  0.0 15.3 %copy-start = (bf16[512,1024]{1,0:T(8,128)(2,1)S(1)}, bf16[512,1024]{1,0:T(8,128)(2,1)}, u32[]{:S(2)}) copy-start(bf16[512,1024]{1,0:T(8,128)(2,1)} %refs_2_.5) | copy-start | bytes 3145732
  0.0 7.2 %collective-permute-start.1 = (bf16[2,8192]{1,0:T(2,128)(2,1)}, bf16[2,8192]{1,0:T(2,128)(2,1)S(1)}, u32[]{:S(2)}, u32[]{:S(2)}) collective-permute-start(bf16[2,8192]{1,0:T(2,128)(2,1)} %in_ref.1), channel_id=1, source_target_pairs={{0,12},{1,13},{2,14},{3,15},{4,8},{5,9},{6,10},{7,11},{8,4},{9,5},... | collective-permute-start | bytes 98312 | tf_op jit(solution)/shard_map/ppermute | solution.py:32
  5.1 5.0 %collective-permute-start = (bf16[2,8192]{1,0:T(2,128)(2,1)}, bf16[2,8192]{1,0:T(2,128)(2,1)S(1)}, u32[]{:S(2)}, u32[]{:S(2)}) collective-permute-start(bf16[2,8192]{1,0:T(2,128)(2,1)} %in_ref.1), channel_id=1, source_target_pairs={{0,8},{1,9},{2,10},{3,11},{4,12},{5,13},{6,14},{7,15},{8,0},{9,1},... | collective-permute-start | bytes 98312 | tf_op jit(solution)/shard_map/ppermute | solution.py:32
  5.1 5.0 %collective-permute-start.2 = (bf16[2,8192]{1,0:T(2,128)(2,1)}, bf16[2,8192]{1,0:T(2,128)(2,1)S(1)}, u32[]{:S(2)}, u32[]{:S(2)}) collective-permute-start(bf16[2,8192]{1,0:T(2,128)(2,1)} %in_ref.1), channel_id=1, source_target_pairs={{0,4},{1,5},{2,6},{3,7},{4,0},{5,1},{6,2},{7,3},{8,12},{9,13},{10,... | collective-permute-start | bytes 98312 | tf_op jit(solution)/shard_map/ppermute | solution.py:32
  5.7 0.8 %copy-start.2 = (bf16[2,8192]{1,0:T(2,128)(2,1)S(1)}, bf16[2,8192]{1,0:T(2,128)(2,1)}, u32[]{:S(2)}) copy-start(bf16[2,8192]{1,0:T(2,128)(2,1)} %in_ref.1) | copy-start | bytes 98308
  10.2 5.0 %collective-permute-start.4 = (bf16[8,8192]{1,0:T(8,128)(2,1)S(1)}, bf16[8,8192]{1,0:T(8,128)(2,1)S(1)}, u32[]{:S(2)}, u32[]{:S(2)}) collective-permute-start(bf16[8,8192]{1,0:T(8,128)(2,1)S(1)} %shard_map.56.refs_0_), channel_id=1, source_target_pairs={{0,2},{1,3},{2,0},{3,1},{4,6},{5,7},{6,4},{7,5},{8,10},{9,11},{10,... | collective-permute-start | bytes 393224 | tf_op jit(solution)/shard_map/ppermute | solution.py:32
  12.4 1.2 %copy-start.1 = (bf16[512,1024]{1,0:T(8,128)(2,1)S(1)}, bf16[512,1024]{1,0:T(8,128)(2,1)}, u32[]{:S(2)}) copy-start(bf16[512,1024]{1,0:T(8,128)(2,1)} %v_ref.1) | copy-start | bytes 3145732
  13.6 0.7 %copy-start.3 = (s32[16,8]{0,1:T(8,128)S(1)}, s32[16,8]{0,1:T(8,128)}, u32[]{:S(2)}) copy-start(s32[16,8]{0,1:T(8,128)} %param.8) | copy-start | bytes 1540
  14.7 1.7 %collective-permute-start.3 = (bf16[8,8192]{1,0:T(8,128)(2,1)S(1)}, bf16[8,8192]{1,0:T(8,128)(2,1)S(1)}, u32[]{:S(2)}, u32[]{:S(2)}) collective-permute-start(bf16[8,8192]{1,0:T(8,128)(2,1)S(1)} %shard_map.56.refs_0_), channel_id=1, source_target_pairs={{0,1},{1,0},{2,3},{3,2},{4,5},{5,4},{6,7},{7,6},{8,9},{9,8},{10,11... | collective-permute-start | bytes 393224 | tf_op jit(solution)/shard_map/ppermute | solution.py:32
  15.2 1.3 %collective-permute-start.5 = (bf16[8,8192]{1,0:T(8,128)(2,1)S(1)}, bf16[8,8192]{1,0:T(8,128)(2,1)S(1)}, u32[]{:S(2)}, u32[]{:S(2)}) collective-permute-start(bf16[8,8192]{1,0:T(8,128)(2,1)S(1)} %collective-permute-done.4.refs_1_), channel_id=1, source_target_pairs={{0,1},{1,0},{2,3},{3,2},{4,5},{5,4},{6,7},{7,6},{8,9},{9,8},{10,11... | collective-permute-start | bytes 393224 | tf_op jit(solution)/shard_map/ppermute | solution.py:32
  18.3 1.6 %collective-permute-start.6 = (s16[16,8448]{1,0:T(8,128)(2,1)S(1)}, s16[16,8448]{1,0:T(8,128)(2,1)S(1)}, u32[]{:S(2)}, u32[]{:S(2)}) collective-permute-start(s16[16,8448]{1,0:T(8,128)(2,1)S(1)} %shard_map.60), channel_id=1, source_target_pairs={{0,1},{1,0},{2,3},{3,2},{4,5},{5,4},{6,7},{7,6},{8,9},{9,8},{10,11... | collective-permute-start | bytes 811016 | tf_op jit(solution)/shard_map/ppermute | solution.py:32
  20.5 5.9 %collective-permute-start.7 = (s16[8,8448]{1,0:T(8,128)(2,1)S(1)}, s16[8,8448]{1,0:T(8,128)(2,1)S(1)}, u32[]{:S(2)}, u32[]{:S(2)}) collective-permute-start(s16[8,8448]{1,0:T(8,128)(2,1)S(1)} %get-tuple-element.44), channel_id=1, source_target_pairs={{0,2},{1,3},{2,0},{3,1},{4,6},{5,7},{6,4},{7,5},{8,10},{9,11},{10,... | collective-permute-start | bytes 405512 | tf_op jit(solution)/shard_map/ppermute | solution.py:32
  26.7 6.2 %collective-permute-start.8 = (s16[2,8448]{1,0:T(2,128)(2,1)S(1)}, s16[2,8448]{1,0:T(2,128)(2,1)S(1)}, u32[]{:S(2)}, u32[]{:S(2)}) collective-permute-start(s16[2,8448]{1,0:T(2,128)(2,1)S(1)} %get-tuple-element.46), channel_id=1, source_target_pairs={{0,12},{1,13},{2,14},{3,15},{4,8},{5,9},{6,10},{7,11},{8,4},{9,5},... | collective-permute-start | bytes 101384 | tf_op jit(solution)/shard_map/ppermute | solution.py:32
  28.3 5.0 %collective-permute-start.9 = (s16[2,8448]{1,0:T(2,128)(2,1)S(1)}, s16[2,8448]{1,0:T(2,128)(2,1)S(1)}, u32[]{:S(2)}, u32[]{:S(2)}) collective-permute-start(s16[2,8448]{1,0:T(2,128)(2,1)S(1)} %get-tuple-element.47), channel_id=1, source_target_pairs={{0,8},{1,9},{2,10},{3,11},{4,12},{5,13},{6,14},{7,15},{8,0},{9,1},... | collective-permute-start | bytes 101384 | tf_op jit(solution)/shard_map/ppermute | solution.py:32
  28.9 4.6 %collective-permute-start.10 = (s16[2,8448]{1,0:T(2,128)(2,1)S(1)}, s16[2,8448]{1,0:T(2,128)(2,1)S(1)}, u32[]{:S(2)}, u32[]{:S(2)}) collective-permute-start(s16[2,8448]{1,0:T(2,128)(2,1)S(1)} %get-tuple-element.48), channel_id=1, source_target_pairs={{0,4},{1,5},{2,6},{3,7},{4,0},{5,1},{6,2},{7,3},{8,12},{9,13},{10,... | collective-permute-start | bytes 101384 | tf_op jit(solution)/shard_map/ppermute | solution.py:32

commit v2 on v1

--- a/solution.py
+++ b/solution.py
@@ -20,9 +20,11 @@
 STEPS = 32766.0
 NO_WEIGHT = -8191.0
 MASKED = -1e30
+AHEAD = 1
 KINDS = 3
 SLOT = HD // 2
 STATS = 2 * HD
+KV_SLOT = SLOT // GROUP
 VMEM = pl.BlockSpec(memory_space=pltpu.VMEM)
 PARAMS = pltpu.CompilerParams(vmem_limit_bytes=24 * 2**20)
 
@@ -96,35 +98,48 @@
     kv_heads = width // (GROUP * HD)
     segments = k_ref.shape[0] // segment
     lanes = GROUP * rows
-    target = lax.broadcasted_iota(jnp.int32, (STATS, lanes), 0)
-    head_of = lax.broadcasted_iota(jnp.int32, (STATS, lanes), 1) // rows
-    stats = jnp.zeros((STATS, lanes), jnp.float32)
-    for g in range(kv_heads):
-        queries = jnp.concatenate(
-            [queries_all[:, (g * GROUP + h) * HD : (g * GROUP + h + 1) * HD] for h in range(GROUP)],
-            0,
-        )
-        peaks, totals, outs = [], [], []
-        for s in range(segments):
-            at = slice(s * segment, (s + 1) * segment)
-            scores = lax.dot_general(
-                k_ref[at, (first + g) * HD : (first + g + 1) * HD],
-                queries,
-                (((1,), (1,)), ((), ())),
+    stats = [[jnp.zeros((1, lanes), jnp.float32)] * KV_SLOT for _ in range(KINDS)]
+    tiles = [(g, s) for g in range(kv_heads) for s in range(segments)]
+    queries = {}
+
+    def score(g, s):
+        if g not in queries:
+            queries[g] = jnp.concatenate(
+                [
+                    queries_all[:, (g * GROUP + h) * HD : (g * GROUP + h + 1) * HD]
+                    for h in range(GROUP)
+                ],
+                0,
+            )
+        at = slice(s * segment, (s + 1) * segment)
+        scores = lax.dot_general(
+            k_ref[at, (first + g) * HD : (first + g + 1) * HD],
+            queries[g],
+            (((1,), (1,)), ((), ())),
+            preferred_element_type=jnp.float32,
+        )
+        return scores + bias_ref[at, :]
+
+    ahead = [score(*tile) for tile in tiles[:AHEAD]]
+    for index, (g, s) in enumerate(tiles):
+        if index + AHEAD < len(tiles):
+            ahead.append(score(*tiles[index + AHEAD]))
+        scores = ahead.pop(0)
+        if s == 0:
+            peaks, totals, outs = [], [], []
+        peak = jnp.maximum(jnp.max(scores, 0, keepdims=True), SCORE_FLOOR * ROOT)
+        weights = jnp.exp2((scores - peak) * TO_BITS)
+        peaks.append(peak)
+        totals.append(jnp.sum(weights, 0, keepdims=True))
+        outs.append(
+            jnp.dot(
+                vt_ref[(first + g) * HD : (first + g + 1) * HD, s * segment : (s + 1) * segment],
+                weights.astype(jnp.bfloat16),
                 preferred_element_type=jnp.float32,
             )
-            scores = scores + bias_ref[at, :]
-            peak = jnp.maximum(jnp.max(scores, 0, keepdims=True), SCORE_FLOOR * ROOT)
-            weights = jnp.exp2((scores - peak) * TO_BITS)
-            peaks.append(peak)
-            totals.append(jnp.sum(weights, 0, keepdims=True))
-            outs.append(
-                jnp.dot(
-                    vt_ref[(first + g) * HD : (first + g + 1) * HD, at],
-                    weights.astype(jnp.bfloat16),
-                    preferred_element_type=jnp.float32,
-                )
-            )
+        )
+        if s < segments - 1:
+            continue
         top = functools.reduce(jnp.maximum, peaks)
         scales = [jnp.exp2((peak - top) * TO_BITS) for peak in peaks]
         total = sum(e * t for e, t in zip(scales, totals))
@@ -139,16 +154,23 @@
         fixed = jnp.round(level * FIX).astype(jnp.int32)
         values = [fixed >> 16, (fixed & 0xFFFF) - 32768, power]
         for kind in range(KINDS):
-            stats = jnp.where(
-                target == kind * SLOT + (first + g) * GROUP + head_of,
-                values[kind].astype(jnp.float32),
-                stats,
-            )
+            stats[kind][first + g] = values[kind].astype(jnp.float32)
         for h in range(GROUP):
             out_ref[:, (g * GROUP + h) * HD : (g * GROUP + h + 1) * HD] = out[h * rows : (h + 1) * rows]
-    stats = stats.T
-    packed = sum(stats[h * rows : (h + 1) * rows] for h in range(GROUP))
-    out_ref[:, kv_heads * GROUP * HD :] = packed.astype(jnp.int32).astype(jnp.int16)
+    gap = jnp.zeros((SLOT - KV_SLOT, lanes), jnp.float32)
+    high, low, power = [jnp.concatenate(kind, 0) for kind in stats]
+    empty = jnp.zeros((KV_SLOT, lanes), jnp.float32)
+    packed = []
+    for upper, lower in ((high, low), (power, empty)):
+        turned = jnp.concatenate([upper, gap, lower, gap], 0).T
+        packed.append(
+            sum(
+                pltpu.roll(turned[h * rows : (h + 1) * rows], h * KV_SLOT, 1) if h else turned[:rows]
+                for h in range(GROUP)
+            )
+        )
+    packed = jnp.concatenate(packed, 1).astype(jnp.int32).astype(jnp.int16)
+    out_ref[:, kv_heads * GROUP * HD :] = packed
 
 
 def combine_kernel(*refs, layout, heads, final):
@@ -184,7 +206,8 @@
             share = heads // len(source)
             ref, local = source[h // share], h % share
             values.append(ref[:, local * HD : (local + 1) * HD].astype(jnp.int32))
-        out = sum(f[:, h : h + 1] * v.astype(jnp.float32) for f, v in zip(factors, values))
+        lane = h % GROUP * KV_SLOT + h // GROUP
+        out = sum(f[:, lane : lane + 1] * v.astype(jnp.float32) for f, v in zip(factors, values))
         if final:
             out = out.astype(jnp.bfloat16)
         else:

time: 34.9 us -> 34.3 us (0.983)
  Pallas kernels: 6.55 us -> 5.71 us
    pallas_call x3, Pallas kernels: 3.96 us -> 3.12 us  [attend(): pl.pallas_call(functools.partial(attend_kernel, segment=kv_dev // 2, firs...]
    ppermute x11, waiting for transfers between devices: 10.9 us -> 11.2 us  [swap(): return lax.ppermute(array, 'kv', [(i, i ^ delta) for i in range(count)])]
  transfers between devices with their start and end apart: 11 -> 11, of which waited for: 9 -> 9; matrix products, arithmetic and copies ran while one was open for 0% -> 0% of each run, Pallas kernels for 8% -> 6%
where the time goes in v2:
time: 34.3 us; the launch traced here: 34.1 us
  starting transfers between devices  13.7 us (40%)
  waiting for transfers between devices  11.2 us (33%)
  Pallas kernels  5.71 us (17%)
  local copies, waits for them, and re-layouts  2.7 us (8%)
  between operations  0.73 us (2%)
    ppermute x11, starting transfers between devices, swap(): return lax.ppermute(array, 'kv', [(i, i ^ delta) for i in range(count)])  13.7 us
    ppermute x11, waiting for transfers between devices, swap(): return lax.ppermute(array, 'kv', [(i, i ^ delta) for i in range(count)])  11.2 us
    pallas_call x3, Pallas kernels, attend(): pl.pallas_call(functools.partial(attend_kernel, segment=kv_dev // 2, firs...  3.12 us
    unnamed x8, local copies, waits for them, and re-layouts  2.7 us
    pallas_call x3, Pallas kernels, combine(): pl.pallas_call(functools.partial(combine_kernel, layout=[len(source) for...  2.1 us
  transfers between devices with their start and end apart: 11, of which 9 were waited for; matrix products, arithmetic and copies ran while one was open for 0% of the time, Pallas kernels for 6%

profile of v2, /device:TPU:0, one launch (start us, length us, event | category | flops | bytes accessed | tf_op | source)
XLA Modules:
  0.0 34.1 jit_solution(13081310237910464760)
XLA Ops:
  0.0 0.0 copy-start
  0.0 5.0 %collective-permute-start.1 = (bf16[2,8192]{1,0:T(2,128)(2,1)}, bf16[2,8192]{1,0:T(2,128)(2,1)S(1)}, u32[]{:S(2)}, u32[]{:S(2)}) collective-permute-start(bf16[2,8192]{1,0:T(2,128)(2,1)} %in_ref.1), channel_id=1, source_target_pairs={{0,12},{1,13},{2,14},{3,15},{4,8},{5,9},{6,10},{7,11},{8,4},{9,5},... | collective-permute-start | bytes 98312 | tf_op jit(solution)/shard_map/ppermute | solution.py:34
  5.1 0.0 collective-permute-start
  5.1 0.6 %collective-permute-start.2 = (bf16[2,8192]{1,0:T(2,128)(2,1)}, bf16[2,8192]{1,0:T(2,128)(2,1)S(1)}, u32[]{:S(2)}, u32[]{:S(2)}) collective-permute-start(bf16[2,8192]{1,0:T(2,128)(2,1)} %in_ref.1), channel_id=1, source_target_pairs={{0,4},{1,5},{2,6},{3,7},{4,0},{5,1},{6,2},{7,3},{8,12},{9,13},{10,... | collective-permute-start | bytes 98312 | tf_op jit(solution)/shard_map/ppermute | solution.py:34
  5.7 0.0 copy-start.2
  5.7 0.8 %copy-done.2 = bf16[2,8192]{1,0:T(2,128)(2,1)S(1)} copy-done((bf16[2,8192]{1,0:T(2,128)(2,1)S(1)}, bf16[2,8192]{1,0:T(2,128)(2,1)}, u32[]{:S(2)}) %copy-start.2) | copy-done | bytes 32792
  6.5 0.7 %collective-permute-done.1.refs_3_ = bf16[2,8192]{1,0:T(2,128)(2,1)S(1)} collective-permute-done((bf16[2,8192]{1,0:T(2,128)(2,1)}, bf16[2,8192]{1,0:T(2,128)(2,1)S(1)}, u32[]{:S(2)}, u32[]{:S(2)}) %collective-permute-start.1) | collective-permute-done | bytes 32800 | tf_op jit(solution)/shard_map/ppermute | solution.py:34
  7.2 2.9 %collective-permute-done.refs_2_ = bf16[2,8192]{1,0:T(2,128)(2,1)S(1)} collective-permute-done((bf16[2,8192]{1,0:T(2,128)(2,1)}, bf16[2,8192]{1,0:T(2,128)(2,1)S(1)}, u32[]{:S(2)}, u32[]{:S(2)}) %collective-permute-start) | collective-permute-done | bytes 32800 | tf_op jit(solution)/shard_map/ppermute | solution.py:34
  10.1 0.0 collective-permute-done.2.refs_1_
  10.1 0.1 shard_map.56.refs_0_
  10.2 1.6 %collective-permute-start.4 = (bf16[8,8192]{1,0:T(8,128)(2,1)S(1)}, bf16[8,8192]{1,0:T(8,128)(2,1)S(1)}, u32[]{:S(2)}, u32[]{:S(2)}) collective-permute-start(bf16[8,8192]{1,0:T(8,128)(2,1)S(1)} %shard_map.56.refs_0_), channel_id=1, source_target_pairs={{0,2},{1,3},{2,0},{3,1},{4,6},{5,7},{6,4},{7,5},{8,10},{9,11},{10,... | collective-permute-start | bytes 393224 | tf_op jit(solution)/shard_map/ppermute | solution.py:34
  12.4 0.0 copy-start.1
  12.4 1.2 %copy-done.1 = bf16[512,1024]{1,0:T(8,128)(2,1)S(1)} copy-done((bf16[512,1024]{1,0:T(8,128)(2,1)S(1)}, bf16[512,1024]{1,0:T(8,128)(2,1)}, u32[]{:S(2)}) %copy-start.1) | copy-done | bytes 1048600
  13.6 0.0 copy-start.3
  13.6 0.7 %copy-done.3 = s32[16,8]{0,1:T(8,128)S(1)} copy-done((s32[16,8]{0,1:T(8,128)S(1)}, s32[16,8]{0,1:T(8,128)}, u32[]{:S(2)}) %copy-start.3) | copy-done | bytes 536
  14.3 0.4 %shard_map.57 = (bf16[1024,512]{1,0:T(8,128)(2,1)S(1)}, f32[512,128]{1,0:T(8,128)S(1)}, f32[512,128]{1,0:T(8,128)S(1)}) custom-call(bf16[512,1024]{1,0:T(8,128)(2,1)S(1)} %copy-done.1, s32[8,16]{1,0:T(8,128)S(1)} %bitcast.1, s32[1]{0:T(128)S(6)} %copy.6.offset_ref), custom_call_target="tpu_custom_call" | custom-call | bytes 4194304 | tf_op jit(solution)/shard_map/pallas_call | solution.py:274
  14.7 0.1 collective-permute-start.3
  14.8 0.4 %collective-permute-done.4.refs_1_ = bf16[8,8192]{1,0:T(8,128)(2,1)S(1)} collective-permute-done((bf16[8,8192]{1,0:T(8,128)(2,1)S(1)}, bf16[8,8192]{1,0:T(8,128)(2,1)S(1)}, u32[]{:S(2)}, u32[]{:S(2)}) %collective-permute-start.4) | collective-permute-done | bytes 131104 | tf_op jit(solution)/shard_map/ppermute | solution.py:34
  15.2 0.1 collective-permute-start.5
  15.3 0.0 copy-done
  15.3 0.9 %shard_map.58.refs_0_ = s16[16,4352]{1,0:T(8,128)(2,1)S(1)} custom-call(bf16[8,8192]{1,0:T(8,128)(2,1)S(1)} %shard_map.56.refs_0_, bf16[8,8192]{1,0:T(8,128)(2,1)S(1)} %collective-permute-done.4.refs_1_, bf16[512,1024]{1,0:T(8,128)(2,1)S(1)} %copy-done, bf16[1024,512]{1,0:T(8,128)(2,1)S(1)} %get-tuple-element.35.refs_3_, ...), custom_call_target="tpu_custom_call" | custom-call | flops 134217728 | bytes 2097152 | tf_op jit(solution)/shard_map/pallas_call | solution.py:300
  16.2 0.0 collective-permute-done.3.refs_0_
  16.2 0.3 %collective-permute-done.5.refs_1_ = bf16[8,8192]{1,0:T(8,128)(2,1)S(1)} collective-permute-done((bf16[8,8192]{1,0:T(8,128)(2,1)S(1)}, bf16[8,8192]{1,0:T(8,128)(2,1)S(1)}, u32[]{:S(2)}, u32[]{:S(2)}) %collective-permute-start.5) | collective-permute-done | bytes 131104 | tf_op jit(solution)/shard_map/ppermute | solution.py:34
  16.6 1.3 %shard_map.60 = s16[16,8448]{1,0:T(8,128)(2,1)S(1)} custom-call(bf16[8,8192]{1,0:T(8,128)(2,1)S(1)} %collective-permute-done.3.refs_0_, bf16[8,8192]{1,0:T(8,128)(2,1)S(1)} %collective-permute-done.5.refs_1_, bf16[512,1024]{1,0:T(8,128)(2,1)S(1)} %copy-done, bf16[1024,512]{1,0:T(8,128)(2,1)S(1)} %get-tuple-element.35.refs_3_, ...), custom_call_target="tpu_custom_call" | custom-call | flops 268435456 | bytes 4194304 | tf_op jit(solution)/shard_map/pallas_call | solution.py:300
  17.9 0.2 collective-permute-start.6
  18.1 0.9 %shard_map.59.refs_1_ = s16[16,4352]{1,0:T(8,128)(2,1)S(1)} custom-call(bf16[8,8192]{1,0:T(8,128)(2,1)S(1)} %shard_map.56.refs_0_, bf16[8,8192]{1,0:T(8,128)(2,1)S(1)} %collective-permute-done.4.refs_1_, bf16[512,1024]{1,0:T(8,128)(2,1)S(1)} %copy-done, bf16[1024,512]{1,0:T(8,128)(2,1)S(1)} %get-tuple-element.35.refs_3_, ...), custom_call_target="tpu_custom_call" | custom-call | flops 134217728 | bytes 2097152 | tf_op jit(solution)/shard_map/pallas_call | solution.py:300
  19.0 0.5 %collective-permute-done.6.refs_2_ = s16[16,8448]{1,0:T(8,128)(2,1)S(1)} collective-permute-done((s16[16,8448]{1,0:T(8,128)(2,1)S(1)}, s16[16,8448]{1,0:T(8,128)(2,1)S(1)}, u32[]{:S(2)}, u32[]{:S(2)}) %collective-permute-start.6) | collective-permute-done | bytes 270368 | tf_op jit(solution)/shard_map/ppermute | solution.py:34
  19.5 0.6 %shard_map.61 = (s16[8,8448]{1,0:T(8,128)(2,1)S(1)}, s16[8,8448]{1,0:T(8,128)(2,1)S(1)}) custom-call(s16[16,4352]{1,0:T(8,128)(2,1)S(1)} %shard_map.58.refs_0_, s16[16,4352]{1,0:T(8,128)(2,1)S(1)} %shard_map.59.refs_1_, s16[16,8448]{1,0:T(8,128)(2,1)S(1)} %collective-permute-done.6.refs_2_), custom_call_target="tpu_custom_call" | custom-call | tf_op jit(solution)/shard_map/pallas_call | solution.py:234
  20.1 1.6 %collective-permute-start.7 = (s16[8,8448]{1,0:T(8,128)(2,1)S(1)}, s16[8,8448]{1,0:T(8,128)(2,1)S(1)}, u32[]{:S(2)}, u32[]{:S(2)}) collective-permute-start(s16[8,8448]{1,0:T(8,128)(2,1)S(1)} %get-tuple-element.44), channel_id=1, source_target_pairs={{0,2},{1,3},{2,0},{3,1},{4,6},{5,7},{6,4},{7,5},{8,10},{9,11},{10,... | collective-permute-start | bytes 405512 | tf_op jit(solution)/shard_map/ppermute | solution.py:34
  21.7 4.1 %collective-permute-done.7.refs_1_ = s16[8,8448]{1,0:T(8,128)(2,1)S(1)} collective-permute-done((s16[8,8448]{1,0:T(8,128)(2,1)S(1)}, s16[8,8448]{1,0:T(8,128)(2,1)S(1)}, u32[]{:S(2)}, u32[]{:S(2)}) %collective-permute-start.7) | collective-permute-done | bytes 135200 | tf_op jit(solution)/shard_map/ppermute | solution.py:34
  25.8 0.4 %shard_map.62 = (s16[2,8448]{1,0:T(2,128)(2,1)S(1)}, s16[2,8448]{1,0:T(2,128)(2,1)S(1)}, s16[2,8448]{1,0:T(2,128)(2,1)S(1)}, s16[2,8448]{1,0:T(2,128)(2,1)S(1)}) custom-call(s16[8,8448]{1,0:T(8,128)(2,1)S(1)} %get-tuple-element.43.refs_0_, s16[8,8448]{1,0:T(8,128)(2,1)S(1)} %collective-permute-done.7.refs_1_), custom_call_target="tpu_custom_call" | custom-call | tf_op jit(solution)/shard_map/pallas_call | solution.py:234
  26.2 1.6 %collective-permute-start.8 = (s16[2,8448]{1,0:T(2,128)(2,1)S(1)}, s16[2,8448]{1,0:T(2,128)(2,1)S(1)}, u32[]{:S(2)}, u32[]{:S(2)}) collective-permute-start(s16[2,8448]{1,0:T(2,128)(2,1)S(1)} %get-tuple-element.46), channel_id=1, source_target_pairs={{0,12},{1,13},{2,14},{3,15},{4,8},{5,9},{6,10},{7,11},{8,4},{9,5},... | collective-permute-start | bytes 101384 | tf_op jit(solution)/shard_map/ppermute | solution.py:34
  27.7 0.6 %collective-permute-start.9 = (s16[2,8448]{1,0:T(2,128)(2,1)S(1)}, s16[2,8448]{1,0:T(2,128)(2,1)S(1)}, u32[]{:S(2)}, u32[]{:S(2)}) collective-permute-start(s16[2,8448]{1,0:T(2,128)(2,1)S(1)} %get-tuple-element.47), channel_id=1, source_target_pairs={{0,8},{1,9},{2,10},{3,11},{4,12},{5,13},{6,14},{7,15},{8,0},{9,1},... | collective-permute-start | bytes 101384 | tf_op jit(solution)/shard_map/ppermute | solution.py:34
  28.3 2.3 %collective-permute-start.10 = (s16[2,8448]{1,0:T(2,128)(2,1)S(1)}, s16[2,8448]{1,0:T(2,128)(2,1)S(1)}, u32[]{:S(2)}, u32[]{:S(2)}) collective-permute-start(s16[2,8448]{1,0:T(2,128)(2,1)S(1)} %get-tuple-element.48), channel_id=1, source_target_pairs={{0,4},{1,5},{2,6},{3,7},{4,0},{5,1},{6,2},{7,3},{8,12},{9,13},{10,... | collective-permute-start | bytes 101384 | tf_op jit(solution)/shard_map/ppermute | solution.py:34
  30.6 1.5 %collective-permute-done.8.refs_1_ = s16[2,8448]{1,0:T(2,128)(2,1)S(1)} collective-permute-done((s16[2,8448]{1,0:T(2,128)(2,1)S(1)}, s16[2,8448]{1,0:T(2,128)(2,1)S(1)}, u32[]{:S(2)}, u32[]{:S(2)}) %collective-permute-start.8) | collective-permute-done | bytes 33824 | tf_op jit(solution)/shard_map/ppermute | solution.py:34
  32.2 0.4 %collective-permute-done.9.refs_2_ = s16[2,8448]{1,0:T(2,128)(2,1)S(1)} collective-permute-done((s16[2,8448]{1,0:T(2,128)(2,1)S(1)}, s16[2,8448]{1,0:T(2,128)(2,1)S(1)}, u32[]{:S(2)}, u32[]{:S(2)}) %collective-permute-start.9) | collective-permute-done | bytes 33824 | tf_op jit(solution)/shard_map/ppermute | solution.py:34
  32.6 0.3 collective-permute-done.10.refs_3_
  32.9 1.2 %shard_map.63 = bf16[2,8192]{1,0:T(2,128)(2,1)} custom-call(s16[2,8448]{1,0:T(2,128)(2,1)S(1)} %get-tuple-element.45.refs_0_, s16[2,8448]{1,0:T(2,128)(2,1)S(1)} %collective-permute-done.8.refs_1_, s16[2,8448]{1,0:T(2,128)(2,1)S(1)} %collective-permute-done.9.refs_2_, s16[2,8448]{1,0:T(2,128)(2,1)S(1)} %collective-permute-done.10.refs_3_), custom_call_target="tpu_custom_call" | custom-call | tf_op jit(solution)/shard_map/pallas_call | solution.py:234
  (1 shorter events, 0.0 us)
Async XLA Ops:
  0.0 15.3 %copy-start = (bf16[512,1024]{1,0:T(8,128)(2,1)S(1)}, bf16[512,1024]{1,0:T(8,128)(2,1)}, u32[]{:S(2)}) copy-start(bf16[512,1024]{1,0:T(8,128)(2,1)} %refs_2_.5) | copy-start | bytes 3145732
  0.0 7.2 %collective-permute-start.1 = (bf16[2,8192]{1,0:T(2,128)(2,1)}, bf16[2,8192]{1,0:T(2,128)(2,1)S(1)}, u32[]{:S(2)}, u32[]{:S(2)}) collective-permute-start(bf16[2,8192]{1,0:T(2,128)(2,1)} %in_ref.1), channel_id=1, source_target_pairs={{0,12},{1,13},{2,14},{3,15},{4,8},{5,9},{6,10},{7,11},{8,4},{9,5},... | collective-permute-start | bytes 98312 | tf_op jit(solution)/shard_map/ppermute | solution.py:34
  5.1 5.0 %collective-permute-start = (bf16[2,8192]{1,0:T(2,128)(2,1)}, bf16[2,8192]{1,0:T(2,128)(2,1)S(1)}, u32[]{:S(2)}, u32[]{:S(2)}) collective-permute-start(bf16[2,8192]{1,0:T(2,128)(2,1)} %in_ref.1), channel_id=1, source_target_pairs={{0,8},{1,9},{2,10},{3,11},{4,12},{5,13},{6,14},{7,15},{8,0},{9,1},... | collective-permute-start | bytes 98312 | tf_op jit(solution)/shard_map/ppermute | solution.py:34
  5.1 5.0 %collective-permute-start.2 = (bf16[2,8192]{1,0:T(2,128)(2,1)}, bf16[2,8192]{1,0:T(2,128)(2,1)S(1)}, u32[]{:S(2)}, u32[]{:S(2)}) collective-permute-start(bf16[2,8192]{1,0:T(2,128)(2,1)} %in_ref.1), channel_id=1, source_target_pairs={{0,4},{1,5},{2,6},{3,7},{4,0},{5,1},{6,2},{7,3},{8,12},{9,13},{10,... | collective-permute-start | bytes 98312 | tf_op jit(solution)/shard_map/ppermute | solution.py:34
  5.7 0.8 %copy-start.2 = (bf16[2,8192]{1,0:T(2,128)(2,1)S(1)}, bf16[2,8192]{1,0:T(2,128)(2,1)}, u32[]{:S(2)}) copy-start(bf16[2,8192]{1,0:T(2,128)(2,1)} %in_ref.1) | copy-start | bytes 98308
  10.2 5.0 %collective-permute-start.4 = (bf16[8,8192]{1,0:T(8,128)(2,1)S(1)}, bf16[8,8192]{1,0:T(8,128)(2,1)S(1)}, u32[]{:S(2)}, u32[]{:S(2)}) collective-permute-start(bf16[8,8192]{1,0:T(8,128)(2,1)S(1)} %shard_map.56.refs_0_), channel_id=1, source_target_pairs={{0,2},{1,3},{2,0},{3,1},{4,6},{5,7},{6,4},{7,5},{8,10},{9,11},{10,... | collective-permute-start | bytes 393224 | tf_op jit(solution)/shard_map/ppermute | solution.py:34
  12.4 1.2 %copy-start.1 = (bf16[512,1024]{1,0:T(8,128)(2,1)S(1)}, bf16[512,1024]{1,0:T(8,128)(2,1)}, u32[]{:S(2)}) copy-start(bf16[512,1024]{1,0:T(8,128)(2,1)} %v_ref.1) | copy-start | bytes 3145732
  13.6 0.7 %copy-start.3 = (s32[16,8]{0,1:T(8,128)S(1)}, s32[16,8]{0,1:T(8,128)}, u32[]{:S(2)}) copy-start(s32[16,8]{0,1:T(8,128)} %param.8) | copy-start | bytes 1540
  14.7 1.5 %collective-permute-start.3 = (bf16[8,8192]{1,0:T(8,128)(2,1)S(1)}, bf16[8,8192]{1,0:T(8,128)(2,1)S(1)}, u32[]{:S(2)}, u32[]{:S(2)}) collective-permute-start(bf16[8,8192]{1,0:T(8,128)(2,1)S(1)} %shard_map.56.refs_0_), channel_id=1, source_target_pairs={{0,1},{1,0},{2,3},{3,2},{4,5},{5,4},{6,7},{7,6},{8,9},{9,8},{10,11... | collective-permute-start | bytes 393224 | tf_op jit(solution)/shard_map/ppermute | solution.py:34
  15.2 1.3 %collective-permute-start.5 = (bf16[8,8192]{1,0:T(8,128)(2,1)S(1)}, bf16[8,8192]{1,0:T(8,128)(2,1)S(1)}, u32[]{:S(2)}, u32[]{:S(2)}) collective-permute-start(bf16[8,8192]{1,0:T(8,128)(2,1)S(1)} %collective-permute-done.4.refs_1_), channel_id=1, source_target_pairs={{0,1},{1,0},{2,3},{3,2},{4,5},{5,4},{6,7},{7,6},{8,9},{9,8},{10,11... | collective-permute-start | bytes 393224 | tf_op jit(solution)/shard_map/ppermute | solution.py:34
  17.9 1.6 %collective-permute-start.6 = (s16[16,8448]{1,0:T(8,128)(2,1)S(1)}, s16[16,8448]{1,0:T(8,128)(2,1)S(1)}, u32[]{:S(2)}, u32[]{:S(2)}) collective-permute-start(s16[16,8448]{1,0:T(8,128)(2,1)S(1)} %shard_map.60), channel_id=1, source_target_pairs={{0,1},{1,0},{2,3},{3,2},{4,5},{5,4},{6,7},{7,6},{8,9},{9,8},{10,11... | collective-permute-start | bytes 811016 | tf_op jit(solution)/shard_map/ppermute | solution.py:34
  20.1 5.7 %collective-permute-start.7 = (s16[8,8448]{1,0:T(8,128)(2,1)S(1)}, s16[8,8448]{1,0:T(8,128)(2,1)S(1)}, u32[]{:S(2)}, u32[]{:S(2)}) collective-permute-start(s16[8,8448]{1,0:T(8,128)(2,1)S(1)} %get-tuple-element.44), channel_id=1, source_target_pairs={{0,2},{1,3},{2,0},{3,1},{4,6},{5,7},{6,4},{7,5},{8,10},{9,11},{10,... | collective-permute-start | bytes 405512 | tf_op jit(solution)/shard_map/ppermute | solution.py:34
  26.2 6.0 %collective-permute-start.8 = (s16[2,8448]{1,0:T(2,128)(2,1)S(1)}, s16[2,8448]{1,0:T(2,128)(2,1)S(1)}, u32[]{:S(2)}, u32[]{:S(2)}) collective-permute-start(s16[2,8448]{1,0:T(2,128)(2,1)S(1)} %get-tuple-element.46), channel_id=1, source_target_pairs={{0,12},{1,13},{2,14},{3,15},{4,8},{5,9},{6,10},{7,11},{8,4},{9,5},... | collective-permute-start | bytes 101384 | tf_op jit(solution)/shard_map/ppermute | solution.py:34
  27.7 4.9 %collective-permute-start.9 = (s16[2,8448]{1,0:T(2,128)(2,1)S(1)}, s16[2,8448]{1,0:T(2,128)(2,1)S(1)}, u32[]{:S(2)}, u32[]{:S(2)}) collective-permute-start(s16[2,8448]{1,0:T(2,128)(2,1)S(1)} %get-tuple-element.47), channel_id=1, source_target_pairs={{0,8},{1,9},{2,10},{3,11},{4,12},{5,13},{6,14},{7,15},{8,0},{9,1},... | collective-permute-start | bytes 101384 | tf_op jit(solution)/shard_map/ppermute | solution.py:34
  28.3 4.6 %collective-permute-start.10 = (s16[2,8448]{1,0:T(2,128)(2,1)S(1)}, s16[2,8448]{1,0:T(2,128)(2,1)S(1)}, u32[]{:S(2)}, u32[]{:S(2)}) collective-permute-start(s16[2,8448]{1,0:T(2,128)(2,1)S(1)} %get-tuple-element.48), channel_id=1, source_target_pairs={{0,4},{1,5},{2,6},{3,7},{4,0},{5,1},{6,2},{7,3},{8,12},{9,13},{10,... | collective-permute-start | bytes 101384 | tf_op jit(solution)/shard_map/ppermute | solution.py:34

commit v3 on v2

--- a/solution.py
+++ b/solution.py
@@ -36,7 +36,7 @@
 
 def exchange_steps(count):
     bits = count.bit_length() - 1
-    steps = [[0, 1], [0, 2]]
+    steps = []
     bit = 2
     while bit < bits:
         width = min(2, bits - bit)
@@ -89,12 +89,11 @@
     )(*pieces)
 
 
-def attend_kernel(*refs, segment, first):
-    *q_refs, k_ref, vt_ref, bias_ref, out_ref = refs
-    width = out_ref.shape[1] - STATS
-    start = first * GROUP * HD
-    queries_all = jnp.concatenate([ref[:, start : start + width] for ref in q_refs], 0)
-    rows = queries_all.shape[0]
+def attend_kernel(*refs, segment):
+    q_refs, (k_ref, vt_ref, bias_ref), out_refs = refs[:2], refs[2:5], refs[5:]
+    queries_all = jnp.concatenate([ref[...] for ref in q_refs], 0)
+    rows, width = queries_all.shape
+    chunk = rows // len(out_refs)
     kv_heads = width // (GROUP * HD)
     segments = k_ref.shape[0] // segment
     lanes = GROUP * rows
@@ -113,7 +112,7 @@
             )
         at = slice(s * segment, (s + 1) * segment)
         scores = lax.dot_general(
-            k_ref[at, (first + g) * HD : (first + g + 1) * HD],
+            k_ref[at, g * HD : (g + 1) * HD],
             queries[g],
             (((1,), (1,)), ((), ())),
             preferred_element_type=jnp.float32,
@@ -133,7 +132,7 @@
         totals.append(jnp.sum(weights, 0, keepdims=True))
         outs.append(
             jnp.dot(
-                vt_ref[(first + g) * HD : (first + g + 1) * HD, s * segment : (s + 1) * segment],
+                vt_ref[g * HD : (g + 1) * HD, s * segment : (s + 1) * segment],
                 weights.astype(jnp.bfloat16),
                 preferred_element_type=jnp.float32,
             )
@@ -150,13 +149,16 @@
         out = out * jnp.where(live, 1.0 / safe, 0.0)
         largest = jnp.max(jnp.abs(out), 0, keepdims=True)
         power = jnp.clip(jnp.ceil(jnp.log2(jnp.maximum(largest, 1e-37))), -100.0, 8.0)
-        out = jnp.round((out * (jnp.exp2(-power) * STEPS)).T).astype(jnp.int32).astype(jnp.int16)
+        out = jnp.round((out * (jnp.exp2(-power) * STEPS)).T).astype(jnp.int32)
         fixed = jnp.round(level * FIX).astype(jnp.int32)
         values = [fixed >> 16, (fixed & 0xFFFF) - 32768, power]
         for kind in range(KINDS):
-            stats[kind][first + g] = values[kind].astype(jnp.float32)
+            stats[kind][g] = values[kind].astype(jnp.float32)
         for h in range(GROUP):
-            out_ref[:, (g * GROUP + h) * HD : (g * GROUP + h + 1) * HD] = out[h * rows : (h + 1) * rows]
+            at = slice((g * GROUP + h) * HD, (g * GROUP + h + 1) * HD)
+            for c, out_ref in enumerate(out_refs):
+                top_row = h * rows + c * chunk
+                out_ref[:, at] = out[top_row : top_row + chunk].astype(jnp.int16)
     gap = jnp.zeros((SLOT - KV_SLOT, lanes), jnp.float32)
     high, low, power = [jnp.concatenate(kind, 0) for kind in stats]
     empty = jnp.zeros((KV_SLOT, lanes), jnp.float32)
@@ -169,22 +171,19 @@
                 for h in range(GROUP)
             )
         )
-    packed = jnp.concatenate(packed, 1).astype(jnp.int32).astype(jnp.int16)
-    out_ref[:, kv_heads * GROUP * HD :] = packed
-
-
-def combine_kernel(*refs, layout, heads, final):
+    packed = jnp.concatenate(packed, 1).astype(jnp.int32)
+    for c, out_ref in enumerate(out_refs):
+        out_ref[:, width:] = packed[c * chunk : (c + 1) * chunk].astype(jnp.int16)
+
+
+def combine_kernel(*refs, parts, heads, final):
+    sources, out_refs = refs[:parts], refs[parts:]
     wide = heads * HD
-    sources = []
-    for number in layout:
-        sources.append(refs[:number])
-        refs = refs[number:]
-    out_refs = refs
-    rows = sources[0][0].shape[0]
+    rows = sources[0].shape[0]
     chunk = rows // len(out_refs)
     fixed, powers = [], []
     for source in sources:
-        stats = sum(ref[:, wide // len(source) :].astype(jnp.int32) for ref in source)
+        stats = source[:, wide:].astype(jnp.int32)
         level = stats[:, :HD]
         fixed.append((level << 16) + pltpu.roll(level, SLOT, 1) + 32768)
         powers.append(stats[:, HD:].astype(jnp.float32))
@@ -201,11 +200,8 @@
         factors = [a * back for a in amounts]
     for h in range(heads):
         at = slice(h * HD, (h + 1) * HD)
-        values = []
-        for source in sources:
-            share = heads // len(source)
-            ref, local = source[h // share], h % share
-            values.append(ref[:, local * HD : (local + 1) * HD].astype(jnp.int32))
+        at = slice(h * HD, (h + 1) * HD)
+        values = [source[:, at].astype(jnp.int32) for source in sources]
         lane = h % GROUP * KV_SLOT + h // GROUP
         out = sum(f[:, lane : lane + 1] * v.astype(jnp.float32) for f, v in zip(factors, values))
         if final:
@@ -226,15 +222,12 @@
             out_ref[:, wide:] = packed[c * chunk : (c + 1) * chunk]
 
 
-def combine(sources, pieces, heads, final):
-    rows = sources[0][0].shape[0]
+def combine(arrays, pieces, heads, final=False):
+    rows = arrays[0].shape[0]
     width = heads * HD + (0 if final else STATS)
     dtype = jnp.bfloat16 if final else jnp.int16
-    arrays = [array for source in sources for array in source]
     return pl.pallas_call(
-        functools.partial(
-            combine_kernel, layout=[len(source) for source in sources], heads=heads, final=final
-        ),
+        functools.partial(combine_kernel, parts=len(arrays), heads=heads, final=final),
         out_shape=[jax.ShapeDtypeStruct((rows // pieces, width), dtype)] * pieces,
         in_specs=[VMEM] * len(arrays),
         out_specs=[VMEM] * pieces,
@@ -268,7 +261,8 @@
     places = []
     for deltas in steps:
         places += [(deltas[1] << b).bit_length() - 1 for b in range(len(deltas).bit_length() - 1)]
-    parts = len(steps[-1])
+    places += [0, 1]
+    parts = 2
     chunk = count * q_dev // parts
 
     prepared = pl.pallas_call(
@@ -282,52 +276,39 @@
     )(values, block_live.T, span_offset)
 
     block = queries
-    for stage, deltas in enumerate(steps[:-2]):
-        others = [swap(block, d) for d in deltas[2:] + deltas[1:2]]
+    for stage, deltas in enumerate(steps):
+        others = [swap(block, d) for d in deltas[:0:-1]]
         if stage == 0:
             others, block = lax.optimization_barrier((others, fetch(block)))
-        block = join([block] + others[-1:] + others[:-1])
-    pieces = [block]
-    for deltas in steps[-2:]:
-        moved = [swap(p, d) for d in deltas[1:] for p in pieces]
-        if deltas is steps[-2]:
-            moved, prepared = lax.optimization_barrier((moved, prepared))
-        pieces = pieces + moved
-    v_turned, *biases = prepared
-
-    def attend(pieces, bias, part, cuts):
-        width = q_width // cuts
+        block = join([block] + others[::-1])
+    v_turned, near_bias, far_bias = prepared
+
+    def attend(pair, bias):
         return pl.pallas_call(
-            functools.partial(
-                attend_kernel, segment=kv_dev // 2, first=part * (heads // GROUP // cuts)
-            ),
-            out_shape=jax.ShapeDtypeStruct((chunk, width + STATS), jnp.int16),
-            in_specs=[VMEM] * (len(pieces) + 3),
-            out_specs=VMEM,
+            functools.partial(attend_kernel, segment=kv_dev // 2),
+            out_shape=[jax.ShapeDtypeStruct((chunk // 2, q_width + STATS), jnp.int16)] * 2,
+            in_specs=[VMEM] * 5,
+            out_specs=[VMEM] * 2,
             compiler_params=PARAMS,
             cost_estimate=pl.CostEstimate(
-                flops=4 * chunk * width * kv_dev,
-                bytes_accessed=4 * 2**20 // cuts,
-                transcendentals=chunk * width // HD * kv_dev,
+                flops=4 * chunk * q_width * kv_dev,
+                bytes_accessed=4 * 2**20,
+                transcendentals=chunk * heads * kv_dev,
             ),
-        )(*pieces, keys, v_turned, bias)
-
-    share = len(pieces) // parts
-    early = attend(pieces[:share], biases[0], 0, 2)
-    *others, early = lax.optimization_barrier((*pieces[share:], early))
-    late = [
-        attend(others[c * share : (c + 1) * share], biases[c + 1], 0, 1) for c in range(parts - 1)
-    ]
-    outs = [early] + late
-    splits = [len(deltas) for deltas in steps[::-1]] + [1]
-    for stage, deltas in enumerate(steps[::-1]):
-        sources = [[swap(p, d)] for p, d in zip(outs[:0:-1], deltas[:0:-1])]
-        own = [outs[0]]
-        if stage == 0:
-            own.append(attend(pieces[:share], biases[0], 1, 2))
-            own[1], sources = lax.optimization_barrier((own[1], sources))
-        outs = combine([own] + sources, splits[stage + 1], heads, stage == len(steps) - 1)
-    return outs[0]
+        )(*pair, keys, v_turned, bias)
+
+    far_block = swap(block, 2)
+    near = attend([block, swap(block, 1)], near_bias)
+    far_block, near = lax.optimization_barrier((far_block, near))
+    far = attend([far_block, swap(far_block, 1)], far_bias)
+    (far_sum,) = combine([far[0], swap(far[1], 1)], 1, heads)
+    (near_sum,) = combine([near[0], swap(near[1], 1)], 1, heads)
+    arrays = [near_sum, swap(far_sum, 2)]
+    for deltas in steps[::-1]:
+        outs = combine(arrays, len(deltas), heads)
+        sent = [swap(p, d) for p, d in zip(outs[1:], deltas[1:])]
+        arrays = [outs[0]] + sent[:1] + sent[:0:-1]
+    return combine(arrays, 1, heads, final=True)[0]
 
 
 def solution(mesh):

time: 34.3 us -> 35.1 us (1.023)
  waiting for transfers between devices: 11.2 us -> 11.8 us
    ppermute x11 -> x12, waiting for transfers between devices: 11.2 us -> 11.8 us  [swap(): return lax.ppermute(array, 'kv', [(i, i ^ delta) for i in range(count)])]
    ppermute x11 -> x12, starting transfers between devices: 13.7 us -> 14 us  [swap(): return lax.ppermute(array, 'kv', [(i, i ^ delta) for i in range(count)])]
  transfers between devices with their start and end apart: 11 -> 12, of which waited for: 9 -> 8; matrix products, arithmetic and copies ran while one was open for 0% -> 0% of each run, Pallas kernels for 6% -> 7%
where the time goes in v3:
time: 35.1 us; the launch traced here: 34.8 us
  starting transfers between devices  14 us (40%)
  waiting for transfers between devices  11.8 us (34%)
  Pallas kernels  5.57 us (16%)
  local copies, waits for them, and re-layouts  2.7 us (8%)
  between operations  0.75 us (2%)
    ppermute x12, starting transfers between devices, swap(): return lax.ppermute(array, 'kv', [(i, i ^ delta) for i in range(count)])  14 us
    ppermute x12, waiting for transfers between devices, swap(): return lax.ppermute(array, 'kv', [(i, i ^ delta) for i in range(count)])  11.8 us
    pallas_call x2, Pallas kernels, attend(): pl.pallas_call(functools.partial(attend_kernel, segment=kv_dev // 2), out...  2.75 us
    unnamed x8, local copies, waits for them, and re-layouts  2.7 us
    pallas_call x4, Pallas kernels, combine(): pl.pallas_call(functools.partial(combine_kernel, parts=len(arrays), heads...  2.34 us
  transfers between devices with their start and end apart: 12, of which 8 were waited for; matrix products, arithmetic and copies ran while one was open for 0% of the time, Pallas kernels for 7%

profile of v3, /device:TPU:0, one launch (start us, length us, event | category | flops | bytes accessed | tf_op | source)
XLA Modules:
  0.0 34.8 jit_solution(8879724559688802577)
XLA Ops:
  0.0 0.0 copy-start
  0.0 5.0 %collective-permute-start = (bf16[2,8192]{1,0:T(2,128)(2,1)}, bf16[2,8192]{1,0:T(2,128)(2,1)S(1)}, u32[]{:S(2)}, u32[]{:S(2)}) collective-permute-start(bf16[2,8192]{1,0:T(2,128)(2,1)} %in_ref.1), channel_id=1, source_target_pairs={{0,12},{1,13},{2,14},{3,15},{4,8},{5,9},{6,10},{7,11},{8,4},{9,5},... | collective-permute-start | bytes 98312 | tf_op jit(solution)/shard_map/ppermute | solution.py:34
  5.1 0.0 collective-permute-start.1
  5.1 0.6 %collective-permute-start.2 = (bf16[2,8192]{1,0:T(2,128)(2,1)}, bf16[2,8192]{1,0:T(2,128)(2,1)S(1)}, u32[]{:S(2)}, u32[]{:S(2)}) collective-permute-start(bf16[2,8192]{1,0:T(2,128)(2,1)} %in_ref.1), channel_id=1, source_target_pairs={{0,4},{1,5},{2,6},{3,7},{4,0},{5,1},{6,2},{7,3},{8,12},{9,13},{10,... | collective-permute-start | bytes 98312 | tf_op jit(solution)/shard_map/ppermute | solution.py:34
  5.7 0.0 copy-start.2
  5.7 0.8 %copy-done.2 = bf16[2,8192]{1,0:T(2,128)(2,1)S(1)} copy-done((bf16[2,8192]{1,0:T(2,128)(2,1)S(1)}, bf16[2,8192]{1,0:T(2,128)(2,1)}, u32[]{:S(2)}) %copy-start.2) | copy-done | bytes 32792
  6.5 0.7 %collective-permute-done.refs_3_ = bf16[2,8192]{1,0:T(2,128)(2,1)S(1)} collective-permute-done((bf16[2,8192]{1,0:T(2,128)(2,1)}, bf16[2,8192]{1,0:T(2,128)(2,1)S(1)}, u32[]{:S(2)}, u32[]{:S(2)}) %collective-permute-start) | collective-permute-done | bytes 32800 | tf_op jit(solution)/shard_map/ppermute | solution.py:34
  7.2 2.9 %collective-permute-done.1.refs_2_ = bf16[2,8192]{1,0:T(2,128)(2,1)S(1)} collective-permute-done((bf16[2,8192]{1,0:T(2,128)(2,1)}, bf16[2,8192]{1,0:T(2,128)(2,1)S(1)}, u32[]{:S(2)}, u32[]{:S(2)}) %collective-permute-start.1) | collective-permute-done | bytes 32800 | tf_op jit(solution)/shard_map/ppermute | solution.py:34
  10.1 0.0 collective-permute-done.2.refs_1_
  10.1 0.1 shard_map.56.refs_0_
  10.2 0.1 collective-permute-start.4
  10.2 1.6 %collective-permute-start.3 = (bf16[8,8192]{1,0:T(8,128)(2,1)S(1)}, bf16[8,8192]{1,0:T(8,128)(2,1)S(1)}, u32[]{:S(2)}, u32[]{:S(2)}) collective-permute-start(bf16[8,8192]{1,0:T(8,128)(2,1)S(1)} %shard_map.56.refs_0_), channel_id=1, source_target_pairs={{0,2},{1,3},{2,0},{3,1},{4,6},{5,7},{6,4},{7,5},{8,10},{9,11},{10,... | collective-permute-start | bytes 393224 | tf_op jit(solution)/shard_map/ppermute | solution.py:34
  12.5 0.0 copy-start.1
  12.5 1.2 %copy-done.1 = bf16[512,1024]{1,0:T(8,128)(2,1)S(1)} copy-done((bf16[512,1024]{1,0:T(8,128)(2,1)S(1)}, bf16[512,1024]{1,0:T(8,128)(2,1)}, u32[]{:S(2)}) %copy-start.1) | copy-done | bytes 1048600
  13.7 0.0 copy-start.3
  13.7 0.7 %copy-done.3 = s32[16,8]{0,1:T(8,128)S(1)} copy-done((s32[16,8]{0,1:T(8,128)S(1)}, s32[16,8]{0,1:T(8,128)}, u32[]{:S(2)}) %copy-start.3) | copy-done | bytes 536
  14.4 0.4 %shard_map.57 = (bf16[1024,512]{1,0:T(8,128)(2,1)S(1)}, f32[512,128]{1,0:T(8,128)S(1)}, f32[512,128]{1,0:T(8,128)S(1)}) custom-call(bf16[512,1024]{1,0:T(8,128)(2,1)S(1)} %copy-done.1, s32[8,16]{1,0:T(8,128)S(1)} %bitcast.1, s32[1]{0:T(128)S(6)} %copy.6.offset_ref), custom_call_target="tpu_custom_call" | custom-call | bytes 4194304 | tf_op jit(solution)/shard_map/pallas_call | solution.py:268
  14.8 0.0 collective-permute-done.4.refs_1_
  14.8 0.0 copy-done
  14.8 1.4 %shard_map.58 = (s16[8,8448]{1,0:T(8,128)(2,1)S(1)}, s16[8,8448]{1,0:T(8,128)(2,1)S(1)}) custom-call(bf16[8,8192]{1,0:T(8,128)(2,1)S(1)} %shard_map.56.refs_0_, bf16[8,8192]{1,0:T(8,128)(2,1)S(1)} %collective-permute-done.4.refs_1_, bf16[512,1024]{1,0:T(8,128)(2,1)S(1)} %copy-done, bf16[1024,512]{1,0:T(8,128)(2,1)S(1)} %get-tuple-element.27.refs_3_, ...), custom_call_target="tpu_custom_call" | custom-call | flops 268435456 | bytes 4194304 | tf_op jit(solution)/shard_map/pallas_call | solution.py:287
  16.2 0.0 collective-permute-done.3.refs_0_
  16.2 0.2 collective-permute-start.6
  16.5 1.2 %collective-permute-done.6.refs_1_ = bf16[8,8192]{1,0:T(8,128)(2,1)S(1)} collective-permute-done((bf16[8,8192]{1,0:T(8,128)(2,1)S(1)}, bf16[8,8192]{1,0:T(8,128)(2,1)S(1)}, u32[]{:S(2)}, u32[]{:S(2)}) %collective-permute-start.6) | collective-permute-done | bytes 131104 | tf_op jit(solution)/shard_map/ppermute | solution.py:34
  17.6 1.3 %shard_map.60 = (s16[8,8448]{1,0:T(8,128)(2,1)S(1)}, s16[8,8448]{1,0:T(8,128)(2,1)S(1)}) custom-call(bf16[8,8192]{1,0:T(8,128)(2,1)S(1)} %collective-permute-done.3.refs_0_, bf16[8,8192]{1,0:T(8,128)(2,1)S(1)} %collective-permute-done.6.refs_1_, bf16[512,1024]{1,0:T(8,128)(2,1)S(1)} %copy-done, bf16[1024,512]{1,0:T(8,128)(2,1)S(1)} %get-tuple-element.27.refs_3_, ...), custom_call_target="tpu_custom_call" | custom-call | flops 268435456 | bytes 4194304 | tf_op jit(solution)/shard_map/pallas_call | solution.py:287
  19.0 0.2 collective-permute-start.7
  19.2 0.3 collective-permute-start.5
  19.6 0.8 %collective-permute-done.7.refs_1_ = s16[8,8448]{1,0:T(8,128)(2,1)S(1)} collective-permute-done((s16[8,8448]{1,0:T(8,128)(2,1)S(1)}, s16[8,8448]{1,0:T(8,128)(2,1)S(1)}, u32[]{:S(2)}, u32[]{:S(2)}) %collective-permute-start.7) | collective-permute-done | bytes 135200 | tf_op jit(solution)/shard_map/ppermute | solution.py:34
  20.4 0.4 %shard_map.61 = s16[8,8448]{1,0:T(8,128)(2,1)S(1)} custom-call(s16[8,8448]{1,0:T(8,128)(2,1)S(1)} %get-tuple-element.35.refs_0_, s16[8,8448]{1,0:T(8,128)(2,1)S(1)} %collective-permute-done.7.refs_1_), custom_call_target="tpu_custom_call" | custom-call | tf_op jit(solution)/shard_map/pallas_call | solution.py:229
  20.8 1.5 %collective-permute-start.8 = (s16[8,8448]{1,0:T(8,128)(2,1)S(1)}, s16[8,8448]{1,0:T(8,128)(2,1)S(1)}, u32[]{:S(2)}, u32[]{:S(2)}) collective-permute-start(s16[8,8448]{1,0:T(8,128)(2,1)S(1)} %shard_map.61), channel_id=1, source_target_pairs={{0,2},{1,3},{2,0},{3,1},{4,6},{5,7},{6,4},{7,5},{8,10},{9,11},{10,... | collective-permute-start | bytes 405512 | tf_op jit(solution)/shard_map/ppermute | solution.py:34
  22.3 0.0 collective-permute-done.5.refs_1_
  22.3 0.4 %shard_map.59.refs_0_ = s16[8,8448]{1,0:T(8,128)(2,1)S(1)} custom-call(s16[8,8448]{1,0:T(8,128)(2,1)S(1)} %get-tuple-element.31.refs_0_, s16[8,8448]{1,0:T(8,128)(2,1)S(1)} %collective-permute-done.5.refs_1_), custom_call_target="tpu_custom_call" | custom-call | tf_op jit(solution)/shard_map/pallas_call | solution.py:229
  22.7 3.9 %collective-permute-done.8.refs_1_ = s16[8,8448]{1,0:T(8,128)(2,1)S(1)} collective-permute-done((s16[8,8448]{1,0:T(8,128)(2,1)S(1)}, s16[8,8448]{1,0:T(8,128)(2,1)S(1)}, u32[]{:S(2)}, u32[]{:S(2)}) %collective-permute-start.8) | collective-permute-done | bytes 135200 | tf_op jit(solution)/shard_map/ppermute | solution.py:34
  26.5 0.4 %shard_map.62 = (s16[2,8448]{1,0:T(2,128)(2,1)S(1)}, s16[2,8448]{1,0:T(2,128)(2,1)S(1)}, s16[2,8448]{1,0:T(2,128)(2,1)S(1)}, s16[2,8448]{1,0:T(2,128)(2,1)S(1)}) custom-call(s16[8,8448]{1,0:T(8,128)(2,1)S(1)} %shard_map.59.refs_0_, s16[8,8448]{1,0:T(8,128)(2,1)S(1)} %collective-permute-done.8.refs_1_), custom_call_target="tpu_custom_call" | custom-call | tf_op jit(solution)/shard_map/pallas_call | solution.py:229
  26.9 1.6 %collective-permute-start.10 = (s16[2,8448]{1,0:T(2,128)(2,1)S(1)}, s16[2,8448]{1,0:T(2,128)(2,1)S(1)}, u32[]{:S(2)}, u32[]{:S(2)}) collective-permute-start(s16[2,8448]{1,0:T(2,128)(2,1)S(1)} %get-tuple-element.39), channel_id=1, source_target_pairs={{0,12},{1,13},{2,14},{3,15},{4,8},{5,9},{6,10},{7,11},{8,4},{9,5},... | collective-permute-start | bytes 101384 | tf_op jit(solution)/shard_map/ppermute | solution.py:34
  28.5 0.6 %collective-permute-start.11 = (s16[2,8448]{1,0:T(2,128)(2,1)S(1)}, s16[2,8448]{1,0:T(2,128)(2,1)S(1)}, u32[]{:S(2)}, u32[]{:S(2)}) collective-permute-start(s16[2,8448]{1,0:T(2,128)(2,1)S(1)} %get-tuple-element.40), channel_id=1, source_target_pairs={{0,8},{1,9},{2,10},{3,11},{4,12},{5,13},{6,14},{7,15},{8,0},{9,1},... | collective-permute-start | bytes 101384 | tf_op jit(solution)/shard_map/ppermute | solution.py:34
  29.1 2.3 %collective-permute-start.9 = (s16[2,8448]{1,0:T(2,128)(2,1)S(1)}, s16[2,8448]{1,0:T(2,128)(2,1)S(1)}, u32[]{:S(2)}, u32[]{:S(2)}) collective-permute-start(s16[2,8448]{1,0:T(2,128)(2,1)S(1)} %get-tuple-element.38), channel_id=1, source_target_pairs={{0,4},{1,5},{2,6},{3,7},{4,0},{5,1},{6,2},{7,3},{8,12},{9,13},{10,... | collective-permute-start | bytes 101384 | tf_op jit(solution)/shard_map/ppermute | solution.py:34
  31.4 1.6 %collective-permute-done.10.refs_2_ = s16[2,8448]{1,0:T(2,128)(2,1)S(1)} collective-permute-done((s16[2,8448]{1,0:T(2,128)(2,1)S(1)}, s16[2,8448]{1,0:T(2,128)(2,1)S(1)}, u32[]{:S(2)}, u32[]{:S(2)}) %collective-permute-start.10) | collective-permute-done | bytes 33824 | tf_op jit(solution)/shard_map/ppermute | solution.py:34
  32.9 0.4 %collective-permute-done.11.refs_3_ = s16[2,8448]{1,0:T(2,128)(2,1)S(1)} collective-permute-done((s16[2,8448]{1,0:T(2,128)(2,1)S(1)}, s16[2,8448]{1,0:T(2,128)(2,1)S(1)}, u32[]{:S(2)}, u32[]{:S(2)}) %collective-permute-start.11) | collective-permute-done | bytes 33824 | tf_op jit(solution)/shard_map/ppermute | solution.py:34
  33.4 0.3 collective-permute-done.9.refs_1_
  33.7 1.2 %shard_map.63 = bf16[2,8192]{1,0:T(2,128)(2,1)} custom-call(s16[2,8448]{1,0:T(2,128)(2,1)S(1)} %get-tuple-element.37.refs_0_, s16[2,8448]{1,0:T(2,128)(2,1)S(1)} %collective-permute-done.9.refs_1_, s16[2,8448]{1,0:T(2,128)(2,1)S(1)} %collective-permute-done.10.refs_2_, s16[2,8448]{1,0:T(2,128)(2,1)S(1)} %collective-permute-done.11.refs_3_), custom_call_target="tpu_custom_call" | custom-call | tf_op jit(solution)/shard_map/pallas_call | solution.py:229
  (1 shorter events, 0.0 us)
Async XLA Ops:
  0.0 14.8 %copy-start = (bf16[512,1024]{1,0:T(8,128)(2,1)S(1)}, bf16[512,1024]{1,0:T(8,128)(2,1)}, u32[]{:S(2)}) copy-start(bf16[512,1024]{1,0:T(8,128)(2,1)} %refs_2_.3) | copy-start | bytes 3145732
  0.0 7.2 %collective-permute-start = (bf16[2,8192]{1,0:T(2,128)(2,1)}, bf16[2,8192]{1,0:T(2,128)(2,1)S(1)}, u32[]{:S(2)}, u32[]{:S(2)}) collective-permute-start(bf16[2,8192]{1,0:T(2,128)(2,1)} %in_ref.1), channel_id=1, source_target_pairs={{0,12},{1,13},{2,14},{3,15},{4,8},{5,9},{6,10},{7,11},{8,4},{9,5},... | collective-permute-start | bytes 98312 | tf_op jit(solution)/shard_map/ppermute | solution.py:34
  5.1 5.0 %collective-permute-start.1 = (bf16[2,8192]{1,0:T(2,128)(2,1)}, bf16[2,8192]{1,0:T(2,128)(2,1)S(1)}, u32[]{:S(2)}, u32[]{:S(2)}) collective-permute-start(bf16[2,8192]{1,0:T(2,128)(2,1)} %in_ref.1), channel_id=1, source_target_pairs={{0,8},{1,9},{2,10},{3,11},{4,12},{5,13},{6,14},{7,15},{8,0},{9,1},... | collective-permute-start | bytes 98312 | tf_op jit(solution)/shard_map/ppermute | solution.py:34
  5.1 5.0 %collective-permute-start.2 = (bf16[2,8192]{1,0:T(2,128)(2,1)}, bf16[2,8192]{1,0:T(2,128)(2,1)S(1)}, u32[]{:S(2)}, u32[]{:S(2)}) collective-permute-start(bf16[2,8192]{1,0:T(2,128)(2,1)} %in_ref.1), channel_id=1, source_target_pairs={{0,4},{1,5},{2,6},{3,7},{4,0},{5,1},{6,2},{7,3},{8,12},{9,13},{10,... | collective-permute-start | bytes 98312 | tf_op jit(solution)/shard_map/ppermute | solution.py:34
  5.7 0.8 %copy-start.2 = (bf16[2,8192]{1,0:T(2,128)(2,1)S(1)}, bf16[2,8192]{1,0:T(2,128)(2,1)}, u32[]{:S(2)}) copy-start(bf16[2,8192]{1,0:T(2,128)(2,1)} %in_ref.1) | copy-start | bytes 98308
  10.2 4.6 %collective-permute-start.4 = (bf16[8,8192]{1,0:T(8,128)(2,1)S(1)}, bf16[8,8192]{1,0:T(8,128)(2,1)S(1)}, u32[]{:S(2)}, u32[]{:S(2)}) collective-permute-start(bf16[8,8192]{1,0:T(8,128)(2,1)S(1)} %shard_map.56.refs_0_), channel_id=1, source_target_pairs={{0,1},{1,0},{2,3},{3,2},{4,5},{5,4},{6,7},{7,6},{8,9},{9,8},{10,11... | collective-permute-start | bytes 393224 | tf_op jit(solution)/shard_map/ppermute | solution.py:34
  10.2 6.0 %collective-permute-start.3 = (bf16[8,8192]{1,0:T(8,128)(2,1)S(1)}, bf16[8,8192]{1,0:T(8,128)(2,1)S(1)}, u32[]{:S(2)}, u32[]{:S(2)}) collective-permute-start(bf16[8,8192]{1,0:T(8,128)(2,1)S(1)} %shard_map.56.refs_0_), channel_id=1, source_target_pairs={{0,2},{1,3},{2,0},{3,1},{4,6},{5,7},{6,4},{7,5},{8,10},{9,11},{10,... | collective-permute-start | bytes 393224 | tf_op jit(solution)/shard_map/ppermute | solution.py:34
  12.5 1.2 %copy-start.1 = (bf16[512,1024]{1,0:T(8,128)(2,1)S(1)}, bf16[512,1024]{1,0:T(8,128)(2,1)}, u32[]{:S(2)}) copy-start(bf16[512,1024]{1,0:T(8,128)(2,1)} %v_ref.1) | copy-start | bytes 3145732
  13.7 0.7 %copy-start.3 = (s32[16,8]{0,1:T(8,128)S(1)}, s32[16,8]{0,1:T(8,128)}, u32[]{:S(2)}) copy-start(s32[16,8]{0,1:T(8,128)} %param.8) | copy-start | bytes 1540
  16.2 1.4 %collective-permute-start.6 = (bf16[8,8192]{1,0:T(8,128)(2,1)S(1)}, bf16[8,8192]{1,0:T(8,128)(2,1)S(1)}, u32[]{:S(2)}, u32[]{:S(2)}) collective-permute-start(bf16[8,8192]{1,0:T(8,128)(2,1)S(1)} %collective-permute-done.3.refs_0_), channel_id=1, source_target_pairs={{0,1},{1,0},{2,3},{3,2},{4,5},{5,4},{6,7},{7,6},{8,9},{9,8},{10,11... | collective-permute-start | bytes 393224 | tf_op jit(solution)/shard_map/ppermute | solution.py:34
  19.0 1.4 %collective-permute-start.7 = (s16[8,8448]{1,0:T(8,128)(2,1)S(1)}, s16[8,8448]{1,0:T(8,128)(2,1)S(1)}, u32[]{:S(2)}, u32[]{:S(2)}) collective-permute-start(s16[8,8448]{1,0:T(8,128)(2,1)S(1)} %get-tuple-element.36), channel_id=1, source_target_pairs={{0,1},{1,0},{2,3},{3,2},{4,5},{5,4},{6,7},{7,6},{8,9},{9,8},{10,11... | collective-permute-start | bytes 405512 | tf_op jit(solution)/shard_map/ppermute | solution.py:34
  19.2 3.0 %collective-permute-start.5 = (s16[8,8448]{1,0:T(8,128)(2,1)S(1)}, s16[8,8448]{1,0:T(8,128)(2,1)S(1)}, u32[]{:S(2)}, u32[]{:S(2)}) collective-permute-start(s16[8,8448]{1,0:T(8,128)(2,1)S(1)} %get-tuple-element.32), channel_id=1, source_target_pairs={{0,1},{1,0},{2,3},{3,2},{4,5},{5,4},{6,7},{7,6},{8,9},{9,8},{10,11... | collective-permute-start | bytes 405512 | tf_op jit(solution)/shard_map/ppermute | solution.py:34
  20.8 5.7 %collective-permute-start.8 = (s16[8,8448]{1,0:T(8,128)(2,1)S(1)}, s16[8,8448]{1,0:T(8,128)(2,1)S(1)}, u32[]{:S(2)}, u32[]{:S(2)}) collective-permute-start(s16[8,8448]{1,0:T(8,128)(2,1)S(1)} %shard_map.61), channel_id=1, source_target_pairs={{0,2},{1,3},{2,0},{3,1},{4,6},{5,7},{6,4},{7,5},{8,10},{9,11},{10,... | collective-permute-start | bytes 405512 | tf_op jit(solution)/shard_map/ppermute | solution.py:34
  26.9 6.0 %collective-permute-start.10 = (s16[2,8448]{1,0:T(2,128)(2,1)S(1)}, s16[2,8448]{1,0:T(2,128)(2,1)S(1)}, u32[]{:S(2)}, u32[]{:S(2)}) collective-permute-start(s16[2,8448]{1,0:T(2,128)(2,1)S(1)} %get-tuple-element.39), channel_id=1, source_target_pairs={{0,12},{1,13},{2,14},{3,15},{4,8},{5,9},{6,10},{7,11},{8,4},{9,5},... | collective-permute-start | bytes 101384 | tf_op jit(solution)/shard_map/ppermute | solution.py:34
  28.5 4.9 %collective-permute-start.11 = (s16[2,8448]{1,0:T(2,128)(2,1)S(1)}, s16[2,8448]{1,0:T(2,128)(2,1)S(1)}, u32[]{:S(2)}, u32[]{:S(2)}) collective-permute-start(s16[2,8448]{1,0:T(2,128)(2,1)S(1)} %get-tuple-element.40), channel_id=1, source_target_pairs={{0,8},{1,9},{2,10},{3,11},{4,12},{5,13},{6,14},{7,15},{8,0},{9,1},... | collective-permute-start | bytes 101384 | tf_op jit(solution)/shard_map/ppermute | solution.py:34
  29.1 4.6 %collective-permute-start.9 = (s16[2,8448]{1,0:T(2,128)(2,1)S(1)}, s16[2,8448]{1,0:T(2,128)(2,1)S(1)}, u32[]{:S(2)}, u32[]{:S(2)}) collective-permute-start(s16[2,8448]{1,0:T(2,128)(2,1)S(1)} %get-tuple-element.38), channel_id=1, source_target_pairs={{0,4},{1,5},{2,6},{3,7},{4,0},{5,1},{6,2},{7,3},{8,12},{9,13},{10,... | collective-permute-start | bytes 101384 | tf_op jit(solution)/shard_map/ppermute | solution.py:34

commit v4 on v2

--- a/solution.py
+++ b/solution.py
@@ -36,7 +36,7 @@
 
 def exchange_steps(count):
     bits = count.bit_length() - 1
-    steps = [[0, 1], [0, 2]]
+    steps = []
     bit = 2
     while bit < bits:
         width = min(2, bits - bit)
@@ -90,11 +90,12 @@
 
 
 def attend_kernel(*refs, segment, first):
-    *q_refs, k_ref, vt_ref, bias_ref, out_ref = refs
-    width = out_ref.shape[1] - STATS
+    q_refs, (k_ref, vt_ref, bias_ref), out_refs = refs[:-5], refs[-5:-2], refs[-2:]
+    width = out_refs[0].shape[1] - STATS
     start = first * GROUP * HD
     queries_all = jnp.concatenate([ref[:, start : start + width] for ref in q_refs], 0)
     rows = queries_all.shape[0]
+    chunk = rows // len(out_refs)
     kv_heads = width // (GROUP * HD)
     segments = k_ref.shape[0] // segment
     lanes = GROUP * rows
@@ -150,13 +151,16 @@
         out = out * jnp.where(live, 1.0 / safe, 0.0)
         largest = jnp.max(jnp.abs(out), 0, keepdims=True)
         power = jnp.clip(jnp.ceil(jnp.log2(jnp.maximum(largest, 1e-37))), -100.0, 8.0)
-        out = jnp.round((out * (jnp.exp2(-power) * STEPS)).T).astype(jnp.int32).astype(jnp.int16)
+        out = jnp.round((out * (jnp.exp2(-power) * STEPS)).T).astype(jnp.int32)
         fixed = jnp.round(level * FIX).astype(jnp.int32)
         values = [fixed >> 16, (fixed & 0xFFFF) - 32768, power]
         for kind in range(KINDS):
             stats[kind][first + g] = values[kind].astype(jnp.float32)
         for h in range(GROUP):
-            out_ref[:, (g * GROUP + h) * HD : (g * GROUP + h + 1) * HD] = out[h * rows : (h + 1) * rows]
+            at = slice((g * GROUP + h) * HD, (g * GROUP + h + 1) * HD)
+            for c, out_ref in enumerate(out_refs):
+                top_row = h * rows + c * chunk
+                out_ref[:, at] = out[top_row : top_row + chunk].astype(jnp.int16)
     gap = jnp.zeros((SLOT - KV_SLOT, lanes), jnp.float32)
     high, low, power = [jnp.concatenate(kind, 0) for kind in stats]
     empty = jnp.zeros((KV_SLOT, lanes), jnp.float32)
@@ -169,8 +173,9 @@
                 for h in range(GROUP)
             )
         )
-    packed = jnp.concatenate(packed, 1).astype(jnp.int32).astype(jnp.int16)
-    out_ref[:, kv_heads * GROUP * HD :] = packed
+    packed = jnp.concatenate(packed, 1).astype(jnp.int32)
+    for c, out_ref in enumerate(out_refs):
+        out_ref[:, width:] = packed[c * chunk : (c + 1) * chunk].astype(jnp.int16)
 
 
 def combine_kernel(*refs, layout, heads, final):
@@ -226,7 +231,7 @@
             out_ref[:, wide:] = packed[c * chunk : (c + 1) * chunk]
 
 
-def combine(sources, pieces, heads, final):
+def combine(sources, pieces, heads, final=False):
     rows = sources[0][0].shape[0]
     width = heads * HD + (0 if final else STATS)
     dtype = jnp.bfloat16 if final else jnp.int16
@@ -268,7 +273,8 @@
     places = []
     for deltas in steps:
         places += [(deltas[1] << b).bit_length() - 1 for b in range(len(deltas).bit_length() - 1)]
-    parts = len(steps[-1])
+    places += [1, 0]
+    parts = 2
     chunk = count * q_dev // parts
 
     prepared = pl.pallas_call(
@@ -282,52 +288,45 @@
     )(values, block_live.T, span_offset)
 
     block = queries
-    for stage, deltas in enumerate(steps[:-2]):
+    for stage, deltas in enumerate(steps):
         others = [swap(block, d) for d in deltas[2:] + deltas[1:2]]
         if stage == 0:
             others, block = lax.optimization_barrier((others, fetch(block)))
         block = join([block] + others[-1:] + others[:-1])
-    pieces = [block]
-    for deltas in steps[-2:]:
-        moved = [swap(p, d) for d in deltas[1:] for p in pieces]
-        if deltas is steps[-2]:
-            moved, prepared = lax.optimization_barrier((moved, prepared))
-        pieces = pieces + moved
-    v_turned, *biases = prepared
-
-    def attend(pieces, bias, part, cuts):
+    far_block, prepared = lax.optimization_barrier((swap(block, 2), prepared))
+    v_turned, own_bias, other_bias = prepared
+
+    def attend(pair, bias, part, cuts):
         width = q_width // cuts
         return pl.pallas_call(
             functools.partial(
                 attend_kernel, segment=kv_dev // 2, first=part * (heads // GROUP // cuts)
             ),
-            out_shape=jax.ShapeDtypeStruct((chunk, width + STATS), jnp.int16),
-            in_specs=[VMEM] * (len(pieces) + 3),
-            out_specs=VMEM,
+            out_shape=[jax.ShapeDtypeStruct((chunk // 2, width + STATS), jnp.int16)] * 2,
+            in_specs=[VMEM] * 5,
+            out_specs=[VMEM] * 2,
             compiler_params=PARAMS,
             cost_estimate=pl.CostEstimate(
                 flops=4 * chunk * width * kv_dev,
                 bytes_accessed=4 * 2**20 // cuts,
                 transcendentals=chunk * width // HD * kv_dev,
             ),
-        )(*pieces, keys, v_turned, bias)
-
-    share = len(pieces) // parts
-    early = attend(pieces[:share], biases[0], 0, 2)
-    *others, early = lax.optimization_barrier((*pieces[share:], early))
-    late = [
-        attend(others[c * share : (c + 1) * share], biases[c + 1], 0, 1) for c in range(parts - 1)
-    ]
-    outs = [early] + late
-    splits = [len(deltas) for deltas in steps[::-1]] + [1]
-    for stage, deltas in enumerate(steps[::-1]):
-        sources = [[swap(p, d)] for p, d in zip(outs[:0:-1], deltas[:0:-1])]
-        own = [outs[0]]
-        if stage == 0:
-            own.append(attend(pieces[:share], biases[0], 1, 2))
-            own[1], sources = lax.optimization_barrier((own[1], sources))
-        outs = combine([own] + sources, splits[stage + 1], heads, stage == len(steps) - 1)
-    return outs[0]
+        )(*pair, keys, v_turned, bias)
+
+    pair, other_pair = [block, far_block], [swap(block, 1), swap(far_block, 1)]
+    early = attend(pair, own_bias, 0, 2)
+    other_pair, early = lax.optimization_barrier((other_pair, early))
+    near, far = attend(other_pair, other_bias, 0, 1)
+    late = attend(pair, own_bias, 1, 2)
+    late, far = lax.optimization_barrier((late, swap(far, 1)))
+    (far_sum,) = combine([[early[1], late[1]], [far]], 1, heads)
+    (near_sum,) = combine([[early[0], late[0]], [swap(near, 1)]], 1, heads)
+    arrays = [near_sum, swap(far_sum, 2)]
+    for deltas in steps[::-1]:
+        outs = combine([[a] for a in arrays], len(deltas), heads)
+        sent = [swap(p, d) for p, d in zip(outs[1:], deltas[1:])]
+        arrays = [outs[0]] + sent[::-1]
+    return combine([[a] for a in arrays], 1, heads, final=True)[0]
 
 
 def solution(mesh):

time: 34.3 us -> 34.1 us (level)
  waiting for transfers between devices: 11.2 us -> 10.3 us
  starting transfers between devices: 13.7 us -> 14.1 us
    ppermute x11 -> x12, waiting for transfers between devices: 11.2 us -> 10.3 us  [swap(): return lax.ppermute(array, 'kv', [(i, i ^ delta) for i in range(count)])]
    ppermute x11 -> x12, starting transfers between devices: 13.7 us -> 14.1 us  [swap(): return lax.ppermute(array, 'kv', [(i, i ^ delta) for i in range(count)])]
    pallas_call x3 -> x4, Pallas kernels: 2.1 us -> 2.34 us  [combine(): pl.pallas_call(functools.partial(combine_kernel, layout=[len(source) for...]
  transfers between devices with their start and end apart: 11 -> 12, of which waited for: 9 -> 8; matrix products, arithmetic and copies ran while one was open for 0% -> 0% of each run, Pallas kernels for 6% -> 9%
where the time goes in v4:
time: 34.1 us; the launch traced here: 33.8 us
  starting transfers between devices  14.1 us (41%)
  waiting for transfers between devices  10.3 us (30%)
  Pallas kernels  5.95 us (17%)
  local copies, waits for them, and re-layouts  2.7 us (8%)
  between operations  0.74 us (2%)
    ppermute x12, starting transfers between devices, swap(): return lax.ppermute(array, 'kv', [(i, i ^ delta) for i in range(count)])  14.1 us
    ppermute x12, waiting for transfers between devices, swap(): return lax.ppermute(array, 'kv', [(i, i ^ delta) for i in range(count)])  10.3 us
    pallas_call x3, Pallas kernels, attend(): pl.pallas_call(functools.partial(attend_kernel, segment=kv_dev // 2, firs...  3.12 us
    unnamed x8, local copies, waits for them, and re-layouts  2.7 us
    pallas_call x4, Pallas kernels, combine(): pl.pallas_call(functools.partial(combine_kernel, layout=[len(source) for...  2.34 us
  transfers between devices with their start and end apart: 12, of which 8 were waited for; matrix products, arithmetic and copies ran while one was open for 0% of the time, Pallas kernels for 9%

profile of v4, /device:TPU:0, one launch (start us, length us, event | category | flops | bytes accessed | tf_op | source)
XLA Modules:
  0.0 33.8 jit_solution(17986248398318994440)
XLA Ops:
  0.0 0.0 copy-start
  0.0 5.0 %collective-permute-start.1 = (bf16[2,8192]{1,0:T(2,128)(2,1)}, bf16[2,8192]{1,0:T(2,128)(2,1)S(1)}, u32[]{:S(2)}, u32[]{:S(2)}) collective-permute-start(bf16[2,8192]{1,0:T(2,128)(2,1)} %in_ref.1), channel_id=1, source_target_pairs={{0,12},{1,13},{2,14},{3,15},{4,8},{5,9},{6,10},{7,11},{8,4},{9,5},... | collective-permute-start | bytes 98312 | tf_op jit(solution)/shard_map/ppermute | solution.py:34
  5.1 0.0 collective-permute-start
  5.1 0.6 %collective-permute-start.2 = (bf16[2,8192]{1,0:T(2,128)(2,1)}, bf16[2,8192]{1,0:T(2,128)(2,1)S(1)}, u32[]{:S(2)}, u32[]{:S(2)}) collective-permute-start(bf16[2,8192]{1,0:T(2,128)(2,1)} %in_ref.1), channel_id=1, source_target_pairs={{0,4},{1,5},{2,6},{3,7},{4,0},{5,1},{6,2},{7,3},{8,12},{9,13},{10,... | collective-permute-start | bytes 98312 | tf_op jit(solution)/shard_map/ppermute | solution.py:34
  5.7 0.0 copy-start.2
  5.7 0.8 %copy-done.2 = bf16[2,8192]{1,0:T(2,128)(2,1)S(1)} copy-done((bf16[2,8192]{1,0:T(2,128)(2,1)S(1)}, bf16[2,8192]{1,0:T(2,128)(2,1)}, u32[]{:S(2)}) %copy-start.2) | copy-done | bytes 32792
  6.5 0.7 %collective-permute-done.1.refs_3_ = bf16[2,8192]{1,0:T(2,128)(2,1)S(1)} collective-permute-done((bf16[2,8192]{1,0:T(2,128)(2,1)}, bf16[2,8192]{1,0:T(2,128)(2,1)S(1)}, u32[]{:S(2)}, u32[]{:S(2)}) %collective-permute-start.1) | collective-permute-done | bytes 32800 | tf_op jit(solution)/shard_map/ppermute | solution.py:34
  7.2 2.9 %collective-permute-done.refs_2_ = bf16[2,8192]{1,0:T(2,128)(2,1)S(1)} collective-permute-done((bf16[2,8192]{1,0:T(2,128)(2,1)}, bf16[2,8192]{1,0:T(2,128)(2,1)S(1)}, u32[]{:S(2)}, u32[]{:S(2)}) %collective-permute-start) | collective-permute-done | bytes 32800 | tf_op jit(solution)/shard_map/ppermute | solution.py:34
  10.1 0.0 collective-permute-done.2.refs_1_
  10.1 0.1 shard_map.56.refs_0_
  10.2 1.6 %collective-permute-start.4 = (bf16[8,8192]{1,0:T(8,128)(2,1)S(1)}, bf16[8,8192]{1,0:T(8,128)(2,1)S(1)}, u32[]{:S(2)}, u32[]{:S(2)}) collective-permute-start(bf16[8,8192]{1,0:T(8,128)(2,1)S(1)} %shard_map.56.refs_0_), channel_id=1, source_target_pairs={{0,2},{1,3},{2,0},{3,1},{4,6},{5,7},{6,4},{7,5},{8,10},{9,11},{10,... | collective-permute-start | bytes 393224 | tf_op jit(solution)/shard_map/ppermute | solution.py:34
  12.4 0.0 copy-start.1
  12.4 1.2 %copy-done.1 = bf16[512,1024]{1,0:T(8,128)(2,1)S(1)} copy-done((bf16[512,1024]{1,0:T(8,128)(2,1)S(1)}, bf16[512,1024]{1,0:T(8,128)(2,1)}, u32[]{:S(2)}) %copy-start.1) | copy-done | bytes 1048600
  13.6 0.0 copy-start.3
  13.6 0.7 %copy-done.3 = s32[16,8]{0,1:T(8,128)S(1)} copy-done((s32[16,8]{0,1:T(8,128)S(1)}, s32[16,8]{0,1:T(8,128)}, u32[]{:S(2)}) %copy-start.3) | copy-done | bytes 536
  14.3 0.4 %shard_map.57 = (bf16[1024,512]{1,0:T(8,128)(2,1)S(1)}, f32[512,128]{1,0:T(8,128)S(1)}, f32[512,128]{1,0:T(8,128)S(1)}) custom-call(bf16[512,1024]{1,0:T(8,128)(2,1)S(1)} %copy-done.1, s32[8,16]{1,0:T(8,128)S(1)} %bitcast.1, s32[1]{0:T(128)S(6)} %copy.6.offset_ref), custom_call_target="tpu_custom_call" | custom-call | bytes 4194304 | tf_op jit(solution)/shard_map/pallas_call | solution.py:280
  14.7 0.1 collective-permute-start.3
  14.8 0.4 %collective-permute-done.4.refs_1_ = bf16[8,8192]{1,0:T(8,128)(2,1)S(1)} collective-permute-done((bf16[8,8192]{1,0:T(8,128)(2,1)S(1)}, bf16[8,8192]{1,0:T(8,128)(2,1)S(1)}, u32[]{:S(2)}, u32[]{:S(2)}) %collective-permute-start.4) | collective-permute-done | bytes 131104 | tf_op jit(solution)/shard_map/ppermute | solution.py:34
  15.2 0.1 collective-permute-start.5
  15.3 0.0 copy-done
  15.3 0.9 %shard_map.58 = (s16[8,4352]{1,0:T(8,128)(2,1)S(1)}, s16[8,4352]{1,0:T(8,128)(2,1)S(1)}) custom-call(bf16[8,8192]{1,0:T(8,128)(2,1)S(1)} %shard_map.56.refs_0_, bf16[8,8192]{1,0:T(8,128)(2,1)S(1)} %collective-permute-done.4.refs_1_, bf16[512,1024]{1,0:T(8,128)(2,1)S(1)} %copy-done, bf16[1024,512]{1,0:T(8,128)(2,1)S(1)} %get-tuple-element.41.refs_3_, ...), custom_call_target="tpu_custom_call" | custom-call | flops 134217728 | bytes 2097152 | tf_op jit(solution)/shard_map/pallas_call | solution.py:301
  16.2 0.0 collective-permute-done.3.refs_0_
  16.2 0.3 %collective-permute-done.5.refs_1_ = bf16[8,8192]{1,0:T(8,128)(2,1)S(1)} collective-permute-done((bf16[8,8192]{1,0:T(8,128)(2,1)S(1)}, bf16[8,8192]{1,0:T(8,128)(2,1)S(1)}, u32[]{:S(2)}, u32[]{:S(2)}) %collective-permute-start.5) | collective-permute-done | bytes 131104 | tf_op jit(solution)/shard_map/ppermute | solution.py:34
  16.6 1.3 %shard_map.60 = (s16[8,8448]{1,0:T(8,128)(2,1)S(1)}, s16[8,8448]{1,0:T(8,128)(2,1)S(1)}) custom-call(bf16[8,8192]{1,0:T(8,128)(2,1)S(1)} %collective-permute-done.3.refs_0_, bf16[8,8192]{1,0:T(8,128)(2,1)S(1)} %collective-permute-done.5.refs_1_, bf16[512,1024]{1,0:T(8,128)(2,1)S(1)} %copy-done, bf16[1024,512]{1,0:T(8,128)(2,1)S(1)} %get-tuple-element.41.refs_3_, ...), custom_call_target="tpu_custom_call" | custom-call | flops 268435456 | bytes 4194304 | tf_op jit(solution)/shard_map/pallas_call | solution.py:301
  17.9 0.2 collective-permute-start.6
  18.1 0.9 %shard_map.59 = (s16[8,4352]{1,0:T(8,128)(2,1)S(1)}, s16[8,4352]{1,0:T(8,128)(2,1)S(1)}) custom-call(bf16[8,8192]{1,0:T(8,128)(2,1)S(1)} %shard_map.56.refs_0_, bf16[8,8192]{1,0:T(8,128)(2,1)S(1)} %collective-permute-done.4.refs_1_, bf16[512,1024]{1,0:T(8,128)(2,1)S(1)} %copy-done, bf16[1024,512]{1,0:T(8,128)(2,1)S(1)} %get-tuple-element.41.refs_3_, ...), custom_call_target="tpu_custom_call" | custom-call | flops 134217728 | bytes 2097152 | tf_op jit(solution)/shard_map/pallas_call | solution.py:301
  19.0 0.4 %collective-permute-start.7 = (s16[8,8448]{1,0:T(8,128)(2,1)S(1)}, s16[8,8448]{1,0:T(8,128)(2,1)S(1)}, u32[]{:S(2)}, u32[]{:S(2)}) collective-permute-start(s16[8,8448]{1,0:T(8,128)(2,1)S(1)} %get-tuple-element.53), channel_id=1, source_target_pairs={{0,1},{1,0},{2,3},{3,2},{4,5},{5,4},{6,7},{7,6},{8,9},{9,8},{10,11... | collective-permute-start | bytes 405512 | tf_op jit(solution)/shard_map/ppermute | solution.py:34
  19.4 0.0 collective-permute-done.6.refs_2_
  19.4 0.4 %shard_map.62 = s16[8,8448]{1,0:T(8,128)(2,1)S(1)} custom-call(s16[8,4352]{1,0:T(8,128)(2,1)S(1)} %get-tuple-element.54.refs_0_, s16[8,4352]{1,0:T(8,128)(2,1)S(1)} %get-tuple-element.55.refs_1_, s16[8,8448]{1,0:T(8,128)(2,1)S(1)} %collective-permute-done.6.refs_2_), custom_call_target="tpu_custom_call" | custom-call | tf_op jit(solution)/shard_map/pallas_call | solution.py:239
  19.8 1.6 %collective-permute-start.8 = (s16[8,8448]{1,0:T(8,128)(2,1)S(1)}, s16[8,8448]{1,0:T(8,128)(2,1)S(1)}, u32[]{:S(2)}, u32[]{:S(2)}) collective-permute-start(s16[8,8448]{1,0:T(8,128)(2,1)S(1)} %shard_map.62), channel_id=1, source_target_pairs={{0,2},{1,3},{2,0},{3,1},{4,6},{5,7},{6,4},{7,5},{8,10},{9,11},{10,... | collective-permute-start | bytes 405512 | tf_op jit(solution)/shard_map/ppermute | solution.py:34
  21.4 0.0 collective-permute-done.7.refs_2_
  21.4 0.4 %shard_map.61.refs_0_ = s16[8,8448]{1,0:T(8,128)(2,1)S(1)} custom-call(s16[8,4352]{1,0:T(8,128)(2,1)S(1)} %get-tuple-element.45.refs_0_, s16[8,4352]{1,0:T(8,128)(2,1)S(1)} %get-tuple-element.52.refs_1_, s16[8,8448]{1,0:T(8,128)(2,1)S(1)} %collective-permute-done.7.refs_2_), custom_call_target="tpu_custom_call" | custom-call | tf_op jit(solution)/shard_map/pallas_call | solution.py:239
  21.8 3.7 %collective-permute-done.8.refs_1_ = s16[8,8448]{1,0:T(8,128)(2,1)S(1)} collective-permute-done((s16[8,8448]{1,0:T(8,128)(2,1)S(1)}, s16[8,8448]{1,0:T(8,128)(2,1)S(1)}, u32[]{:S(2)}, u32[]{:S(2)}) %collective-permute-start.8) | collective-permute-done | bytes 135200 | tf_op jit(solution)/shard_map/ppermute | solution.py:34
  25.5 0.4 %shard_map.63 = (s16[2,8448]{1,0:T(2,128)(2,1)S(1)}, s16[2,8448]{1,0:T(2,128)(2,1)S(1)}, s16[2,8448]{1,0:T(2,128)(2,1)S(1)}, s16[2,8448]{1,0:T(2,128)(2,1)S(1)}) custom-call(s16[8,8448]{1,0:T(8,128)(2,1)S(1)} %shard_map.61.refs_0_, s16[8,8448]{1,0:T(8,128)(2,1)S(1)} %collective-permute-done.8.refs_1_), custom_call_target="tpu_custom_call" | custom-call | tf_op jit(solution)/shard_map/pallas_call | solution.py:239
  25.9 1.6 %collective-permute-start.9 = (s16[2,8448]{1,0:T(2,128)(2,1)S(1)}, s16[2,8448]{1,0:T(2,128)(2,1)S(1)}, u32[]{:S(2)}, u32[]{:S(2)}) collective-permute-start(s16[2,8448]{1,0:T(2,128)(2,1)S(1)} %get-tuple-element.58), channel_id=1, source_target_pairs={{0,12},{1,13},{2,14},{3,15},{4,8},{5,9},{6,10},{7,11},{8,4},{9,5},... | collective-permute-start | bytes 101384 | tf_op jit(solution)/shard_map/ppermute | solution.py:34
  27.5 0.6 %collective-permute-start.10 = (s16[2,8448]{1,0:T(2,128)(2,1)S(1)}, s16[2,8448]{1,0:T(2,128)(2,1)S(1)}, u32[]{:S(2)}, u32[]{:S(2)}) collective-permute-start(s16[2,8448]{1,0:T(2,128)(2,1)S(1)} %get-tuple-element.59), channel_id=1, source_target_pairs={{0,8},{1,9},{2,10},{3,11},{4,12},{5,13},{6,14},{7,15},{8,0},{9,1},... | collective-permute-start | bytes 101384 | tf_op jit(solution)/shard_map/ppermute | solution.py:34
  28.1 2.3 %collective-permute-start.11 = (s16[2,8448]{1,0:T(2,128)(2,1)S(1)}, s16[2,8448]{1,0:T(2,128)(2,1)S(1)}, u32[]{:S(2)}, u32[]{:S(2)}) collective-permute-start(s16[2,8448]{1,0:T(2,128)(2,1)S(1)} %get-tuple-element.60), channel_id=1, source_target_pairs={{0,4},{1,5},{2,6},{3,7},{4,0},{5,1},{6,2},{7,3},{8,12},{9,13},{10,... | collective-permute-start | bytes 101384 | tf_op jit(solution)/shard_map/ppermute | solution.py:34
  30.4 1.5 %collective-permute-done.9.refs_1_ = s16[2,8448]{1,0:T(2,128)(2,1)S(1)} collective-permute-done((s16[2,8448]{1,0:T(2,128)(2,1)S(1)}, s16[2,8448]{1,0:T(2,128)(2,1)S(1)}, u32[]{:S(2)}, u32[]{:S(2)}) %collective-permute-start.9) | collective-permute-done | bytes 33824 | tf_op jit(solution)/shard_map/ppermute | solution.py:34
  31.9 0.4 %collective-permute-done.10.refs_2_ = s16[2,8448]{1,0:T(2,128)(2,1)S(1)} collective-permute-done((s16[2,8448]{1,0:T(2,128)(2,1)S(1)}, s16[2,8448]{1,0:T(2,128)(2,1)S(1)}, u32[]{:S(2)}, u32[]{:S(2)}) %collective-permute-start.10) | collective-permute-done | bytes 33824 | tf_op jit(solution)/shard_map/ppermute | solution.py:34
  32.4 0.3 collective-permute-done.11.refs_3_
  32.7 1.2 %shard_map.64 = bf16[2,8192]{1,0:T(2,128)(2,1)} custom-call(s16[2,8448]{1,0:T(2,128)(2,1)S(1)} %get-tuple-element.57.refs_0_, s16[2,8448]{1,0:T(2,128)(2,1)S(1)} %collective-permute-done.9.refs_1_, s16[2,8448]{1,0:T(2,128)(2,1)S(1)} %collective-permute-done.10.refs_2_, s16[2,8448]{1,0:T(2,128)(2,1)S(1)} %collective-permute-done.11.refs_3_), custom_call_target="tpu_custom_call" | custom-call | tf_op jit(solution)/shard_map/pallas_call | solution.py:239
  (1 shorter events, 0.0 us)
Async XLA Ops:
  0.0 15.3 %copy-start = (bf16[512,1024]{1,0:T(8,128)(2,1)S(1)}, bf16[512,1024]{1,0:T(8,128)(2,1)}, u32[]{:S(2)}) copy-start(bf16[512,1024]{1,0:T(8,128)(2,1)} %refs_2_.5) | copy-start | bytes 3145732
  0.0 7.2 %collective-permute-start.1 = (bf16[2,8192]{1,0:T(2,128)(2,1)}, bf16[2,8192]{1,0:T(2,128)(2,1)S(1)}, u32[]{:S(2)}, u32[]{:S(2)}) collective-permute-start(bf16[2,8192]{1,0:T(2,128)(2,1)} %in_ref.1), channel_id=1, source_target_pairs={{0,12},{1,13},{2,14},{3,15},{4,8},{5,9},{6,10},{7,11},{8,4},{9,5},... | collective-permute-start | bytes 98312 | tf_op jit(solution)/shard_map/ppermute | solution.py:34
  5.1 5.0 %collective-permute-start = (bf16[2,8192]{1,0:T(2,128)(2,1)}, bf16[2,8192]{1,0:T(2,128)(2,1)S(1)}, u32[]{:S(2)}, u32[]{:S(2)}) collective-permute-start(bf16[2,8192]{1,0:T(2,128)(2,1)} %in_ref.1), channel_id=1, source_target_pairs={{0,8},{1,9},{2,10},{3,11},{4,12},{5,13},{6,14},{7,15},{8,0},{9,1},... | collective-permute-start | bytes 98312 | tf_op jit(solution)/shard_map/ppermute | solution.py:34
  5.1 5.0 %collective-permute-start.2 = (bf16[2,8192]{1,0:T(2,128)(2,1)}, bf16[2,8192]{1,0:T(2,128)(2,1)S(1)}, u32[]{:S(2)}, u32[]{:S(2)}) collective-permute-start(bf16[2,8192]{1,0:T(2,128)(2,1)} %in_ref.1), channel_id=1, source_target_pairs={{0,4},{1,5},{2,6},{3,7},{4,0},{5,1},{6,2},{7,3},{8,12},{9,13},{10,... | collective-permute-start | bytes 98312 | tf_op jit(solution)/shard_map/ppermute | solution.py:34
  5.7 0.8 %copy-start.2 = (bf16[2,8192]{1,0:T(2,128)(2,1)S(1)}, bf16[2,8192]{1,0:T(2,128)(2,1)}, u32[]{:S(2)}) copy-start(bf16[2,8192]{1,0:T(2,128)(2,1)} %in_ref.1) | copy-start | bytes 98308
  10.2 5.0 %collective-permute-start.4 = (bf16[8,8192]{1,0:T(8,128)(2,1)S(1)}, bf16[8,8192]{1,0:T(8,128)(2,1)S(1)}, u32[]{:S(2)}, u32[]{:S(2)}) collective-permute-start(bf16[8,8192]{1,0:T(8,128)(2,1)S(1)} %shard_map.56.refs_0_), channel_id=1, source_target_pairs={{0,2},{1,3},{2,0},{3,1},{4,6},{5,7},{6,4},{7,5},{8,10},{9,11},{10,... | collective-permute-start | bytes 393224 | tf_op jit(solution)/shard_map/ppermute | solution.py:34
  12.4 1.2 %copy-start.1 = (bf16[512,1024]{1,0:T(8,128)(2,1)S(1)}, bf16[512,1024]{1,0:T(8,128)(2,1)}, u32[]{:S(2)}) copy-start(bf16[512,1024]{1,0:T(8,128)(2,1)} %v_ref.1) | copy-start | bytes 3145732
  13.6 0.7 %copy-start.3 = (s32[16,8]{0,1:T(8,128)S(1)}, s32[16,8]{0,1:T(8,128)}, u32[]{:S(2)}) copy-start(s32[16,8]{0,1:T(8,128)} %param.8) | copy-start | bytes 1540
  14.7 1.5 %collective-permute-start.3 = (bf16[8,8192]{1,0:T(8,128)(2,1)S(1)}, bf16[8,8192]{1,0:T(8,128)(2,1)S(1)}, u32[]{:S(2)}, u32[]{:S(2)}) collective-permute-start(bf16[8,8192]{1,0:T(8,128)(2,1)S(1)} %shard_map.56.refs_0_), channel_id=1, source_target_pairs={{0,1},{1,0},{2,3},{3,2},{4,5},{5,4},{6,7},{7,6},{8,9},{9,8},{10,11... | collective-permute-start | bytes 393224 | tf_op jit(solution)/shard_map/ppermute | solution.py:34
  15.2 1.3 %collective-permute-start.5 = (bf16[8,8192]{1,0:T(8,128)(2,1)S(1)}, bf16[8,8192]{1,0:T(8,128)(2,1)S(1)}, u32[]{:S(2)}, u32[]{:S(2)}) collective-permute-start(bf16[8,8192]{1,0:T(8,128)(2,1)S(1)} %collective-permute-done.4.refs_1_), channel_id=1, source_target_pairs={{0,1},{1,0},{2,3},{3,2},{4,5},{5,4},{6,7},{7,6},{8,9},{9,8},{10,11... | collective-permute-start | bytes 393224 | tf_op jit(solution)/shard_map/ppermute | solution.py:34
  17.9 1.5 %collective-permute-start.6 = (s16[8,8448]{1,0:T(8,128)(2,1)S(1)}, s16[8,8448]{1,0:T(8,128)(2,1)S(1)}, u32[]{:S(2)}, u32[]{:S(2)}) collective-permute-start(s16[8,8448]{1,0:T(8,128)(2,1)S(1)} %get-tuple-element.51), channel_id=1, source_target_pairs={{0,1},{1,0},{2,3},{3,2},{4,5},{5,4},{6,7},{7,6},{8,9},{9,8},{10,11... | collective-permute-start | bytes 405512 | tf_op jit(solution)/shard_map/ppermute | solution.py:34
  19.0 2.4 %collective-permute-start.7 = (s16[8,8448]{1,0:T(8,128)(2,1)S(1)}, s16[8,8448]{1,0:T(8,128)(2,1)S(1)}, u32[]{:S(2)}, u32[]{:S(2)}) collective-permute-start(s16[8,8448]{1,0:T(8,128)(2,1)S(1)} %get-tuple-element.53), channel_id=1, source_target_pairs={{0,1},{1,0},{2,3},{3,2},{4,5},{5,4},{6,7},{7,6},{8,9},{9,8},{10,11... | collective-permute-start | bytes 405512 | tf_op jit(solution)/shard_map/ppermute | solution.py:34
  19.8 5.7 %collective-permute-start.8 = (s16[8,8448]{1,0:T(8,128)(2,1)S(1)}, s16[8,8448]{1,0:T(8,128)(2,1)S(1)}, u32[]{:S(2)}, u32[]{:S(2)}) collective-permute-start(s16[8,8448]{1,0:T(8,128)(2,1)S(1)} %shard_map.62), channel_id=1, source_target_pairs={{0,2},{1,3},{2,0},{3,1},{4,6},{5,7},{6,4},{7,5},{8,10},{9,11},{10,... | collective-permute-start | bytes 405512 | tf_op jit(solution)/shard_map/ppermute | solution.py:34
  25.9 6.0 %collective-permute-start.9 = (s16[2,8448]{1,0:T(2,128)(2,1)S(1)}, s16[2,8448]{1,0:T(2,128)(2,1)S(1)}, u32[]{:S(2)}, u32[]{:S(2)}) collective-permute-start(s16[2,8448]{1,0:T(2,128)(2,1)S(1)} %get-tuple-element.58), channel_id=1, source_target_pairs={{0,12},{1,13},{2,14},{3,15},{4,8},{5,9},{6,10},{7,11},{8,4},{9,5},... | collective-permute-start | bytes 101384 | tf_op jit(solution)/shard_map/ppermute | solution.py:34
  27.5 4.9 %collective-permute-start.10 = (s16[2,8448]{1,0:T(2,128)(2,1)S(1)}, s16[2,8448]{1,0:T(2,128)(2,1)S(1)}, u32[]{:S(2)}, u32[]{:S(2)}) collective-permute-start(s16[2,8448]{1,0:T(2,128)(2,1)S(1)} %get-tuple-element.59), channel_id=1, source_target_pairs={{0,8},{1,9},{2,10},{3,11},{4,12},{5,13},{6,14},{7,15},{8,0},{9,1},... | collective-permute-start | bytes 101384 | tf_op jit(solution)/shard_map/ppermute | solution.py:34
  28.1 4.6 %collective-permute-start.11 = (s16[2,8448]{1,0:T(2,128)(2,1)S(1)}, s16[2,8448]{1,0:T(2,128)(2,1)S(1)}, u32[]{:S(2)}, u32[]{:S(2)}) collective-permute-start(s16[2,8448]{1,0:T(2,128)(2,1)S(1)} %get-tuple-element.60), channel_id=1, source_target_pairs={{0,4},{1,5},{2,6},{3,7},{4,0},{5,1},{6,2},{7,3},{8,12},{9,13},{10,... | collective-permute-start | bytes 101384 | tf_op jit(solution)/shard_map/ppermute | solution.py:34

commit v5 on v4

--- a/solution.py
+++ b/solution.py
@@ -21,6 +21,7 @@
 NO_WEIGHT = -8191.0
 MASKED = -1e30
 AHEAD = 1
+WRITES = 4
 KINDS = 3
 SLOT = HD // 2
 STATS = 2 * HD
@@ -185,6 +186,10 @@
         sources.append(refs[:number])
         refs = refs[number:]
     out_refs = refs
+    copies = []
+    if final:
+        target, stage, sems = refs
+        out_refs = [stage]
     rows = sources[0][0].shape[0]
     chunk = rows // len(out_refs)
     fixed, powers = [], []
@@ -219,6 +224,15 @@
             out = jnp.round(out).astype(jnp.int32).astype(jnp.int16)
         for c, out_ref in enumerate(out_refs):
             out_ref[:, at] = out[c * chunk : (c + 1) * chunk]
+        if final and (h + 1) % (heads // WRITES) == 0:
+            piece = wide // WRITES
+            done = pl.ds(len(copies) * piece, piece)
+            copies.append(
+                pltpu.make_async_copy(stage.at[:, done], target.at[:, done], sems.at[len(copies)])
+            )
+            copies[-1].start()
+    for copy in copies:
+        copy.wait()
     if not final:
         level = top + jnp.round(jnp.log2(total) * FIX).astype(jnp.int32)
         lane = lax.broadcasted_iota(jnp.int32, level.shape, 1)
@@ -242,7 +256,10 @@
         ),
         out_shape=[jax.ShapeDtypeStruct((rows // pieces, width), dtype)] * pieces,
         in_specs=[VMEM] * len(arrays),
-        out_specs=[VMEM] * pieces,
+        out_specs=[pl.BlockSpec(memory_space=pl.ANY) if final else VMEM] * pieces,
+        scratch_shapes=[pltpu.VMEM((rows, width), dtype), pltpu.SemaphoreType.DMA((WRITES,))]
+        if final
+        else [],
         compiler_params=PARAMS,
     )(*arrays)
 

time: 34.1 us -> 34.1 us (level)
  no operation moved by 1% of the time
where the time goes in v5:
time: 34.1 us; the launch traced here: 33.8 us
  starting transfers between devices  14.1 us (41%)
  waiting for transfers between devices  10.3 us (30%)
  Pallas kernels  5.96 us (17%)
  local copies, waits for them, and re-layouts  2.7 us (8%)
  between operations  0.74 us (2%)
    ppermute x12, starting transfers between devices, swap(): return lax.ppermute(array, 'kv', [(i, i ^ delta) for i in range(count)])  14.1 us
    ppermute x12, waiting for transfers between devices, swap(): return lax.ppermute(array, 'kv', [(i, i ^ delta) for i in range(count)])  10.3 us
    pallas_call x3, Pallas kernels, attend(): pl.pallas_call(functools.partial(attend_kernel, segment=kv_dev // 2, firs...  3.12 us
    unnamed x8, local copies, waits for them, and re-layouts  2.7 us
    pallas_call x4, Pallas kernels, combine(): pl.pallas_call(functools.partial(combine_kernel, layout=[len(source) for...  2.35 us
  transfers between devices with their start and end apart: 12, of which 8 were waited for; matrix products, arithmetic and copies ran while one was open for 0% of the time, Pallas kernels for 9%

profile of v5, /device:TPU:0, one launch (start us, length us, event | category | flops | bytes accessed | tf_op | source)
XLA Modules:
  0.0 33.8 jit_solution(4241313380712157351)
XLA Ops:
  0.0 0.0 copy-start
  0.0 5.0 %collective-permute-start.1 = (bf16[2,8192]{1,0:T(2,128)(2,1)}, bf16[2,8192]{1,0:T(2,128)(2,1)S(1)}, u32[]{:S(2)}, u32[]{:S(2)}) collective-permute-start(bf16[2,8192]{1,0:T(2,128)(2,1)} %in_ref.1), channel_id=1, source_target_pairs={{0,12},{1,13},{2,14},{3,15},{4,8},{5,9},{6,10},{7,11},{8,4},{9,5},... | collective-permute-start | bytes 98312 | tf_op jit(solution)/shard_map/ppermute | solution.py:35
  5.1 0.0 collective-permute-start
  5.1 0.6 %collective-permute-start.2 = (bf16[2,8192]{1,0:T(2,128)(2,1)}, bf16[2,8192]{1,0:T(2,128)(2,1)S(1)}, u32[]{:S(2)}, u32[]{:S(2)}) collective-permute-start(bf16[2,8192]{1,0:T(2,128)(2,1)} %in_ref.1), channel_id=1, source_target_pairs={{0,4},{1,5},{2,6},{3,7},{4,0},{5,1},{6,2},{7,3},{8,12},{9,13},{10,... | collective-permute-start | bytes 98312 | tf_op jit(solution)/shard_map/ppermute | solution.py:35
  5.7 0.0 copy-start.2
  5.7 0.8 %copy-done.2 = bf16[2,8192]{1,0:T(2,128)(2,1)S(1)} copy-done((bf16[2,8192]{1,0:T(2,128)(2,1)S(1)}, bf16[2,8192]{1,0:T(2,128)(2,1)}, u32[]{:S(2)}) %copy-start.2) | copy-done | bytes 32792
  6.5 0.7 %collective-permute-done.1.refs_3_ = bf16[2,8192]{1,0:T(2,128)(2,1)S(1)} collective-permute-done((bf16[2,8192]{1,0:T(2,128)(2,1)}, bf16[2,8192]{1,0:T(2,128)(2,1)S(1)}, u32[]{:S(2)}, u32[]{:S(2)}) %collective-permute-start.1) | collective-permute-done | bytes 32800 | tf_op jit(solution)/shard_map/ppermute | solution.py:35
  7.2 2.9 %collective-permute-done.refs_2_ = bf16[2,8192]{1,0:T(2,128)(2,1)S(1)} collective-permute-done((bf16[2,8192]{1,0:T(2,128)(2,1)}, bf16[2,8192]{1,0:T(2,128)(2,1)S(1)}, u32[]{:S(2)}, u32[]{:S(2)}) %collective-permute-start) | collective-permute-done | bytes 32800 | tf_op jit(solution)/shard_map/ppermute | solution.py:35
  10.1 0.0 collective-permute-done.2.refs_1_
  10.1 0.1 shard_map.56.refs_0_
  10.2 1.6 %collective-permute-start.4 = (bf16[8,8192]{1,0:T(8,128)(2,1)S(1)}, bf16[8,8192]{1,0:T(8,128)(2,1)S(1)}, u32[]{:S(2)}, u32[]{:S(2)}) collective-permute-start(bf16[8,8192]{1,0:T(8,128)(2,1)S(1)} %shard_map.56.refs_0_), channel_id=1, source_target_pairs={{0,2},{1,3},{2,0},{3,1},{4,6},{5,7},{6,4},{7,5},{8,10},{9,11},{10,... | collective-permute-start | bytes 393224 | tf_op jit(solution)/shard_map/ppermute | solution.py:35
  12.4 0.0 copy-start.1
  12.4 1.2 %copy-done.1 = bf16[512,1024]{1,0:T(8,128)(2,1)S(1)} copy-done((bf16[512,1024]{1,0:T(8,128)(2,1)S(1)}, bf16[512,1024]{1,0:T(8,128)(2,1)}, u32[]{:S(2)}) %copy-start.1) | copy-done | bytes 1048600
  13.6 0.0 copy-start.3
  13.6 0.7 %copy-done.3 = s32[16,8]{0,1:T(8,128)S(1)} copy-done((s32[16,8]{0,1:T(8,128)S(1)}, s32[16,8]{0,1:T(8,128)}, u32[]{:S(2)}) %copy-start.3) | copy-done | bytes 536
  14.3 0.4 %shard_map.57 = (bf16[1024,512]{1,0:T(8,128)(2,1)S(1)}, f32[512,128]{1,0:T(8,128)S(1)}, f32[512,128]{1,0:T(8,128)S(1)}) custom-call(bf16[512,1024]{1,0:T(8,128)(2,1)S(1)} %copy-done.1, s32[8,16]{1,0:T(8,128)S(1)} %bitcast.1, s32[1]{0:T(128)S(6)} %copy.6.offset_ref), custom_call_target="tpu_custom_call" | custom-call | bytes 4194304 | tf_op jit(solution)/shard_map/pallas_call | solution.py:297
  14.7 0.1 collective-permute-start.3
  14.8 0.4 %collective-permute-done.4.refs_1_ = bf16[8,8192]{1,0:T(8,128)(2,1)S(1)} collective-permute-done((bf16[8,8192]{1,0:T(8,128)(2,1)S(1)}, bf16[8,8192]{1,0:T(8,128)(2,1)S(1)}, u32[]{:S(2)}, u32[]{:S(2)}) %collective-permute-start.4) | collective-permute-done | bytes 131104 | tf_op jit(solution)/shard_map/ppermute | solution.py:35
  15.2 0.1 collective-permute-start.5
  15.3 0.0 copy-done
  15.3 0.9 %shard_map.58 = (s16[8,4352]{1,0:T(8,128)(2,1)S(1)}, s16[8,4352]{1,0:T(8,128)(2,1)S(1)}) custom-call(bf16[8,8192]{1,0:T(8,128)(2,1)S(1)} %shard_map.56.refs_0_, bf16[8,8192]{1,0:T(8,128)(2,1)S(1)} %collective-permute-done.4.refs_1_, bf16[512,1024]{1,0:T(8,128)(2,1)S(1)} %copy-done, bf16[1024,512]{1,0:T(8,128)(2,1)S(1)} %get-tuple-element.41.refs_3_, ...), custom_call_target="tpu_custom_call" | custom-call | flops 134217728 | bytes 2097152 | tf_op jit(solution)/shard_map/pallas_call | solution.py:318
  16.2 0.0 collective-permute-done.3.refs_0_
  16.2 0.3 %collective-permute-done.5.refs_1_ = bf16[8,8192]{1,0:T(8,128)(2,1)S(1)} collective-permute-done((bf16[8,8192]{1,0:T(8,128)(2,1)S(1)}, bf16[8,8192]{1,0:T(8,128)(2,1)S(1)}, u32[]{:S(2)}, u32[]{:S(2)}) %collective-permute-start.5) | collective-permute-done | bytes 131104 | tf_op jit(solution)/shard_map/ppermute | solution.py:35
  16.6 1.3 %shard_map.60 = (s16[8,8448]{1,0:T(8,128)(2,1)S(1)}, s16[8,8448]{1,0:T(8,128)(2,1)S(1)}) custom-call(bf16[8,8192]{1,0:T(8,128)(2,1)S(1)} %collective-permute-done.3.refs_0_, bf16[8,8192]{1,0:T(8,128)(2,1)S(1)} %collective-permute-done.5.refs_1_, bf16[512,1024]{1,0:T(8,128)(2,1)S(1)} %copy-done, bf16[1024,512]{1,0:T(8,128)(2,1)S(1)} %get-tuple-element.41.refs_3_, ...), custom_call_target="tpu_custom_call" | custom-call | flops 268435456 | bytes 4194304 | tf_op jit(solution)/shard_map/pallas_call | solution.py:318
  17.9 0.2 collective-permute-start.6
  18.1 0.9 %shard_map.59 = (s16[8,4352]{1,0:T(8,128)(2,1)S(1)}, s16[8,4352]{1,0:T(8,128)(2,1)S(1)}) custom-call(bf16[8,8192]{1,0:T(8,128)(2,1)S(1)} %shard_map.56.refs_0_, bf16[8,8192]{1,0:T(8,128)(2,1)S(1)} %collective-permute-done.4.refs_1_, bf16[512,1024]{1,0:T(8,128)(2,1)S(1)} %copy-done, bf16[1024,512]{1,0:T(8,128)(2,1)S(1)} %get-tuple-element.41.refs_3_, ...), custom_call_target="tpu_custom_call" | custom-call | flops 134217728 | bytes 2097152 | tf_op jit(solution)/shard_map/pallas_call | solution.py:318
  19.0 0.4 %collective-permute-start.7 = (s16[8,8448]{1,0:T(8,128)(2,1)S(1)}, s16[8,8448]{1,0:T(8,128)(2,1)S(1)}, u32[]{:S(2)}, u32[]{:S(2)}) collective-permute-start(s16[8,8448]{1,0:T(8,128)(2,1)S(1)} %get-tuple-element.53), channel_id=1, source_target_pairs={{0,1},{1,0},{2,3},{3,2},{4,5},{5,4},{6,7},{7,6},{8,9},{9,8},{10,11... | collective-permute-start | bytes 405512 | tf_op jit(solution)/shard_map/ppermute | solution.py:35
  19.4 0.0 collective-permute-done.6.refs_2_
  19.4 0.4 %shard_map.62 = s16[8,8448]{1,0:T(8,128)(2,1)S(1)} custom-call(s16[8,4352]{1,0:T(8,128)(2,1)S(1)} %get-tuple-element.54.refs_0_, s16[8,4352]{1,0:T(8,128)(2,1)S(1)} %get-tuple-element.55.refs_1_, s16[8,8448]{1,0:T(8,128)(2,1)S(1)} %collective-permute-done.6.refs_2_), custom_call_target="tpu_custom_call" | custom-call | tf_op jit(solution)/shard_map/pallas_call | solution.py:253
  19.8 1.6 %collective-permute-start.8 = (s16[8,8448]{1,0:T(8,128)(2,1)S(1)}, s16[8,8448]{1,0:T(8,128)(2,1)S(1)}, u32[]{:S(2)}, u32[]{:S(2)}) collective-permute-start(s16[8,8448]{1,0:T(8,128)(2,1)S(1)} %shard_map.62), channel_id=1, source_target_pairs={{0,2},{1,3},{2,0},{3,1},{4,6},{5,7},{6,4},{7,5},{8,10},{9,11},{10,... | collective-permute-start | bytes 405512 | tf_op jit(solution)/shard_map/ppermute | solution.py:35
  21.4 0.0 collective-permute-done.7.refs_2_
  21.4 0.4 %shard_map.61.refs_0_ = s16[8,8448]{1,0:T(8,128)(2,1)S(1)} custom-call(s16[8,4352]{1,0:T(8,128)(2,1)S(1)} %get-tuple-element.45.refs_0_, s16[8,4352]{1,0:T(8,128)(2,1)S(1)} %get-tuple-element.52.refs_1_, s16[8,8448]{1,0:T(8,128)(2,1)S(1)} %collective-permute-done.7.refs_2_), custom_call_target="tpu_custom_call" | custom-call | tf_op jit(solution)/shard_map/pallas_call | solution.py:253
  21.8 3.7 %collective-permute-done.8.refs_1_ = s16[8,8448]{1,0:T(8,128)(2,1)S(1)} collective-permute-done((s16[8,8448]{1,0:T(8,128)(2,1)S(1)}, s16[8,8448]{1,0:T(8,128)(2,1)S(1)}, u32[]{:S(2)}, u32[]{:S(2)}) %collective-permute-start.8) | collective-permute-done | bytes 135200 | tf_op jit(solution)/shard_map/ppermute | solution.py:35
  25.5 0.4 %shard_map.63 = (s16[2,8448]{1,0:T(2,128)(2,1)S(1)}, s16[2,8448]{1,0:T(2,128)(2,1)S(1)}, s16[2,8448]{1,0:T(2,128)(2,1)S(1)}, s16[2,8448]{1,0:T(2,128)(2,1)S(1)}) custom-call(s16[8,8448]{1,0:T(8,128)(2,1)S(1)} %shard_map.61.refs_0_, s16[8,8448]{1,0:T(8,128)(2,1)S(1)} %collective-permute-done.8.refs_1_), custom_call_target="tpu_custom_call" | custom-call | tf_op jit(solution)/shard_map/pallas_call | solution.py:253
  25.9 1.6 %collective-permute-start.9 = (s16[2,8448]{1,0:T(2,128)(2,1)S(1)}, s16[2,8448]{1,0:T(2,128)(2,1)S(1)}, u32[]{:S(2)}, u32[]{:S(2)}) collective-permute-start(s16[2,8448]{1,0:T(2,128)(2,1)S(1)} %get-tuple-element.58), channel_id=1, source_target_pairs={{0,12},{1,13},{2,14},{3,15},{4,8},{5,9},{6,10},{7,11},{8,4},{9,5},... | collective-permute-start | bytes 101384 | tf_op jit(solution)/shard_map/ppermute | solution.py:35
  27.5 0.6 %collective-permute-start.10 = (s16[2,8448]{1,0:T(2,128)(2,1)S(1)}, s16[2,8448]{1,0:T(2,128)(2,1)S(1)}, u32[]{:S(2)}, u32[]{:S(2)}) collective-permute-start(s16[2,8448]{1,0:T(2,128)(2,1)S(1)} %get-tuple-element.59), channel_id=1, source_target_pairs={{0,8},{1,9},{2,10},{3,11},{4,12},{5,13},{6,14},{7,15},{8,0},{9,1},... | collective-permute-start | bytes 101384 | tf_op jit(solution)/shard_map/ppermute | solution.py:35
  28.1 2.3 %collective-permute-start.11 = (s16[2,8448]{1,0:T(2,128)(2,1)S(1)}, s16[2,8448]{1,0:T(2,128)(2,1)S(1)}, u32[]{:S(2)}, u32[]{:S(2)}) collective-permute-start(s16[2,8448]{1,0:T(2,128)(2,1)S(1)} %get-tuple-element.60), channel_id=1, source_target_pairs={{0,4},{1,5},{2,6},{3,7},{4,0},{5,1},{6,2},{7,3},{8,12},{9,13},{10,... | collective-permute-start | bytes 101384 | tf_op jit(solution)/shard_map/ppermute | solution.py:35
  30.4 1.5 %collective-permute-done.9.refs_1_ = s16[2,8448]{1,0:T(2,128)(2,1)S(1)} collective-permute-done((s16[2,8448]{1,0:T(2,128)(2,1)S(1)}, s16[2,8448]{1,0:T(2,128)(2,1)S(1)}, u32[]{:S(2)}, u32[]{:S(2)}) %collective-permute-start.9) | collective-permute-done | bytes 33824 | tf_op jit(solution)/shard_map/ppermute | solution.py:35
  31.9 0.4 %collective-permute-done.10.refs_2_ = s16[2,8448]{1,0:T(2,128)(2,1)S(1)} collective-permute-done((s16[2,8448]{1,0:T(2,128)(2,1)S(1)}, s16[2,8448]{1,0:T(2,128)(2,1)S(1)}, u32[]{:S(2)}, u32[]{:S(2)}) %collective-permute-start.10) | collective-permute-done | bytes 33824 | tf_op jit(solution)/shard_map/ppermute | solution.py:35
  32.4 0.3 collective-permute-done.11.refs_3_
  32.7 1.2 %shard_map.64 = bf16[2,8192]{1,0:T(2,128)(2,1)} custom-call(s16[2,8448]{1,0:T(2,128)(2,1)S(1)} %get-tuple-element.57.refs_0_, s16[2,8448]{1,0:T(2,128)(2,1)S(1)} %collective-permute-done.9.refs_1_, s16[2,8448]{1,0:T(2,128)(2,1)S(1)} %collective-permute-done.10.refs_2_, s16[2,8448]{1,0:T(2,128)(2,1)S(1)} %collective-permute-done.11.refs_3_), custom_call_target="tpu_custom_call" | custom-call | tf_op jit(solution)/shard_map/pallas_call | solution.py:253
  (1 shorter events, 0.0 us)
Async XLA Ops:
  0.0 15.3 %copy-start = (bf16[512,1024]{1,0:T(8,128)(2,1)S(1)}, bf16[512,1024]{1,0:T(8,128)(2,1)}, u32[]{:S(2)}) copy-start(bf16[512,1024]{1,0:T(8,128)(2,1)} %refs_2_.5) | copy-start | bytes 3145732
  0.0 7.2 %collective-permute-start.1 = (bf16[2,8192]{1,0:T(2,128)(2,1)}, bf16[2,8192]{1,0:T(2,128)(2,1)S(1)}, u32[]{:S(2)}, u32[]{:S(2)}) collective-permute-start(bf16[2,8192]{1,0:T(2,128)(2,1)} %in_ref.1), channel_id=1, source_target_pairs={{0,12},{1,13},{2,14},{3,15},{4,8},{5,9},{6,10},{7,11},{8,4},{9,5},... | collective-permute-start | bytes 98312 | tf_op jit(solution)/shard_map/ppermute | solution.py:35
  5.1 5.0 %collective-permute-start = (bf16[2,8192]{1,0:T(2,128)(2,1)}, bf16[2,8192]{1,0:T(2,128)(2,1)S(1)}, u32[]{:S(2)}, u32[]{:S(2)}) collective-permute-start(bf16[2,8192]{1,0:T(2,128)(2,1)} %in_ref.1), channel_id=1, source_target_pairs={{0,8},{1,9},{2,10},{3,11},{4,12},{5,13},{6,14},{7,15},{8,0},{9,1},... | collective-permute-start | bytes 98312 | tf_op jit(solution)/shard_map/ppermute | solution.py:35
  5.1 5.0 %collective-permute-start.2 = (bf16[2,8192]{1,0:T(2,128)(2,1)}, bf16[2,8192]{1,0:T(2,128)(2,1)S(1)}, u32[]{:S(2)}, u32[]{:S(2)}) collective-permute-start(bf16[2,8192]{1,0:T(2,128)(2,1)} %in_ref.1), channel_id=1, source_target_pairs={{0,4},{1,5},{2,6},{3,7},{4,0},{5,1},{6,2},{7,3},{8,12},{9,13},{10,... | collective-permute-start | bytes 98312 | tf_op jit(solution)/shard_map/ppermute | solution.py:35
  5.7 0.8 %copy-start.2 = (bf16[2,8192]{1,0:T(2,128)(2,1)S(1)}, bf16[2,8192]{1,0:T(2,128)(2,1)}, u32[]{:S(2)}) copy-start(bf16[2,8192]{1,0:T(2,128)(2,1)} %in_ref.1) | copy-start | bytes 98308
  10.2 5.0 %collective-permute-start.4 = (bf16[8,8192]{1,0:T(8,128)(2,1)S(1)}, bf16[8,8192]{1,0:T(8,128)(2,1)S(1)}, u32[]{:S(2)}, u32[]{:S(2)}) collective-permute-start(bf16[8,8192]{1,0:T(8,128)(2,1)S(1)} %shard_map.56.refs_0_), channel_id=1, source_target_pairs={{0,2},{1,3},{2,0},{3,1},{4,6},{5,7},{6,4},{7,5},{8,10},{9,11},{10,... | collective-permute-start | bytes 393224 | tf_op jit(solution)/shard_map/ppermute | solution.py:35
  12.4 1.2 %copy-start.1 = (bf16[512,1024]{1,0:T(8,128)(2,1)S(1)}, bf16[512,1024]{1,0:T(8,128)(2,1)}, u32[]{:S(2)}) copy-start(bf16[512,1024]{1,0:T(8,128)(2,1)} %v_ref.1) | copy-start | bytes 3145732
  13.6 0.7 %copy-start.3 = (s32[16,8]{0,1:T(8,128)S(1)}, s32[16,8]{0,1:T(8,128)}, u32[]{:S(2)}) copy-start(s32[16,8]{0,1:T(8,128)} %param.8) | copy-start | bytes 1540
  14.7 1.5 %collective-permute-start.3 = (bf16[8,8192]{1,0:T(8,128)(2,1)S(1)}, bf16[8,8192]{1,0:T(8,128)(2,1)S(1)}, u32[]{:S(2)}, u32[]{:S(2)}) collective-permute-start(bf16[8,8192]{1,0:T(8,128)(2,1)S(1)} %shard_map.56.refs_0_), channel_id=1, source_target_pairs={{0,1},{1,0},{2,3},{3,2},{4,5},{5,4},{6,7},{7,6},{8,9},{9,8},{10,11... | collective-permute-start | bytes 393224 | tf_op jit(solution)/shard_map/ppermute | solution.py:35
  15.2 1.3 %collective-permute-start.5 = (bf16[8,8192]{1,0:T(8,128)(2,1)S(1)}, bf16[8,8192]{1,0:T(8,128)(2,1)S(1)}, u32[]{:S(2)}, u32[]{:S(2)}) collective-permute-start(bf16[8,8192]{1,0:T(8,128)(2,1)S(1)} %collective-permute-done.4.refs_1_), channel_id=1, source_target_pairs={{0,1},{1,0},{2,3},{3,2},{4,5},{5,4},{6,7},{7,6},{8,9},{9,8},{10,11... | collective-permute-start | bytes 393224 | tf_op jit(solution)/shard_map/ppermute | solution.py:35
  17.9 1.5 %collective-permute-start.6 = (s16[8,8448]{1,0:T(8,128)(2,1)S(1)}, s16[8,8448]{1,0:T(8,128)(2,1)S(1)}, u32[]{:S(2)}, u32[]{:S(2)}) collective-permute-start(s16[8,8448]{1,0:T(8,128)(2,1)S(1)} %get-tuple-element.51), channel_id=1, source_target_pairs={{0,1},{1,0},{2,3},{3,2},{4,5},{5,4},{6,7},{7,6},{8,9},{9,8},{10,11... | collective-permute-start | bytes 405512 | tf_op jit(solution)/shard_map/ppermute | solution.py:35
  19.0 2.4 %collective-permute-start.7 = (s16[8,8448]{1,0:T(8,128)(2,1)S(1)}, s16[8,8448]{1,0:T(8,128)(2,1)S(1)}, u32[]{:S(2)}, u32[]{:S(2)}) collective-permute-start(s16[8,8448]{1,0:T(8,128)(2,1)S(1)} %get-tuple-element.53), channel_id=1, source_target_pairs={{0,1},{1,0},{2,3},{3,2},{4,5},{5,4},{6,7},{7,6},{8,9},{9,8},{10,11... | collective-permute-start | bytes 405512 | tf_op jit(solution)/shard_map/ppermute | solution.py:35
  19.8 5.7 %collective-permute-start.8 = (s16[8,8448]{1,0:T(8,128)(2,1)S(1)}, s16[8,8448]{1,0:T(8,128)(2,1)S(1)}, u32[]{:S(2)}, u32[]{:S(2)}) collective-permute-start(s16[8,8448]{1,0:T(8,128)(2,1)S(1)} %shard_map.62), channel_id=1, source_target_pairs={{0,2},{1,3},{2,0},{3,1},{4,6},{5,7},{6,4},{7,5},{8,10},{9,11},{10,... | collective-permute-start | bytes 405512 | tf_op jit(solution)/shard_map/ppermute | solution.py:35
  25.9 6.0 %collective-permute-start.9 = (s16[2,8448]{1,0:T(2,128)(2,1)S(1)}, s16[2,8448]{1,0:T(2,128)(2,1)S(1)}, u32[]{:S(2)}, u32[]{:S(2)}) collective-permute-start(s16[2,8448]{1,0:T(2,128)(2,1)S(1)} %get-tuple-element.58), channel_id=1, source_target_pairs={{0,12},{1,13},{2,14},{3,15},{4,8},{5,9},{6,10},{7,11},{8,4},{9,5},... | collective-permute-start | bytes 101384 | tf_op jit(solution)/shard_map/ppermute | solution.py:35
  27.5 4.9 %collective-permute-start.10 = (s16[2,8448]{1,0:T(2,128)(2,1)S(1)}, s16[2,8448]{1,0:T(2,128)(2,1)S(1)}, u32[]{:S(2)}, u32[]{:S(2)}) collective-permute-start(s16[2,8448]{1,0:T(2,128)(2,1)S(1)} %get-tuple-element.59), channel_id=1, source_target_pairs={{0,8},{1,9},{2,10},{3,11},{4,12},{5,13},{6,14},{7,15},{8,0},{9,1},... | collective-permute-start | bytes 101384 | tf_op jit(solution)/shard_map/ppermute | solution.py:35
  28.1 4.6 %collective-permute-start.11 = (s16[2,8448]{1,0:T(2,128)(2,1)S(1)}, s16[2,8448]{1,0:T(2,128)(2,1)S(1)}, u32[]{:S(2)}, u32[]{:S(2)}) collective-permute-start(s16[2,8448]{1,0:T(2,128)(2,1)S(1)} %get-tuple-element.60), channel_id=1, source_target_pairs={{0,4},{1,5},{2,6},{3,7},{4,0},{5,1},{6,2},{7,3},{8,12},{9,13},{10,... | collective-permute-start | bytes 101384 | tf_op jit(solution)/shard_map/ppermute | solution.py:35

commit v6 on v5

--- a/solution.py
+++ b/solution.py
@@ -20,7 +20,7 @@
 STEPS = 32766.0
 NO_WEIGHT = -8191.0
 MASKED = -1e30
-AHEAD = 1
+AHEAD = 2
 WRITES = 4
 KINDS = 3
 SLOT = HD // 2

time: 34.1 us -> 34.1 us (level)
  no operation moved by 1% of the time
where the time goes in v6:
time: 34.1 us; the launch traced here: 33.8 us
  starting transfers between devices  14.1 us (41%)
  waiting for transfers between devices  10.3 us (30%)
  Pallas kernels  5.97 us (18%)
  local copies, waits for them, and re-layouts  2.7 us (8%)
  between operations  0.74 us (2%)
    ppermute x12, starting transfers between devices, swap(): return lax.ppermute(array, 'kv', [(i, i ^ delta) for i in range(count)])  14.1 us
    ppermute x12, waiting for transfers between devices, swap(): return lax.ppermute(array, 'kv', [(i, i ^ delta) for i in range(count)])  10.3 us
    pallas_call x3, Pallas kernels, attend(): pl.pallas_call(functools.partial(attend_kernel, segment=kv_dev // 2, firs...  3.12 us
    unnamed x8, local copies, waits for them, and re-layouts  2.7 us
    pallas_call x4, Pallas kernels, combine(): pl.pallas_call(functools.partial(combine_kernel, layout=[len(source) for...  2.35 us
  transfers between devices with their start and end apart: 12, of which 8 were waited for; matrix products, arithmetic and copies ran while one was open for 0% of the time, Pallas kernels for 9%

profile of v6, /device:TPU:0, one launch (start us, length us, event | category | flops | bytes accessed | tf_op | source)
XLA Modules:
  0.0 33.8 jit_solution(1171887749732089307)
XLA Ops:
  0.0 0.0 copy-start
  0.0 5.0 %collective-permute-start.1 = (bf16[2,8192]{1,0:T(2,128)(2,1)}, bf16[2,8192]{1,0:T(2,128)(2,1)S(1)}, u32[]{:S(2)}, u32[]{:S(2)}) collective-permute-start(bf16[2,8192]{1,0:T(2,128)(2,1)} %in_ref.1), channel_id=1, source_target_pairs={{0,12},{1,13},{2,14},{3,15},{4,8},{5,9},{6,10},{7,11},{8,4},{9,5},... | collective-permute-start | bytes 98312 | tf_op jit(solution)/shard_map/ppermute | solution.py:35
  5.1 0.0 collective-permute-start
  5.1 0.6 %collective-permute-start.2 = (bf16[2,8192]{1,0:T(2,128)(2,1)}, bf16[2,8192]{1,0:T(2,128)(2,1)S(1)}, u32[]{:S(2)}, u32[]{:S(2)}) collective-permute-start(bf16[2,8192]{1,0:T(2,128)(2,1)} %in_ref.1), channel_id=1, source_target_pairs={{0,4},{1,5},{2,6},{3,7},{4,0},{5,1},{6,2},{7,3},{8,12},{9,13},{10,... | collective-permute-start | bytes 98312 | tf_op jit(solution)/shard_map/ppermute | solution.py:35
  5.7 0.0 copy-start.2
  5.7 0.8 %copy-done.2 = bf16[2,8192]{1,0:T(2,128)(2,1)S(1)} copy-done((bf16[2,8192]{1,0:T(2,128)(2,1)S(1)}, bf16[2,8192]{1,0:T(2,128)(2,1)}, u32[]{:S(2)}) %copy-start.2) | copy-done | bytes 32792
  6.5 0.7 %collective-permute-done.1.refs_3_ = bf16[2,8192]{1,0:T(2,128)(2,1)S(1)} collective-permute-done((bf16[2,8192]{1,0:T(2,128)(2,1)}, bf16[2,8192]{1,0:T(2,128)(2,1)S(1)}, u32[]{:S(2)}, u32[]{:S(2)}) %collective-permute-start.1) | collective-permute-done | bytes 32800 | tf_op jit(solution)/shard_map/ppermute | solution.py:35
  7.2 2.9 %collective-permute-done.refs_2_ = bf16[2,8192]{1,0:T(2,128)(2,1)S(1)} collective-permute-done((bf16[2,8192]{1,0:T(2,128)(2,1)}, bf16[2,8192]{1,0:T(2,128)(2,1)S(1)}, u32[]{:S(2)}, u32[]{:S(2)}) %collective-permute-start) | collective-permute-done | bytes 32800 | tf_op jit(solution)/shard_map/ppermute | solution.py:35
  10.1 0.0 collective-permute-done.2.refs_1_
  10.1 0.1 shard_map.56.refs_0_
  10.2 1.6 %collective-permute-start.4 = (bf16[8,8192]{1,0:T(8,128)(2,1)S(1)}, bf16[8,8192]{1,0:T(8,128)(2,1)S(1)}, u32[]{:S(2)}, u32[]{:S(2)}) collective-permute-start(bf16[8,8192]{1,0:T(8,128)(2,1)S(1)} %shard_map.56.refs_0_), channel_id=1, source_target_pairs={{0,2},{1,3},{2,0},{3,1},{4,6},{5,7},{6,4},{7,5},{8,10},{9,11},{10,... | collective-permute-start | bytes 393224 | tf_op jit(solution)/shard_map/ppermute | solution.py:35
  12.4 0.0 copy-start.1
  12.4 1.2 %copy-done.1 = bf16[512,1024]{1,0:T(8,128)(2,1)S(1)} copy-done((bf16[512,1024]{1,0:T(8,128)(2,1)S(1)}, bf16[512,1024]{1,0:T(8,128)(2,1)}, u32[]{:S(2)}) %copy-start.1) | copy-done | bytes 1048600
  13.6 0.0 copy-start.3
  13.6 0.7 %copy-done.3 = s32[16,8]{0,1:T(8,128)S(1)} copy-done((s32[16,8]{0,1:T(8,128)S(1)}, s32[16,8]{0,1:T(8,128)}, u32[]{:S(2)}) %copy-start.3) | copy-done | bytes 536
  14.3 0.4 %shard_map.57 = (bf16[1024,512]{1,0:T(8,128)(2,1)S(1)}, f32[512,128]{1,0:T(8,128)S(1)}, f32[512,128]{1,0:T(8,128)S(1)}) custom-call(bf16[512,1024]{1,0:T(8,128)(2,1)S(1)} %copy-done.1, s32[8,16]{1,0:T(8,128)S(1)} %bitcast.1, s32[1]{0:T(128)S(6)} %copy.6.offset_ref), custom_call_target="tpu_custom_call" | custom-call | bytes 4194304 | tf_op jit(solution)/shard_map/pallas_call | solution.py:297
  14.7 0.1 collective-permute-start.3
  14.8 0.4 %collective-permute-done.4.refs_1_ = bf16[8,8192]{1,0:T(8,128)(2,1)S(1)} collective-permute-done((bf16[8,8192]{1,0:T(8,128)(2,1)S(1)}, bf16[8,8192]{1,0:T(8,128)(2,1)S(1)}, u32[]{:S(2)}, u32[]{:S(2)}) %collective-permute-start.4) | collective-permute-done | bytes 131104 | tf_op jit(solution)/shard_map/ppermute | solution.py:35
  15.2 0.1 collective-permute-start.5
  15.3 0.0 copy-done
  15.3 0.9 %shard_map.58 = (s16[8,4352]{1,0:T(8,128)(2,1)S(1)}, s16[8,4352]{1,0:T(8,128)(2,1)S(1)}) custom-call(bf16[8,8192]{1,0:T(8,128)(2,1)S(1)} %shard_map.56.refs_0_, bf16[8,8192]{1,0:T(8,128)(2,1)S(1)} %collective-permute-done.4.refs_1_, bf16[512,1024]{1,0:T(8,128)(2,1)S(1)} %copy-done, bf16[1024,512]{1,0:T(8,128)(2,1)S(1)} %get-tuple-element.41.refs_3_, ...), custom_call_target="tpu_custom_call" | custom-call | flops 134217728 | bytes 2097152 | tf_op jit(solution)/shard_map/pallas_call | solution.py:318
  16.2 0.0 collective-permute-done.3.refs_0_
  16.2 0.3 %collective-permute-done.5.refs_1_ = bf16[8,8192]{1,0:T(8,128)(2,1)S(1)} collective-permute-done((bf16[8,8192]{1,0:T(8,128)(2,1)S(1)}, bf16[8,8192]{1,0:T(8,128)(2,1)S(1)}, u32[]{:S(2)}, u32[]{:S(2)}) %collective-permute-start.5) | collective-permute-done | bytes 131104 | tf_op jit(solution)/shard_map/ppermute | solution.py:35
  16.6 1.3 %shard_map.60 = (s16[8,8448]{1,0:T(8,128)(2,1)S(1)}, s16[8,8448]{1,0:T(8,128)(2,1)S(1)}) custom-call(bf16[8,8192]{1,0:T(8,128)(2,1)S(1)} %collective-permute-done.3.refs_0_, bf16[8,8192]{1,0:T(8,128)(2,1)S(1)} %collective-permute-done.5.refs_1_, bf16[512,1024]{1,0:T(8,128)(2,1)S(1)} %copy-done, bf16[1024,512]{1,0:T(8,128)(2,1)S(1)} %get-tuple-element.41.refs_3_, ...), custom_call_target="tpu_custom_call" | custom-call | flops 268435456 | bytes 4194304 | tf_op jit(solution)/shard_map/pallas_call | solution.py:318
  17.9 0.2 collective-permute-start.6
  18.1 0.9 %shard_map.59 = (s16[8,4352]{1,0:T(8,128)(2,1)S(1)}, s16[8,4352]{1,0:T(8,128)(2,1)S(1)}) custom-call(bf16[8,8192]{1,0:T(8,128)(2,1)S(1)} %shard_map.56.refs_0_, bf16[8,8192]{1,0:T(8,128)(2,1)S(1)} %collective-permute-done.4.refs_1_, bf16[512,1024]{1,0:T(8,128)(2,1)S(1)} %copy-done, bf16[1024,512]{1,0:T(8,128)(2,1)S(1)} %get-tuple-element.41.refs_3_, ...), custom_call_target="tpu_custom_call" | custom-call | flops 134217728 | bytes 2097152 | tf_op jit(solution)/shard_map/pallas_call | solution.py:318
  19.0 0.4 %collective-permute-start.7 = (s16[8,8448]{1,0:T(8,128)(2,1)S(1)}, s16[8,8448]{1,0:T(8,128)(2,1)S(1)}, u32[]{:S(2)}, u32[]{:S(2)}) collective-permute-start(s16[8,8448]{1,0:T(8,128)(2,1)S(1)} %get-tuple-element.53), channel_id=1, source_target_pairs={{0,1},{1,0},{2,3},{3,2},{4,5},{5,4},{6,7},{7,6},{8,9},{9,8},{10,11... | collective-permute-start | bytes 405512 | tf_op jit(solution)/shard_map/ppermute | solution.py:35
  19.4 0.0 collective-permute-done.6.refs_2_
  19.4 0.4 %shard_map.62 = s16[8,8448]{1,0:T(8,128)(2,1)S(1)} custom-call(s16[8,4352]{1,0:T(8,128)(2,1)S(1)} %get-tuple-element.54.refs_0_, s16[8,4352]{1,0:T(8,128)(2,1)S(1)} %get-tuple-element.55.refs_1_, s16[8,8448]{1,0:T(8,128)(2,1)S(1)} %collective-permute-done.6.refs_2_), custom_call_target="tpu_custom_call" | custom-call | tf_op jit(solution)/shard_map/pallas_call | solution.py:253
  19.8 1.6 %collective-permute-start.8 = (s16[8,8448]{1,0:T(8,128)(2,1)S(1)}, s16[8,8448]{1,0:T(8,128)(2,1)S(1)}, u32[]{:S(2)}, u32[]{:S(2)}) collective-permute-start(s16[8,8448]{1,0:T(8,128)(2,1)S(1)} %shard_map.62), channel_id=1, source_target_pairs={{0,2},{1,3},{2,0},{3,1},{4,6},{5,7},{6,4},{7,5},{8,10},{9,11},{10,... | collective-permute-start | bytes 405512 | tf_op jit(solution)/shard_map/ppermute | solution.py:35
  21.4 0.0 collective-permute-done.7.refs_2_
  21.4 0.4 %shard_map.61.refs_0_ = s16[8,8448]{1,0:T(8,128)(2,1)S(1)} custom-call(s16[8,4352]{1,0:T(8,128)(2,1)S(1)} %get-tuple-element.45.refs_0_, s16[8,4352]{1,0:T(8,128)(2,1)S(1)} %get-tuple-element.52.refs_1_, s16[8,8448]{1,0:T(8,128)(2,1)S(1)} %collective-permute-done.7.refs_2_), custom_call_target="tpu_custom_call" | custom-call | tf_op jit(solution)/shard_map/pallas_call | solution.py:253
  21.8 3.7 %collective-permute-done.8.refs_1_ = s16[8,8448]{1,0:T(8,128)(2,1)S(1)} collective-permute-done((s16[8,8448]{1,0:T(8,128)(2,1)S(1)}, s16[8,8448]{1,0:T(8,128)(2,1)S(1)}, u32[]{:S(2)}, u32[]{:S(2)}) %collective-permute-start.8) | collective-permute-done | bytes 135200 | tf_op jit(solution)/shard_map/ppermute | solution.py:35
  25.5 0.4 %shard_map.63 = (s16[2,8448]{1,0:T(2,128)(2,1)S(1)}, s16[2,8448]{1,0:T(2,128)(2,1)S(1)}, s16[2,8448]{1,0:T(2,128)(2,1)S(1)}, s16[2,8448]{1,0:T(2,128)(2,1)S(1)}) custom-call(s16[8,8448]{1,0:T(8,128)(2,1)S(1)} %shard_map.61.refs_0_, s16[8,8448]{1,0:T(8,128)(2,1)S(1)} %collective-permute-done.8.refs_1_), custom_call_target="tpu_custom_call" | custom-call | tf_op jit(solution)/shard_map/pallas_call | solution.py:253
  25.9 1.6 %collective-permute-start.9 = (s16[2,8448]{1,0:T(2,128)(2,1)S(1)}, s16[2,8448]{1,0:T(2,128)(2,1)S(1)}, u32[]{:S(2)}, u32[]{:S(2)}) collective-permute-start(s16[2,8448]{1,0:T(2,128)(2,1)S(1)} %get-tuple-element.58), channel_id=1, source_target_pairs={{0,12},{1,13},{2,14},{3,15},{4,8},{5,9},{6,10},{7,11},{8,4},{9,5},... | collective-permute-start | bytes 101384 | tf_op jit(solution)/shard_map/ppermute | solution.py:35
  27.5 0.6 %collective-permute-start.10 = (s16[2,8448]{1,0:T(2,128)(2,1)S(1)}, s16[2,8448]{1,0:T(2,128)(2,1)S(1)}, u32[]{:S(2)}, u32[]{:S(2)}) collective-permute-start(s16[2,8448]{1,0:T(2,128)(2,1)S(1)} %get-tuple-element.59), channel_id=1, source_target_pairs={{0,8},{1,9},{2,10},{3,11},{4,12},{5,13},{6,14},{7,15},{8,0},{9,1},... | collective-permute-start | bytes 101384 | tf_op jit(solution)/shard_map/ppermute | solution.py:35
  28.1 2.3 %collective-permute-start.11 = (s16[2,8448]{1,0:T(2,128)(2,1)S(1)}, s16[2,8448]{1,0:T(2,128)(2,1)S(1)}, u32[]{:S(2)}, u32[]{:S(2)}) collective-permute-start(s16[2,8448]{1,0:T(2,128)(2,1)S(1)} %get-tuple-element.60), channel_id=1, source_target_pairs={{0,4},{1,5},{2,6},{3,7},{4,0},{5,1},{6,2},{7,3},{8,12},{9,13},{10,... | collective-permute-start | bytes 101384 | tf_op jit(solution)/shard_map/ppermute | solution.py:35
  30.4 1.5 %collective-permute-done.9.refs_1_ = s16[2,8448]{1,0:T(2,128)(2,1)S(1)} collective-permute-done((s16[2,8448]{1,0:T(2,128)(2,1)S(1)}, s16[2,8448]{1,0:T(2,128)(2,1)S(1)}, u32[]{:S(2)}, u32[]{:S(2)}) %collective-permute-start.9) | collective-permute-done | bytes 33824 | tf_op jit(solution)/shard_map/ppermute | solution.py:35
  31.9 0.4 %collective-permute-done.10.refs_2_ = s16[2,8448]{1,0:T(2,128)(2,1)S(1)} collective-permute-done((s16[2,8448]{1,0:T(2,128)(2,1)S(1)}, s16[2,8448]{1,0:T(2,128)(2,1)S(1)}, u32[]{:S(2)}, u32[]{:S(2)}) %collective-permute-start.10) | collective-permute-done | bytes 33824 | tf_op jit(solution)/shard_map/ppermute | solution.py:35
  32.4 0.3 collective-permute-done.11.refs_3_
  32.7 1.2 %shard_map.64 = bf16[2,8192]{1,0:T(2,128)(2,1)} custom-call(s16[2,8448]{1,0:T(2,128)(2,1)S(1)} %get-tuple-element.57.refs_0_, s16[2,8448]{1,0:T(2,128)(2,1)S(1)} %collective-permute-done.9.refs_1_, s16[2,8448]{1,0:T(2,128)(2,1)S(1)} %collective-permute-done.10.refs_2_, s16[2,8448]{1,0:T(2,128)(2,1)S(1)} %collective-permute-done.11.refs_3_), custom_call_target="tpu_custom_call" | custom-call | tf_op jit(solution)/shard_map/pallas_call | solution.py:253
  (1 shorter events, 0.0 us)
Async XLA Ops:
  0.0 15.3 %copy-start = (bf16[512,1024]{1,0:T(8,128)(2,1)S(1)}, bf16[512,1024]{1,0:T(8,128)(2,1)}, u32[]{:S(2)}) copy-start(bf16[512,1024]{1,0:T(8,128)(2,1)} %refs_2_.5) | copy-start | bytes 3145732
  0.0 7.2 %collective-permute-start.1 = (bf16[2,8192]{1,0:T(2,128)(2,1)}, bf16[2,8192]{1,0:T(2,128)(2,1)S(1)}, u32[]{:S(2)}, u32[]{:S(2)}) collective-permute-start(bf16[2,8192]{1,0:T(2,128)(2,1)} %in_ref.1), channel_id=1, source_target_pairs={{0,12},{1,13},{2,14},{3,15},{4,8},{5,9},{6,10},{7,11},{8,4},{9,5},... | collective-permute-start | bytes 98312 | tf_op jit(solution)/shard_map/ppermute | solution.py:35
  5.1 5.0 %collective-permute-start = (bf16[2,8192]{1,0:T(2,128)(2,1)}, bf16[2,8192]{1,0:T(2,128)(2,1)S(1)}, u32[]{:S(2)}, u32[]{:S(2)}) collective-permute-start(bf16[2,8192]{1,0:T(2,128)(2,1)} %in_ref.1), channel_id=1, source_target_pairs={{0,8},{1,9},{2,10},{3,11},{4,12},{5,13},{6,14},{7,15},{8,0},{9,1},... | collective-permute-start | bytes 98312 | tf_op jit(solution)/shard_map/ppermute | solution.py:35
  5.1 5.0 %collective-permute-start.2 = (bf16[2,8192]{1,0:T(2,128)(2,1)}, bf16[2,8192]{1,0:T(2,128)(2,1)S(1)}, u32[]{:S(2)}, u32[]{:S(2)}) collective-permute-start(bf16[2,8192]{1,0:T(2,128)(2,1)} %in_ref.1), channel_id=1, source_target_pairs={{0,4},{1,5},{2,6},{3,7},{4,0},{5,1},{6,2},{7,3},{8,12},{9,13},{10,... | collective-permute-start | bytes 98312 | tf_op jit(solution)/shard_map/ppermute | solution.py:35
  5.7 0.8 %copy-start.2 = (bf16[2,8192]{1,0:T(2,128)(2,1)S(1)}, bf16[2,8192]{1,0:T(2,128)(2,1)}, u32[]{:S(2)}) copy-start(bf16[2,8192]{1,0:T(2,128)(2,1)} %in_ref.1) | copy-start | bytes 98308
  10.2 5.0 %collective-permute-start.4 = (bf16[8,8192]{1,0:T(8,128)(2,1)S(1)}, bf16[8,8192]{1,0:T(8,128)(2,1)S(1)}, u32[]{:S(2)}, u32[]{:S(2)}) collective-permute-start(bf16[8,8192]{1,0:T(8,128)(2,1)S(1)} %shard_map.56.refs_0_), channel_id=1, source_target_pairs={{0,2},{1,3},{2,0},{3,1},{4,6},{5,7},{6,4},{7,5},{8,10},{9,11},{10,... | collective-permute-start | bytes 393224 | tf_op jit(solution)/shard_map/ppermute | solution.py:35
  12.4 1.2 %copy-start.1 = (bf16[512,1024]{1,0:T(8,128)(2,1)S(1)}, bf16[512,1024]{1,0:T(8,128)(2,1)}, u32[]{:S(2)}) copy-start(bf16[512,1024]{1,0:T(8,128)(2,1)} %v_ref.1) | copy-start | bytes 3145732
  13.6 0.7 %copy-start.3 = (s32[16,8]{0,1:T(8,128)S(1)}, s32[16,8]{0,1:T(8,128)}, u32[]{:S(2)}) copy-start(s32[16,8]{0,1:T(8,128)} %param.8) | copy-start | bytes 1540
  14.7 1.5 %collective-permute-start.3 = (bf16[8,8192]{1,0:T(8,128)(2,1)S(1)}, bf16[8,8192]{1,0:T(8,128)(2,1)S(1)}, u32[]{:S(2)}, u32[]{:S(2)}) collective-permute-start(bf16[8,8192]{1,0:T(8,128)(2,1)S(1)} %shard_map.56.refs_0_), channel_id=1, source_target_pairs={{0,1},{1,0},{2,3},{3,2},{4,5},{5,4},{6,7},{7,6},{8,9},{9,8},{10,11... | collective-permute-start | bytes 393224 | tf_op jit(solution)/shard_map/ppermute | solution.py:35
  15.2 1.3 %collective-permute-start.5 = (bf16[8,8192]{1,0:T(8,128)(2,1)S(1)}, bf16[8,8192]{1,0:T(8,128)(2,1)S(1)}, u32[]{:S(2)}, u32[]{:S(2)}) collective-permute-start(bf16[8,8192]{1,0:T(8,128)(2,1)S(1)} %collective-permute-done.4.refs_1_), channel_id=1, source_target_pairs={{0,1},{1,0},{2,3},{3,2},{4,5},{5,4},{6,7},{7,6},{8,9},{9,8},{10,11... | collective-permute-start | bytes 393224 | tf_op jit(solution)/shard_map/ppermute | solution.py:35
  17.9 1.5 %collective-permute-start.6 = (s16[8,8448]{1,0:T(8,128)(2,1)S(1)}, s16[8,8448]{1,0:T(8,128)(2,1)S(1)}, u32[]{:S(2)}, u32[]{:S(2)}) collective-permute-start(s16[8,8448]{1,0:T(8,128)(2,1)S(1)} %get-tuple-element.51), channel_id=1, source_target_pairs={{0,1},{1,0},{2,3},{3,2},{4,5},{5,4},{6,7},{7,6},{8,9},{9,8},{10,11... | collective-permute-start | bytes 405512 | tf_op jit(solution)/shard_map/ppermute | solution.py:35
  19.0 2.4 %collective-permute-start.7 = (s16[8,8448]{1,0:T(8,128)(2,1)S(1)}, s16[8,8448]{1,0:T(8,128)(2,1)S(1)}, u32[]{:S(2)}, u32[]{:S(2)}) collective-permute-start(s16[8,8448]{1,0:T(8,128)(2,1)S(1)} %get-tuple-element.53), channel_id=1, source_target_pairs={{0,1},{1,0},{2,3},{3,2},{4,5},{5,4},{6,7},{7,6},{8,9},{9,8},{10,11... | collective-permute-start | bytes 405512 | tf_op jit(solution)/shard_map/ppermute | solution.py:35
  19.8 5.7 %collective-permute-start.8 = (s16[8,8448]{1,0:T(8,128)(2,1)S(1)}, s16[8,8448]{1,0:T(8,128)(2,1)S(1)}, u32[]{:S(2)}, u32[]{:S(2)}) collective-permute-start(s16[8,8448]{1,0:T(8,128)(2,1)S(1)} %shard_map.62), channel_id=1, source_target_pairs={{0,2},{1,3},{2,0},{3,1},{4,6},{5,7},{6,4},{7,5},{8,10},{9,11},{10,... | collective-permute-start | bytes 405512 | tf_op jit(solution)/shard_map/ppermute | solution.py:35
  25.9 6.0 %collective-permute-start.9 = (s16[2,8448]{1,0:T(2,128)(2,1)S(1)}, s16[2,8448]{1,0:T(2,128)(2,1)S(1)}, u32[]{:S(2)}, u32[]{:S(2)}) collective-permute-start(s16[2,8448]{1,0:T(2,128)(2,1)S(1)} %get-tuple-element.58), channel_id=1, source_target_pairs={{0,12},{1,13},{2,14},{3,15},{4,8},{5,9},{6,10},{7,11},{8,4},{9,5},... | collective-permute-start | bytes 101384 | tf_op jit(solution)/shard_map/ppermute | solution.py:35
  27.5 4.9 %collective-permute-start.10 = (s16[2,8448]{1,0:T(2,128)(2,1)S(1)}, s16[2,8448]{1,0:T(2,128)(2,1)S(1)}, u32[]{:S(2)}, u32[]{:S(2)}) collective-permute-start(s16[2,8448]{1,0:T(2,128)(2,1)S(1)} %get-tuple-element.59), channel_id=1, source_target_pairs={{0,8},{1,9},{2,10},{3,11},{4,12},{5,13},{6,14},{7,15},{8,0},{9,1},... | collective-permute-start | bytes 101384 | tf_op jit(solution)/shard_map/ppermute | solution.py:35
  28.1 4.6 %collective-permute-start.11 = (s16[2,8448]{1,0:T(2,128)(2,1)S(1)}, s16[2,8448]{1,0:T(2,128)(2,1)S(1)}, u32[]{:S(2)}, u32[]{:S(2)}) collective-permute-start(s16[2,8448]{1,0:T(2,128)(2,1)S(1)} %get-tuple-element.60), channel_id=1, source_target_pairs={{0,4},{1,5},{2,6},{3,7},{4,0},{5,1},{6,2},{7,3},{8,12},{9,13},{10,... | collective-permute-start | bytes 101384 | tf_op jit(solution)/shard_map/ppermute | solution.py:35
